TPU v7x, 32 devices: a whole 2x2x4 slice. The times are simulated.
32 devices in a mesh: role: 4 (over x, core), fsdp: 8 (over z, y).
Axes of the slice: x: 2, y: 2, z: 4, core: 2. Of those that a mesh axis runs over, the one named last changes fastest.
Arguments:
- source_noise: bfloat16 [3072, 64], P('fsdp'), may hold values from -6 to 6
- score_noise: bfloat16 [3072, 64], P('fsdp'), may hold values from -6 to 6
- noise_level: float32 [3072], P('fsdp'), may hold values from 0.05 to 0.95
- embed_weight: bfloat16 [4, 64, 3072], P('role'), may hold values from -0.75 to 0.75
- time_vector: float32 [4, 3072], P('role'), may hold values from -6 to 6
- norm_gain: float32 [4, 3072], P('role'), may hold values from 0.5 to 1.5
- block_weight: bfloat16 [4, 3072, 1536], P('role', 'fsdp'), may hold values from -0.109375 to 0.109375
- readout_weight: bfloat16 [4, 1536, 64], P('role'), may hold values from -0.15625 to 0.15625
Outputs:
- grads: float32 [4, 3072, 1536], P('role', 'fsdp')
- generated: bfloat16 [3072, 64], P('fsdp')
All inputs are finite; a program needn't handle non-finite values. Where the computation divides by a largest or mean magnitude, that divisor is 1e-20 or more.
Results may differ from a plain program's by a relative error of at most 0.0065.
Values may be sent and summed in bfloat16 or wider, within the bound.
No kernel may reach another device: no remote copies, remote signals or barrier semaphores. Data moves between devices by JAX's collectives and lax.ppermute only.
A program may use at most 128 MiB of HBM per device.

v0:
```python
import math

import jax
import jax.numpy as jnp
from jax import lax
from jax.sharding import PartitionSpec as P

adv_weight = 3.0


def broadcast(value, axis, root):
    mine = lax.axis_index(axis) == root
    return lax.psum(jnp.where(mine, value, jnp.zeros_like(value)), axis)


def norm_rows(preact, gain_row):
    return preact * lax.rsqrt(jnp.mean(preact * preact, axis=-1, keepdims=True) + 1e-06) * gain_row


def score_net(latent, level, embed_w, time_w, gain_row, block_w, readout_w):
    preact = (
        jnp.dot(latent, embed_w, preferred_element_type=jnp.float32)
        + level[:, None] * time_w[None, :]
    )
    normed = norm_rows(preact, gain_row).astype(jnp.bfloat16)
    hidden = jnp.dot(normed, block_w, preferred_element_type=jnp.float32)
    activated = jax.nn.gelu(hidden, approximate=True).astype(jnp.bfloat16)
    output = jnp.dot(activated, readout_w, preferred_element_type=jnp.float32).astype(jnp.bfloat16)
    return (preact, normed, hidden, output)


def hidden_grad(hidden, cotangent, readout_w):
    back = jnp.dot(cotangent, readout_w.astype(jnp.float32).T, precision=lax.Precision.HIGHEST)
    unused, gelu_back = jax.vjp(lambda value: jax.nn.gelu(value, approximate=True), hidden)
    return gelu_back(back)[0].astype(jnp.bfloat16)


def input_grad(hcot, preact, gain_row, block_w, embed_w):
    normed_back = lax.dot_general(
        hcot, block_w, (((1,), (1,)), ((), ())), preferred_element_type=jnp.float32
    )
    unused, norm_back = jax.vjp(lambda value: norm_rows(value, gain_row), preact)
    pre_back = norm_back(normed_back)[0]
    return jnp.dot(pre_back, embed_w.astype(jnp.float32).T, precision=lax.Precision.HIGHEST)


def shards(
    source_noise,
    score_noise,
    noise_level,
    embed_weight,
    time_vector,
    norm_gain,
    block_weight,
    readout_weight,
):
    group_index = lax.axis_index("role")
    embed_w = embed_weight[0]
    time_w = time_vector[0]
    gain_row = norm_gain[0]
    readout_w = readout_weight[0]
    gathered = lax.all_gather(block_weight[0], "fsdp", axis=0, tiled=True)
    ones = jnp.ones_like(noise_level)
    pre_first, normed_first, hidden_first, own_first = score_net(
        source_noise, ones, embed_w, time_w, gain_row, gathered, readout_w
    )
    generated = broadcast(own_first, "role", 0)
    level = noise_level[:, None]
    noised = (
        (1.0 - level) * generated.astype(jnp.float32) + level * score_noise.astype(jnp.float32)
    ).astype(jnp.bfloat16)
    pre_second, normed_second, hidden_second, scores = score_net(
        noised, noise_level, embed_w, time_w, gain_row, gathered, readout_w
    )
    gen32 = generated.astype(jnp.float32)
    score32 = scores.astype(jnp.float32)
    logit = jnp.sum(score32, axis=-1, keepdims=True)
    adv_cot = jnp.broadcast_to(-jax.nn.sigmoid(-logit), scores.shape)
    adv_hcot = hidden_grad(hidden_second, adv_cot, readout_w)
    latent_back = input_grad(adv_hcot, pre_second, gain_row, gathered, embed_w)
    adversarial = (adv_weight * (1.0 - level) * latent_back).astype(jnp.bfloat16)
    empty_rows = jnp.zeros_like(scores)
    is_score = (group_index == 1) | (group_index == 2)
    piece = jnp.where(is_score, scores, jnp.where(group_index == 3, adversarial, empty_rows))
    collected = lax.all_gather(piece[None], "role", axis=0, tiled=True)
    real32 = collected[1].astype(jnp.float32)
    fake32 = collected[2].astype(jnp.float32)
    spread = jnp.mean(jnp.abs(gen32 - real32), axis=-1, keepdims=True) + 1e-05
    dmd = ((fake32 - real32) / spread).astype(jnp.bfloat16)
    push = dmd.astype(jnp.float32) + collected[3].astype(jnp.float32)
    critic_cot = jnp.broadcast_to(jax.nn.sigmoid(logit), scores.shape)
    zero_cot = jnp.zeros_like(push)
    cotangent = jnp.where(
        group_index == 0,
        push,
        jnp.where(
            group_index == 2, score32 - gen32, jnp.where(group_index == 3, critic_cot, zero_cot)
        ),
    )
    chosen_normed = jnp.where(group_index == 0, normed_first, normed_second)
    chosen_hidden = jnp.where(group_index == 0, hidden_first, hidden_second)
    hcot = hidden_grad(chosen_hidden, cotangent, readout_w)
    factor = 1.0 / math.sqrt(source_noise.shape[0] * lax.axis_size("fsdp"))
    partial_grad = lax.psum_scatter(
        lax.dot_general(
            chosen_normed, hcot, (((0,), (0,)), ((), ())), preferred_element_type=jnp.float32
        )
        * factor,
        "fsdp",
        scatter_dimension=0,
        tiled=True,
    )
    return (partial_grad[None], generated)


def solution(mesh):
    in_specs = (
        P("fsdp", None),
        P("fsdp", None),
        P("fsdp"),
        P("role", None, None),
        P("role", None),
        P("role", None),
        P("role", "fsdp", None),
        P("role", None, None),
    )
    out_specs = (P("role", "fsdp", None), P("fsdp", None))
    return jax.shard_map(shards, mesh=mesh, in_specs=in_specs, out_specs=out_specs, check_vma=False)
```

profile of v0, /device:TPU:0, one launch (start us, length us, event | category | flops | bytes accessed | tf_op | source)
XLA Modules:
  0.0 528.7 jit_solution(12884930664228712607)
XLA Ops:
  7.2 0.0 copy-start
  7.2 0.0 all-gather.4.cloned.1.call-start
  7.2 0.7 all-gather.4.cloned.1.call-update
  7.9 0.0 reduce-scatter.2.cloned.1.call-start
  8.0 0.2 copy-done
  8.2 3.9 multiply_reduce_fusion.2
  12.0 0.0 copy-done.5
  12.1 138.9 %all-gather.4.cloned.1.call-done = bf16[1,3072,1536]{2,1,0:T(8,128)(2,1)} async-done(((bf16[1,384,1536]{2,1,0:T(8,128)(2,1)}), bf16[1,3072,1536]{2,1,0:T(8,128)(2,1)}) %all-gather.4.cloned.1.call-update) | async-done | bytes 9437200 | tf_op jit(solution)/shard_map/all_gather | solution.py:62
  151.0 0.0 copy-done.3
  151.0 7.9 %fusion.4 = f32[384,1536]{1,0:T(8,128)S(1)} fusion(bf16[1,3072,1536]{2,1,0:T(8,128)(2,1)} %all-gather.4.cloned.1.call-done, f32[384,3072]{1,0:T(8,128)} %get-tuple-element.7, f32[3072]{0:T(1024)S(1)} %bitcast.41, f32[384]{0:T(512)S(1)} %add_rsqrt_fusion), kind=kOutput, calls=%fused_computation.5 | convolution fusion | flops 3627417600 | bytes 16528896 | tf_op jit(solution)/shard_map/dot_general | solution.py:26
  158.9 0.0 copy-done.6
  158.9 0.0 copy-start.2
  159.0 0.0 copy-start.4
  159.0 0.9 fusion.47
  159.9 11.0 %psum.7 = bf16[384,64]{0,1:T(8,128)(2,1)S(1)} all-reduce(bf16[384,64]{0,1:T(8,128)(2,1)S(1)} %fusion.47), channel_id=1, replica_groups=mesh['role'=4,'fsdp'=8] {'role'}, use_global_device_ids=true, to_apply=%region_1.2 | all-reduce | flops 24576 | bytes 98304 | tf_op jit(solution)/shard_map/psum | solution.py:13
  170.8 0.0 copy-start.1
  170.9 1.0 multiply_reduce_fusion.1
  171.9 6.6 %fusion.2 = f32[384,1536]{1,0:T(8,128)S(1)} fusion(bf16[1,3072,1536]{2,1,0:T(8,128)(2,1)} %all-gather.4.cloned.1.call-done, f32[384,3072]{1,0:T(8,128)S(1)} %get-tuple-element.9, f32[384]{0:T(512)S(1)} %fusion.81, f32[3072]{0:T(1024)S(1)} %bitcast.42), kind=kOutput, calls=%fused_computation.3 | convolution fusion | flops 3627417600 | bytes 16528896 | tf_op jit(solution)/shard_map/dot_general | solution.py:26
  178.5 0.9 convert_reduce_fusion
  179.5 2.8 fusion.18
  182.3 6.6 %multiply_reduce_fusion = (f32[384]{0:T(512)S(1)}, f32[384,3072]{1,0:T(8,128)S(1)}) fusion(f32[384,3072]{1,0:T(8,128)S(1)} %get-tuple-element.9, f32[3072]{0:T(1024)S(1)} %bitcast.43, bf16[384,1536]{1,0:T(8,128)(2,1)S(1)} %fusion.18, bf16[1,3072,1536]{2,1,0:T(8,128)(2,1)} %all-gather.4.cloned.1.call-done), kind=kOutput, calls=%fused_computation.10 | convolution fusion | flops 3627417088 | bytes 20067840 | tf_op jit(solution)/shard_map/dot_general | solution.py:39
  188.9 0.0 slice-start
  188.9 3.2 fusion.51
  192.2 5.8 %all-gather.1 = bf16[1536,64]{0,1:T(8,128)(2,1)S(1)} all-gather(bf16[384,64]{0,1:T(8,128)(2,1)S(1)} %fusion.51), channel_id=3, replica_groups=mesh['role'=4,'fsdp'=8] {'role'}, dimensions={0}, use_global_device_ids=true | all-gather | bytes 245760 | tf_op jit(solution)/shard_map/all_gather | solution.py:85
  198.1 0.0 copy-done.1
  198.1 0.0 slice-start.1
  198.1 2.7 fusion.25
  200.8 0.0 slice-done
  200.8 0.0 slice-done.1
  200.8 9.6 %convolution_multiply_fusion = f32[3072,1536]{1,0:T(8,128)} fusion(bf16[384,1536]{1,0:T(8,128)(2,1)S(1)} %fusion.25, pred[]{:T(512)S(6)} %eq.8, f32[384,3072]{1,0:T(8,128)S(1)} %bitcast.40, f32[3072]{0:T(1024)S(1)} %bitcast.44, f32[384]{0:T(512)S(1)} %add_rsqrt_fusion, f32[384,3072]{1,0:T(8,128)S(1)} %get-tuple-element.9, f32[384]{0:T(512)S(1)} %fusion.81), kind=kOutput, calls=%fused_computation | convolution fusion | flops 3636854784 | bytes 29506560 | tf_op jit(solution)/shard_map/dot_general | solution.py:105
  210.5 0.0 reduce-scatter.2.cloned.1.call-update
  210.5 311.4 %reduce-scatter.2.cloned.1.call-done = f32[384,1536]{1,0:T(8,128)} async-done(((f32[3072,1536]{1,0:T(8,128)}), f32[384,1536]{1,0:T(8,128)}) %reduce-scatter.2.cloned.1.call-update) | async-done | bytes 2359312 | tf_op jit(solution)/shard_map/reduce_scatter | solution.py:104
  (13 shorter events, 0.1 us)
Async XLA Ops:
  7.2 1.0 copy-start
  7.2 143.8 %all-gather.4.cloned.1.call-start = ((), (), s32[]{:S(2)}) async-start(), calls=%async_computation.2 | async-start | bytes 10616832 | tf_op jit(solution)/shard_map/all_gather | solution.py:62
  7.9 513.9 %reduce-scatter.2.cloned.1.call-start = ((), (), s32[]{:S(2)}) async-start(), calls=%async_computation.1 | async-start | bytes 21233664 | tf_op jit(solution)/shard_map/reduce_scatter | solution.py:104
  8.2 3.9 copy-start.5
  8.2 142.8 %copy-start.3 = (f32[1,3072]{1,0:T(1,128)S(1)}, f32[1,3072]{1,0:T(1,128)}, u32[]{:S(2)}) copy-start(f32[1,3072]{1,0:T(1,128)} %param.13) | copy-start | bytes 36868
  151.0 7.9 %copy-start.6 = (bf16[1,1536,64]{1,2,0:T(8,128)(2,1)S(1)}, bf16[1,1536,64]{1,2,0:T(8,128)(2,1)}, u32[]{:S(2)}) copy-start(bf16[1,1536,64]{1,2,0:T(8,128)(2,1)} %param.15) | copy-start | bytes 589828
  158.9 11.9 %copy-start.2 = (bf16[384,64]{0,1:T(8,128)(2,1)S(1)}, bf16[384,64]{0,1:T(8,128)(2,1)}, u32[]{:S(2)}) copy-start(bf16[384,64]{0,1:T(8,128)(2,1)} %param.9) | copy-start | bytes 147460
  159.0 11.9 %copy-start.4 = (f32[1,3072]{1,0:T(1,128)S(1)}, f32[1,3072]{1,0:T(1,128)}, u32[]{:S(2)}) copy-start(f32[1,3072]{1,0:T(1,128)} %param.12) | copy-start | bytes 36868
  170.8 27.2 %copy-start.1 = (bf16[384,64]{0,1:T(8,128)(2,1)}, bf16[384,64]{0,1:T(8,128)(2,1)S(1)}, u32[]{:S(2)}) copy-start(bf16[384,64]{0,1:T(8,128)(2,1)S(1)} %psum.7) | copy-start | bytes 147460
  188.9 11.9 %slice-start = ((s8[4718592]{0:T(1024)(128)(4,1)}), s8[4194304]{0:T(1024)(128)(4,1)S(1)}, s32[]{:S(2)}) async-start(s8[4718592]{0:T(1024)(128)(4,1)} %bitcast.39), calls=%async_computation.3 | async-start | bytes 8388608
  198.1 2.7 slice-start.1
Sparse Core Ops, SparseCore 0:
  10.2 140.7 all-gather.3
  210.6 311.2 reduce-scatter.1
where the time goes:
time: 529 us
  waiting for transfers between devices  451 us (85%)
  matrix products  46.3 us (9%)
  blocking collectives  16.8 us (3%)
  between operations  14.2 us (3%)
    reduce_scatter x1, waiting for transfers between devices, shards(): lax.psum_scatter(lax.dot_general(chosen_normed, hcot, (((0,), (0,)), ((),...  311 us
    all_gather x1, waiting for transfers between devices, shards(): gathered = lax.all_gather(block_weight[0], 'fsdp', axis=0, tiled=True)  139 us
    dot_general x2, matrix products, score_net(): hidden = jnp.dot(normed, block_w, preferred_element_type=jnp.float32)  14.5 us
    psum x1, blocking collectives, broadcast(): return lax.psum(jnp.where(mine, value, jnp.zeros_like(value)), axis)  11 us
  transfers between devices with their start and end apart: 2, of which 2 were waited for; matrix products, arithmetic and copies ran while one was open for 1% of the time, Pallas kernels for 0%

commit v1 on v0

v1 whole, which is shorter than its diff:
```python
import functools
import math

import jax
import jax.numpy as jnp
from jax import lax
from jax.experimental import pallas as pl
from jax.experimental.pallas import tpu as pltpu
from jax.sharding import PartitionSpec as P

adv_weight = 3.0
f32 = jnp.float32
bf16 = jnp.bfloat16
extra = 8
pieces = 2
part_limit = 54528
curve = math.sqrt(2.0 / math.pi)
bend = 0.044715


def halves(value):
    high = value.astype(bf16)
    return high, (value - high.astype(f32)).astype(bf16)


def mm(left, right, left_dim, right_dim):
    return lax.dot_general(
        left, right, (((left_dim,), (right_dim,)), ((), ())), preferred_element_type=f32
    )


def gelu_parts(hidden):
    square = hidden * hidden
    bent = jnp.tanh(curve * hidden * (1.0 + bend * square))
    return square, bent


def gelu_value(hidden, bent):
    return 0.5 * hidden * (1.0 + bent)


def gelu_slope(hidden, square, bent):
    return 0.5 * (1.0 + bent) + (0.5 * curve) * hidden * (1.0 - bent * bent) * (
        1.0 + (3.0 * bend) * square
    )


def level_rows(level):
    high = level.astype(bf16).astype(f32)
    mid = (level - high).astype(bf16).astype(f32)
    low = (level - high - mid).astype(bf16).astype(f32)
    row = lax.broadcasted_iota(jnp.int32, (extra, level.shape[1]), 0)
    return jnp.where(row == 0, high, jnp.where(row == 1, mid, jnp.where(row == 2, low, 0.0)))


def widen(latent, level):
    return jnp.concatenate([latent.astype(f32), level_rows(level)], axis=0)


def norm_scale(wide, gram, width):
    seen = lax.dot_general(
        gram,
        wide,
        (((1,), (0,)), ((), ())),
        precision=lax.Precision.HIGHEST,
        preferred_element_type=f32,
    )
    square = jnp.sum(seen * wide, axis=0, keepdims=True)
    return lax.rsqrt(square * (1.0 / width) + 1e-06), seen


def columns_of(at, half, upper):
    tile = half // pieces
    base = upper * half if at < pieces else (1 - upper) * half
    return pl.ds(pl.multiple_of(base + (at % pieces) * tile, tile), tile)


def part_kernel(embed_ref, vectors_ref, block_ref, *rest):
    *outs, embed, buffer, sems = rest
    place = lax.axis_index("fsdp")
    upper = place & 1
    depth, cols = buffer.shape
    half = cols // 2
    tile = half // pieces
    own = slice(None)
    if embed_ref.shape[1] != depth:
        own = pl.ds(pl.multiple_of(place * depth, depth), depth)
    small = pltpu.make_async_copy(embed_ref.at[:, own], embed, sems.at[2 * pieces])
    order = [*range(pieces, 2 * pieces), *range(pieces)]
    large = [
        pltpu.make_async_copy(
            block_ref.at[0, :, columns_of(at, half, upper)],
            buffer.at[:, at * tile : (at + 1) * tile],
            sems.at[at],
        )
        for at in order
    ]
    small.start()
    for copy in large:
        copy.start()
    stamp, gain = vectors_ref[0:1, own], vectors_ref[1:2, own]
    row = lax.broadcasted_iota(jnp.int32, (extra, depth), 0)
    stamped = jnp.where(row < 3, stamp * gain, 0.0)
    small.wait()
    gained = jnp.concatenate([embed[...].astype(f32) * gain, stamped], axis=0)
    rows = gained.shape[0]
    both = jnp.concatenate([gained, gained - gained.astype(bf16).astype(f32)], axis=0).astype(bf16)
    outs[2 * pieces][...] = both
    for at, copy in zip(order, large):
        copy.wait()
        part = mm(both, buffer[:, at * tile : (at + 1) * tile], 1, 0)
        outs[at][...] = (part[:rows] + part[rows:]).astype(outs[at].dtype)


def forward(wide, gram_ref, proj_refs, readout_ref, width, slope_ref=None):
    upper = lax.axis_index("fsdp") & 1
    half = proj_refs[0].shape[1] * pieces
    tile = half // pieces
    scale, seen = norm_scale(wide, gram_ref[...], width)
    wide16 = wide.astype(bf16)
    total = jnp.zeros((readout_ref.shape[0], wide.shape[1]), f32)
    for at, proj_ref in enumerate(proj_refs):
        hidden = scale * mm(proj_ref[...], wide16, 0, 0)
        square, bent = gelu_parts(hidden)
        activated = gelu_value(hidden, bent).astype(bf16)
        total = total + mm(readout_ref[:, columns_of(at, half, upper)], activated, 1, 0)
        if slope_ref is not None:
            slope_ref[at * tile : (at + 1) * tile, :] = gelu_slope(hidden, square, bent)
    return total.astype(bf16), scale, seen


def first_kernel(latent_ref, noise_ref, level_ref, gram_ref, *rest, width):
    *proj_refs, readout_ref, out_ref, mix_ref, gram_out_ref = rest
    channels, tokens = latent_ref.shape
    wide = widen(latent_ref[...], jnp.ones((1, tokens), f32))
    out_ref[...], unused, unused = forward(wide, gram_ref, proj_refs, readout_ref, width)
    level = level_ref[...]
    mix_ref[:channels, :] = level * noise_ref[...].astype(f32)
    mix_ref[channels:, :] = jnp.broadcast_to(level, (extra, tokens))
    gram_out_ref[...] = gram_ref[...]


def second_kernel(source_ref, own_ref, by1_ref, by2_ref, by3_ref, mix_ref, gram_ref, *rest, width):
    proj_refs = rest[: 2 * pieces]
    readout_ref, columns_ref, generated_ref, piece_ref, flat_ref, slope_ref, scaled_ref = rest[2 * pieces :]
    role, upper = lax.axis_index("role"), lax.axis_index("fsdp") & 1
    channels, tokens = source_ref.shape
    half = proj_refs[0].shape[1] * pieces
    tile = half // pieces
    level = mix_ref[channels : channels + 1, :]
    first = role == 0
    generated = jnp.where(
        first,
        own_ref[...].astype(f32),
        jnp.where(
            role == 3,
            by3_ref[...].astype(f32),
            jnp.where(role == 2, by2_ref[...].astype(f32), by1_ref[...].astype(f32)),
        ),
    )
    generated_ref[...] = generated.astype(bf16)
    noised = (1.0 - level) * generated + mix_ref[:channels, :]
    latent = jnp.where(first, source_ref[...].astype(f32), noised.astype(bf16).astype(f32))
    wide = widen(latent, jnp.where(first, 1.0, level))
    scores, scale, seen = forward(wide, gram_ref, proj_refs, readout_ref, width, slope_ref)
    piece_ref[...] = scores
    logit = jnp.sum(scores.astype(f32), axis=0, keepdims=True)
    flat_ref[...] = 1.0 / (1.0 + jnp.exp(-logit))

    @pl.when(role == 3)
    def _():
        high, low = halves(-1.0 / (1.0 + jnp.exp(logit)))
        cot = jnp.concatenate(
            [
                jnp.broadcast_to(high, (channels, tokens)),
                jnp.broadcast_to(low, (channels, tokens)),
            ],
            axis=0,
        )
        back_rows = jnp.zeros(wide.shape, f32)
        for at, proj_ref in enumerate(proj_refs):
            back = mm(columns_ref[columns_of(at, half, upper), :], cot, 1, 0)
            hcot = (back * slope_ref[at * tile : (at + 1) * tile, :]).astype(bf16)
            back_rows = back_rows + mm(proj_ref[...], hcot, 1, 0)
        inner = scale * jnp.sum(back_rows * wide, axis=0, keepdims=True)
        latent_back = scale * back_rows[:channels] - (scale * scale * inner * (1.0 / width)) * seen[:channels]
        piece_ref[...] = (adv_weight * (1.0 - level) * latent_back).astype(bf16)

    scaled = scale * wide
    scaled_ref[...] = jnp.concatenate([scaled, scaled - scaled.astype(bf16).astype(f32)], axis=0).astype(bf16)


def pull_back(cot, slope_ref, scaled_ref, columns_ref, out_refs, first_piece):
    upper = lax.axis_index("fsdp") & 1
    rows, tile = out_refs[0].shape
    half = tile * pieces
    scaled = scaled_ref[...]
    for at, out_ref in enumerate(out_refs, first_piece):
        back = mm(columns_ref[columns_of(at, half, upper), :], cot, 1, 0)
        hcot = (back * slope_ref[at * tile : (at + 1) * tile, :]).astype(bf16)
        part = mm(scaled, hcot, 1, 1)
        out_ref[...] = (part[:rows] + part[rows:]).astype(out_ref.dtype)


def send_kernel(
    adversarial_ref,
    real_ref,
    fake_ref,
    generated_ref,
    piece_ref,
    flat_ref,
    slope_ref,
    scaled_ref,
    columns_ref,
    cot_ref,
    *out_refs,
):
    role = lax.axis_index("role")
    first = role == 0
    generated = generated_ref[...].astype(f32)
    piece = piece_ref[...].astype(f32)
    fake = fake_ref[...].astype(f32)
    real = real_ref[...].astype(f32)
    adversarial = adversarial_ref[...].astype(f32)
    spread = jnp.mean(jnp.abs(generated - real), axis=0, keepdims=True) + 1e-05
    dmd = (fake - real) / spread
    flat = jnp.broadcast_to(flat_ref[...], generated.shape)
    flat_high = flat.astype(bf16).astype(f32)
    left = jnp.where(
        first, dmd, jnp.where(role == 2, piece, jnp.where(role == 3, flat_high, 0.0))
    ).astype(bf16)
    right = jnp.where(
        first,
        adversarial,
        jnp.where(role == 2, -generated, jnp.where(role == 3, flat - flat_high, 0.0)),
    ).astype(bf16)
    cot = jnp.concatenate([left, right], axis=0)
    cot_ref[...] = cot
    pull_back(cot, slope_ref, scaled_ref, columns_ref, out_refs, pieces)


def keep_kernel(cot_ref, slope_ref, scaled_ref, columns_ref, *out_refs):
    pull_back(cot_ref[...], slope_ref, scaled_ref, columns_ref, out_refs, 0)


def grad_kernel(own_ref, *rest, factor, keep):
    total_refs = rest[:pieces]
    *unused, out_ref, buffer, sems = rest[pieces:]
    upper = lax.axis_index("fsdp") & 1
    half = buffer.shape[1]
    tile = half // pieces
    own = own_ref[...]
    copies = []
    for at, total_ref in enumerate(total_refs):
        here = slice(at * tile, (at + 1) * tile)
        total = total_ref[...].astype(f32)
        part = mm(own, jnp.concatenate([total, total], axis=0).astype(bf16), 0, 0)
        buffer[:, here] = part * factor
        cols = columns_of(at if keep else at + pieces, half, upper)
        copy = pltpu.make_async_copy(buffer.at[:, here], out_ref.at[0, :, cols], sems.at[at])
        copy.start()
        copies.append(copy)
    for copy in copies:
        copy.wait()


def call(kernel, name, out_shape, inputs, scratch=(), cost=0):
    many = isinstance(out_shape, list)
    vmem = pl.BlockSpec(memory_space=pltpu.VMEM)
    return pl.pallas_call(
        kernel,
        out_shape=out_shape,
        in_specs=[vmem] * len(inputs),
        out_specs=[vmem] * len(out_shape) if many else vmem,
        scratch_shapes=list(scratch),
        compiler_params=pltpu.CompilerParams(vmem_limit_bytes=16 * 1024 * 1024),
        cost_estimate=pl.CostEstimate(flops=cost, bytes_accessed=cost // 1000, transcendentals=cost // 1000),
        name=name,
    )(*inputs)


def part_of(embed_w, vectors, block_weight):
    depth, cols = block_weight.shape[1:]
    channels = embed_w.shape[0]
    rows, half = channels + extra, cols // 2
    if depth % 128 != 0:
        embed_w, vectors = (
            lax.dynamic_slice_in_dim(value, lax.axis_index("fsdp") * depth, depth, 1)
            for value in (embed_w, vectors)
        )
    shapes = [jax.ShapeDtypeStruct((rows, half // pieces), dtype) for dtype in (f32, bf16) for at in range(pieces)]
    shapes.append(jax.ShapeDtypeStruct((2 * rows, depth), bf16))
    vmem = pl.BlockSpec(memory_space=pltpu.VMEM)
    hbm = pl.BlockSpec(memory_space=pltpu.HBM)
    return pl.pallas_call(
        part_kernel,
        out_shape=shapes,
        in_specs=[hbm, vmem, hbm],
        out_specs=[vmem] * len(shapes),
        scratch_shapes=[
            pltpu.VMEM((channels, depth), bf16),
            pltpu.VMEM((depth, cols), bf16),
            pltpu.SemaphoreType.DMA((2 * pieces + 1,)),
        ],
        compiler_params=pltpu.CompilerParams(vmem_limit_bytes=part_limit * 1024),
        cost_estimate=pl.CostEstimate(
            flops=8 * rows * depth * half, bytes_accessed=4 * depth * half, transcendentals=0
        ),
        name="part",
    )(embed_w, vectors, block_weight)


def gradient(own, totals, factor, cols, buffer=None):
    depth, half = own.shape[1], cols // 2
    keep = buffer is None
    vmem = pl.BlockSpec(memory_space=pltpu.VMEM)
    hbm = pl.BlockSpec(memory_space=pltpu.HBM)
    specs = [vmem] * (1 + pieces)
    inputs = [own, *totals]
    if not keep:
        specs.append(hbm)
        inputs.append(buffer)
    return pl.pallas_call(
        functools.partial(grad_kernel, factor=factor, keep=keep),
        out_shape=jax.ShapeDtypeStruct((1, depth, cols), f32),
        in_specs=specs,
        out_specs=hbm,
        input_output_aliases={} if keep else {len(inputs) - 1: 0},
        scratch_shapes=[pltpu.VMEM((depth, half), f32), pltpu.SemaphoreType.DMA((pieces,))],
        compiler_params=pltpu.CompilerParams(vmem_limit_bytes=16 * 1024 * 1024),
        cost_estimate=pl.CostEstimate(
            flops=4 * own.shape[0] * depth * half, bytes_accessed=4 * depth * half, transcendentals=0
        ),
        name="gradient_keep" if keep else "gradient_rest",
    )(*inputs)


def swap(values, axis, n, bit):
    pairs = [(i, i ^ bit) for i in range(n)]
    return [lax.ppermute(value, axis, pairs) for value in values]


def with_first(value, roles, other):
    pairs = [(0, other), (other, 0)] + [(i, i) for i in range(1, roles) if i != other]
    return lax.ppermute(value, "role", pairs)


def add_along(mine, received, n):
    mine = [value + part.astype(f32) for value, part in zip(mine, received)]
    bit = 2
    while bit < n:
        parts = swap([value.astype(bf16) for value in mine], "fsdp", n, bit)
        mine = [value + part.astype(f32) for value, part in zip(mine, parts)]
        bit *= 2
    return [value.astype(bf16) for value in mine]


def shards(
    source_noise,
    score_noise,
    noise_level,
    embed_weight,
    time_vector,
    norm_gain,
    block_weight,
    readout_weight,
):
    role = lax.axis_index("role")
    n = lax.axis_size("fsdp")
    embed_w = embed_weight[0]
    readout = readout_weight[0].T
    depth, cols = block_weight.shape[1:]
    channels, width = embed_w.shape
    tokens = source_noise.shape[0]
    rows = channels + extra
    half = cols // 2
    shape = jax.ShapeDtypeStruct
    roles = lax.axis_size("role")

    vectors = jnp.concatenate([time_vector, norm_gain], axis=0)
    *parts, own_rows = part_of(embed_w, vectors, block_weight)
    received = swap(parts[pieces:], "fsdp", n, 1)
    mine = add_along(parts[:pieces], received, n)
    proj = mine + swap(mine, "fsdp", n, 1)

    tall = jnp.concatenate(
        [embed_w.astype(f32), jnp.broadcast_to(time_vector, (3, width)), jnp.zeros((extra - 3, width), f32)]
    )
    gram = jnp.dot(tall, tall.T, precision=lax.Precision.HIGHEST)
    columns = jnp.concatenate([readout, readout], axis=0).T
    level = noise_level[None, :]
    source = source_noise.T
    latent_shape = shape((channels, tokens), bf16)

    own_first, mix, gram = call(
        functools.partial(first_kernel, width=width),
        "generator",
        [latent_shape, shape((rows, tokens), f32), shape((rows, rows), f32)],
        (source, score_noise.T, level, gram, *proj, readout),
    )
    by3, by2, by1 = (with_first(own_first, roles, other) for other in (3, 2, 1))
    drawn = jnp.where(role == 0, own_first, jnp.where(role == 1, by1, jnp.where(role == 2, by2, by3)))
    generated, piece, flat, slope, scaled = call(
        functools.partial(second_kernel, width=width),
        "score",
        [
            latent_shape,
            latent_shape,
            shape((1, tokens), f32),
            shape((cols, tokens), f32),
            shape((2 * rows, tokens), bf16),
        ],
        (source, own_first, by1, by2, by3, mix, gram, *proj, readout, columns),
    )
    real, fake, adversarial = (with_first(piece, roles, other) for other in (1, 2, 3))
    flat, drawn = lax.optimization_barrier((flat, drawn))

    cost = 4 * rows * tokens * half
    tail = (slope, scaled, columns)
    cot, *send = call(
        send_kernel,
        "cotangent_send",
        [shape((2 * channels, tokens), bf16)] + [shape((rows, half // pieces), bf16)] * pieces,
        (adversarial, real, fake, generated, piece, flat, *tail),
        cost=cost,
    )
    received = swap(send, "fsdp", n, 1)
    kept = call(
        keep_kernel, "cotangent_keep", [shape((rows, half // pieces), f32)] * pieces, (cot, *tail), cost=cost
    )
    totals = add_along(kept, received, n)
    others = swap(totals, "fsdp", n, 1)
    factor = 1.0 / math.sqrt(tokens * n)
    grads = gradient(own_rows, totals, factor, cols)
    grads = gradient(own_rows, others, factor, cols, grads)
    return (grads, drawn.T)


def solution(mesh):
    in_specs = (
        P("fsdp", None),
        P("fsdp", None),
        P("fsdp"),
        P("role", None, None),
        P("role", None),
        P("role", None),
        P("role", "fsdp", None),
        P("role", None, None),
    )
    out_specs = (P("role", "fsdp", None), P("fsdp", None))
    return jax.shard_map(shards, mesh=mesh, in_specs=in_specs, out_specs=out_specs, check_vma=False)
```

time: 529 us -> 69.9 us (0.13)
  waiting for transfers between devices: 451 us -> 18.3 us
  matrix products: 46.3 us -> 0.98 us
  starting transfers between devices: 0.08 us -> 36 us
  blocking collectives: 16.8 us -> 0 us
  between operations: 14.2 us -> 0.91 us
  Pallas kernels: 0 us -> 9.87 us
    reduce_scatter x1 -> x0, waiting for transfers between devices: 311 us -> none  [shards(): lax.psum_scatter(lax.dot_general(chosen_normed, hcot, (((0,), (0,)), ((),...]
    all_gather x1 -> x0, waiting for transfers between devices: 139 us -> none  [shards(): gathered = lax.all_gather(block_weight[0], 'fsdp', axis=0, tiled=True)]
    dot_general x11 -> x1, matrix products: 46.3 us -> 0.98 us  [shards(): gram = jnp.dot(tall, tall.T, precision=lax.Precision.HIGHEST)]
    ppermute x0 -> x22, starting transfers between devices: none -> 36 us  [the longest x16 24.1 us: swap(): return [lax.ppermute(value, axis, pairs) for value in values]]
    ppermute x0 -> x22, waiting for transfers between devices: none -> 18.3 us  [the longest x16 13.8 us: swap(): return [lax.ppermute(value, axis, pairs) for value in values]]
    psum x1 -> x0, blocking collectives: 11 us -> none  [broadcast(): return lax.psum(jnp.where(mine, value, jnp.zeros_like(value)), axis)]
    pallas_call x0 -> x7, Pallas kernels: none -> 9.87 us  [the longest x4 5.22 us: call(): pl.pallas_call(kernel, out_shape=out_shape, in_specs=[vmem] * len(inputs)...]
    all_gather x1 -> x0, blocking collectives: 5.83 us -> none  [shards(): collected = lax.all_gather(piece[None], 'role', axis=0, tiled=True)]
  transfers between devices with their start and end apart: 2 -> 22, of which waited for: 2 -> 12; matrix products, arithmetic and copies ran while one was open for 1% -> 5% of each run, Pallas kernels for 0% -> 3%
where the time goes in v1:
time: 69.9 us; the launch traced here: 69.5 us
  starting transfers between devices  36 us (52%)
  waiting for transfers between devices  18.3 us (26%)
  Pallas kernels  9.87 us (14%)
  other arithmetic  3 us (4%)
  matrix products  0.98 us (1%)
  between operations  0.91 us (1%)
    ppermute x16, starting transfers between devices, swap(): return [lax.ppermute(value, axis, pairs) for value in values]  24.1 us
    ppermute x16, waiting for transfers between devices, swap(): return [lax.ppermute(value, axis, pairs) for value in values]  13.8 us
    ppermute x6, starting transfers between devices, with_first(): return lax.ppermute(value, 'role', pairs)  12 us
    pallas_call x4, Pallas kernels, call(): pl.pallas_call(kernel, out_shape=out_shape, in_specs=[vmem] * len(inputs)...  5.22 us
    ppermute x6, waiting for transfers between devices, with_first(): return lax.ppermute(value, 'role', pairs)  4.51 us
    pallas_call x2, Pallas kernels, gradient(): pl.pallas_call(functools.partial(grad_kernel, factor=factor, keep=keep),...  2.66 us
    pallas_call x1, Pallas kernels, part_of(): pl.pallas_call(part_kernel, out_shape=shapes, in_specs=[hbm, vmem, hbm],...  1.99 us
  transfers between devices with their start and end apart: 22, of which 12 were waited for; matrix products, arithmetic and copies ran while one was open for 5% of the time, Pallas kernels for 3%

profile of v1, /device:TPU:0, one launch (start us, length us, event | category | flops | bytes accessed | tf_op | source)
XLA Modules:
  0.0 69.5 jit_solution(16096863366858074571)
XLA Ops:
  1.4 2.0 %part.1 = (f32[72,384]{1,0:T(8,128)S(1)}, f32[72,384]{1,0:T(8,128)S(1)}, bf16[72,384]{1,0:T(8,128)(2,1)S(1)}, bf16[72,384]{1,0:T(8,128)(2,1)S(1)}, bf16[144,384]{1,0:T(8,128)(2,1)S(1)}) custom-call(bf16[64,3072]{1,0:T(8,128)(2,1)} %bitcast.19, f32[2,3072]{1,0:T(2,128)S(1)} %pad_maximum_fusion.vectors_ref, bf16[1,384,1536]{2,1,0:T(8,128)(2,1)} %block_ref.1), custom_call_target="tpu_custom_call" | custom-call | flops 169869312 | bytes 1179648 | tf_op jit(solution)/shard_map/part/pallas_call | solution.py:295
  3.5 3.0 %collective-permute-start = (bf16[72,384]{1,0:T(8,128)(2,1)S(1)}, bf16[72,384]{1,0:T(8,128)(2,1)S(1)}, u32[]{:S(2)}, u32[]{:S(2)}) collective-permute-start(bf16[72,384]{1,0:T(8,128)(2,1)S(1)} %get-tuple-element.24), channel_id=1, source_target_pairs={{0,1},{1,0},{2,3},{3,2},{4,5},{5,4},{6,7},{7,6},{8,9},{9,8},{10,11... | collective-permute-start | bytes 165896 | tf_op jit(solution)/shard_map/ppermute | solution.py:340
  6.6 1.0 %bitcast_convert_fusion = f32[64,3072]{1,0:T(8,128)S(1)} fusion(bf16[1,64,3072]{2,1,0:T(8,128)(2,1)} %param.11), kind=kLoop, calls=%fused_computation.30 | loop fusion | flops 196608 | bytes 1179648 | tf_op jit(solution)/shard_map/convert_element_type | solution.py:387
  8.7 2.6 %collective-permute-start.1 = (bf16[72,384]{1,0:T(8,128)(2,1)S(1)}, bf16[72,384]{1,0:T(8,128)(2,1)S(1)}, u32[]{:S(2)}, u32[]{:S(2)}) collective-permute-start(bf16[72,384]{1,0:T(8,128)(2,1)S(1)} %fusion.6), channel_id=1, source_target_pairs={{0,2},{1,3},{2,0},{3,1},{4,6},{5,7},{6,4},{7,5},{8,10},{9,11},{10,... | collective-permute-start | bytes 165896 | tf_op jit(solution)/shard_map/ppermute | solution.py:340
  11.3 1.0 %collective-permute-start.4 = (bf16[72,384]{1,0:T(8,128)(2,1)S(1)}, bf16[72,384]{1,0:T(8,128)(2,1)S(1)}, u32[]{:S(2)}, u32[]{:S(2)}) collective-permute-start(bf16[72,384]{1,0:T(8,128)(2,1)S(1)} %fusion.7), channel_id=1, source_target_pairs={{0,2},{1,3},{2,0},{3,1},{4,6},{5,7},{6,4},{7,5},{8,10},{9,11},{10,... | collective-permute-start | bytes 165896 | tf_op jit(solution)/shard_map/ppermute | solution.py:340
  12.3 1.1 %collective-permute-done.1 = bf16[72,384]{1,0:T(8,128)(2,1)S(1)} collective-permute-done((bf16[72,384]{1,0:T(8,128)(2,1)S(1)}, bf16[72,384]{1,0:T(8,128)(2,1)S(1)}, u32[]{:S(2)}, u32[]{:S(2)}) %collective-permute-start.1) | collective-permute-done | bytes 55328 | tf_op jit(solution)/shard_map/ppermute | solution.py:340
  13.5 3.5 %collective-permute-start.2 = (bf16[72,384]{1,0:T(8,128)(2,1)S(1)}, bf16[72,384]{1,0:T(8,128)(2,1)S(1)}, u32[]{:S(2)}, u32[]{:S(2)}) collective-permute-start(bf16[72,384]{1,0:T(8,128)(2,1)S(1)} %fusion.10), channel_id=1, source_target_pairs={{0,4},{1,5},{2,6},{3,7},{4,0},{5,1},{6,2},{7,3},{8,12},{9,13},{10,... | collective-permute-start | bytes 165896 | tf_op jit(solution)/shard_map/ppermute | solution.py:340
  17.0 1.3 %collective-permute-start.5 = (bf16[72,384]{1,0:T(8,128)(2,1)S(1)}, bf16[72,384]{1,0:T(8,128)(2,1)S(1)}, u32[]{:S(2)}, u32[]{:S(2)}) collective-permute-start(bf16[72,384]{1,0:T(8,128)(2,1)S(1)} %fusion.11), channel_id=1, source_target_pairs={{0,4},{1,5},{2,6},{3,7},{4,0},{5,1},{6,2},{7,3},{8,12},{9,13},{10,... | collective-permute-start | bytes 165896 | tf_op jit(solution)/shard_map/ppermute | solution.py:340
  19.2 2.2 %collective-permute-start.6 = (bf16[72,384]{1,0:T(8,128)(2,1)S(1)}, bf16[72,384]{1,0:T(8,128)(2,1)S(1)}, u32[]{:S(2)}, u32[]{:S(2)}) collective-permute-start(bf16[72,384]{1,0:T(8,128)(2,1)S(1)} %add_convert_fusion.3.rest_0_), channel_id=1, source_target_pairs={{0,1},{1,0},{2,3},{3,2},{4,5},{5,4},{6,7},{7,6},{8,9},{9,8},{10,11... | collective-permute-start | bytes 165896 | tf_op jit(solution)/shard_map/ppermute | solution.py:340
  24.2 2.2 %collective-permute-done.7.rest_3_ = bf16[72,384]{1,0:T(8,128)(2,1)S(1)} collective-permute-done((bf16[72,384]{1,0:T(8,128)(2,1)S(1)}, bf16[72,384]{1,0:T(8,128)(2,1)S(1)}, u32[]{:S(2)}, u32[]{:S(2)}) %collective-permute-start.7) | collective-permute-done | bytes 55328 | tf_op jit(solution)/shard_map/ppermute | solution.py:340
  26.4 1.5 %generator.1 = (bf16[64,384]{1,0:T(8,128)(2,1)S(1)}, f32[72,384]{1,0:T(8,128)S(1)}, f32[72,72]{1,0:T(8,128)S(1)}) custom-call(bf16[64,384]{1,0:T(8,128)(2,1)S(1)} %bitcast.15, bf16[64,384]{1,0:T(8,128)(2,1)S(1)} %bitcast.17, f32[1,384]{1,0:T(1,128)S(1)} %broadcast_in_dim.13.level_ref, f32[72,72]{1,0:T(8,128)S(1)} %fusion.gram_ref, ...), custom_call_target="tpu_custom_call" | custom-call | tf_op jit(solution)/shard_map/generator/pallas_call | solution.py:270
  27.9 1.9 %collective-permute-start.10 = (bf16[64,384]{1,0:T(8,128)(2,1)S(1)}, bf16[64,384]{1,0:T(8,128)(2,1)S(1)}, u32[]{:S(2)}, u32[]{:S(2)}) collective-permute-start(bf16[64,384]{1,0:T(8,128)(2,1)S(1)} %get-tuple-element.27.own_ref), channel_id=1, source_target_pairs={{0,24},{24,0},{8,8},{16,16},{1,25},{25,1},{9,9},{17,17},{2,26},{26... | collective-permute-start | bytes 147464 | tf_op jit(solution)/shard_map/ppermute | solution.py:345
  29.8 2.1 %collective-permute-start.9 = (bf16[64,384]{1,0:T(8,128)(2,1)S(1)}, bf16[64,384]{1,0:T(8,128)(2,1)S(1)}, u32[]{:S(2)}, u32[]{:S(2)}) collective-permute-start(bf16[64,384]{1,0:T(8,128)(2,1)S(1)} %get-tuple-element.27.own_ref), channel_id=1, source_target_pairs={{0,16},{16,0},{8,8},{24,24},{1,17},{17,1},{9,9},{25,25},{2,18},{18... | collective-permute-start | bytes 147464 | tf_op jit(solution)/shard_map/ppermute | solution.py:345
  31.9 1.9 %collective-permute-start.8 = (bf16[64,384]{1,0:T(8,128)(2,1)S(1)}, bf16[64,384]{1,0:T(8,128)(2,1)S(1)}, u32[]{:S(2)}, u32[]{:S(2)}) collective-permute-start(bf16[64,384]{1,0:T(8,128)(2,1)S(1)} %get-tuple-element.27.own_ref), channel_id=1, source_target_pairs={{0,8},{8,0},{16,16},{24,24},{1,9},{9,1},{17,17},{25,25},{2,10},{10... | collective-permute-start | bytes 147464 | tf_op jit(solution)/shard_map/ppermute | solution.py:345
  34.1 1.7 %collective-permute-done.9.by2_ref = bf16[64,384]{1,0:T(8,128)(2,1)S(1)} collective-permute-done((bf16[64,384]{1,0:T(8,128)(2,1)S(1)}, bf16[64,384]{1,0:T(8,128)(2,1)S(1)}, u32[]{:S(2)}, u32[]{:S(2)}) %collective-permute-start.9) | collective-permute-done | bytes 49184 | tf_op jit(solution)/shard_map/ppermute | solution.py:345
  35.8 2.3 %score.1 = (bf16[64,384]{1,0:T(8,128)(2,1)S(1)}, bf16[64,384]{1,0:T(8,128)(2,1)S(1)}, f32[1,384]{1,0:T(1,128)S(1)}, f32[1536,384]{1,0:T(8,128)S(1)}, bf16[144,384]{1,0:T(8,128)(2,1)S(1)}) custom-call(bf16[64,384]{1,0:T(8,128)(2,1)S(1)} %bitcast.16, bf16[64,384]{1,0:T(8,128)(2,1)S(1)} %get-tuple-element.27.own_ref, ...), custom_call_target="tpu_custom_call" | custom-call | tf_op jit(solution)/shard_map/score/pallas_call | solution.py:270
  38.0 2.1 %collective-permute-start.13 = (bf16[64,384]{1,0:T(8,128)(2,1)S(1)}, bf16[64,384]{1,0:T(8,128)(2,1)S(1)}, u32[]{:S(2)}, u32[]{:S(2)}) collective-permute-start(bf16[64,384]{1,0:T(8,128)(2,1)S(1)} %get-tuple-element.30.piece_ref), channel_id=1, source_target_pairs={{0,16},{16,0},{8,8},{24,24},{1,17},{17,1},{9,9},{25,25},{2,18},{18... | collective-permute-start | bytes 147464 | tf_op jit(solution)/shard_map/ppermute | solution.py:345
  40.2 1.9 %collective-permute-start.12 = (bf16[64,384]{1,0:T(8,128)(2,1)S(1)}, bf16[64,384]{1,0:T(8,128)(2,1)S(1)}, u32[]{:S(2)}, u32[]{:S(2)}) collective-permute-start(bf16[64,384]{1,0:T(8,128)(2,1)S(1)} %get-tuple-element.30.piece_ref), channel_id=1, source_target_pairs={{0,8},{8,0},{16,16},{24,24},{1,9},{9,1},{17,17},{25,25},{2,10},{10... | collective-permute-start | bytes 147464 | tf_op jit(solution)/shard_map/ppermute | solution.py:345
  42.1 1.9 %collective-permute-start.11 = (bf16[64,384]{1,0:T(8,128)(2,1)S(1)}, bf16[64,384]{1,0:T(8,128)(2,1)S(1)}, u32[]{:S(2)}, u32[]{:S(2)}) collective-permute-start(bf16[64,384]{1,0:T(8,128)(2,1)S(1)} %get-tuple-element.30.piece_ref), channel_id=1, source_target_pairs={{0,24},{24,0},{8,8},{16,16},{1,25},{25,1},{9,9},{17,17},{2,26},{26... | collective-permute-start | bytes 147464 | tf_op jit(solution)/shard_map/ppermute | solution.py:345
  44.7 2.8 %collective-permute-done.11.adversarial_ref = bf16[64,384]{1,0:T(8,128)(2,1)S(1)} collective-permute-done((bf16[64,384]{1,0:T(8,128)(2,1)S(1)}, bf16[64,384]{1,0:T(8,128)(2,1)S(1)}, u32[]{:S(2)}, u32[]{:S(2)}) %collective-permute-start.11) | collective-permute-done | bytes 49184 | tf_op jit(solution)/shard_map/ppermute | solution.py:345
  49.1 1.3 %collective-permute-start.18 = (bf16[72,384]{1,0:T(8,128)(2,1)S(1)}, bf16[72,384]{1,0:T(8,128)(2,1)S(1)}, u32[]{:S(2)}, u32[]{:S(2)}) collective-permute-start(bf16[72,384]{1,0:T(8,128)(2,1)S(1)} %get-tuple-element.40), channel_id=1, source_target_pairs={{0,1},{1,0},{2,3},{3,2},{4,5},{5,4},{6,7},{7,6},{8,9},{9,8},{10,11... | collective-permute-start | bytes 165896 | tf_op jit(solution)/shard_map/ppermute | solution.py:340
  51.1 1.4 %collective-permute-done.14 = bf16[72,384]{1,0:T(8,128)(2,1)S(1)} collective-permute-done((bf16[72,384]{1,0:T(8,128)(2,1)S(1)}, bf16[72,384]{1,0:T(8,128)(2,1)S(1)}, u32[]{:S(2)}, u32[]{:S(2)}) %collective-permute-start.14) | collective-permute-done | bytes 55328 | tf_op jit(solution)/shard_map/ppermute | solution.py:340
  52.5 1.3 %collective-permute-start.15 = (bf16[72,384]{1,0:T(8,128)(2,1)S(1)}, bf16[72,384]{1,0:T(8,128)(2,1)S(1)}, u32[]{:S(2)}, u32[]{:S(2)}) collective-permute-start(bf16[72,384]{1,0:T(8,128)(2,1)S(1)} %fusion.8), channel_id=1, source_target_pairs={{0,2},{1,3},{2,0},{3,1},{4,6},{5,7},{6,4},{7,5},{8,10},{9,11},{10,... | collective-permute-start | bytes 165896 | tf_op jit(solution)/shard_map/ppermute | solution.py:340
  53.8 1.1 %collective-permute-start.19 = (bf16[72,384]{1,0:T(8,128)(2,1)S(1)}, bf16[72,384]{1,0:T(8,128)(2,1)S(1)}, u32[]{:S(2)}, u32[]{:S(2)}) collective-permute-start(bf16[72,384]{1,0:T(8,128)(2,1)S(1)} %fusion.9), channel_id=1, source_target_pairs={{0,2},{1,3},{2,0},{3,1},{4,6},{5,7},{6,4},{7,5},{8,10},{9,11},{10,... | collective-permute-start | bytes 165896 | tf_op jit(solution)/shard_map/ppermute | solution.py:340
  54.9 2.1 %collective-permute-done.15 = bf16[72,384]{1,0:T(8,128)(2,1)S(1)} collective-permute-done((bf16[72,384]{1,0:T(8,128)(2,1)S(1)}, bf16[72,384]{1,0:T(8,128)(2,1)S(1)}, u32[]{:S(2)}, u32[]{:S(2)}) %collective-permute-start.15) | collective-permute-done | bytes 55328 | tf_op jit(solution)/shard_map/ppermute | solution.py:340
  57.0 1.5 %collective-permute-start.16 = (bf16[72,384]{1,0:T(8,128)(2,1)S(1)}, bf16[72,384]{1,0:T(8,128)(2,1)S(1)}, u32[]{:S(2)}, u32[]{:S(2)}) collective-permute-start(bf16[72,384]{1,0:T(8,128)(2,1)S(1)} %fusion.12), channel_id=1, source_target_pairs={{0,4},{1,5},{2,6},{3,7},{4,0},{5,1},{6,2},{7,3},{8,12},{9,13},{10,... | collective-permute-start | bytes 165896 | tf_op jit(solution)/shard_map/ppermute | solution.py:340
  58.5 1.6 %collective-permute-start.20 = (bf16[72,384]{1,0:T(8,128)(2,1)S(1)}, bf16[72,384]{1,0:T(8,128)(2,1)S(1)}, u32[]{:S(2)}, u32[]{:S(2)}) collective-permute-start(bf16[72,384]{1,0:T(8,128)(2,1)S(1)} %fusion.13), channel_id=1, source_target_pairs={{0,4},{1,5},{2,6},{3,7},{4,0},{5,1},{6,2},{7,3},{8,12},{9,13},{10,... | collective-permute-start | bytes 165896 | tf_op jit(solution)/shard_map/ppermute | solution.py:340
  60.1 2.6 %collective-permute-done.16 = bf16[72,384]{1,0:T(8,128)(2,1)S(1)} collective-permute-done((bf16[72,384]{1,0:T(8,128)(2,1)S(1)}, bf16[72,384]{1,0:T(8,128)(2,1)S(1)}, u32[]{:S(2)}, u32[]{:S(2)}) %collective-permute-start.16) | collective-permute-done | bytes 55328 | tf_op jit(solution)/shard_map/ppermute | solution.py:340
  62.7 1.2 %collective-permute-start.17 = (bf16[72,384]{1,0:T(8,128)(2,1)S(1)}, bf16[72,384]{1,0:T(8,128)(2,1)S(1)}, u32[]{:S(2)}, u32[]{:S(2)}) collective-permute-start(bf16[72,384]{1,0:T(8,128)(2,1)S(1)} %add_convert_fusion.1.rest_0_), channel_id=1, source_target_pairs={{0,1},{1,0},{2,3},{3,2},{4,5},{5,4},{6,7},{7,6},{8,9},{9,8},{10,11... | collective-permute-start | bytes 165896 | tf_op jit(solution)/shard_map/ppermute | solution.py:340
  64.9 1.3 %gradient_keep.1.rest_2_ = f32[1,384,1536]{2,1,0:T(8,128)} custom-call(bf16[144,384]{1,0:T(8,128)(2,1)S(1)} %get-tuple-element.22.own_ref, bf16[72,384]{1,0:T(8,128)(2,1)S(1)} %add_convert_fusion.1.rest_0_, bf16[72,384]{1,0:T(8,128)(2,1)S(1)} %add_convert_fusion.rest_1_), custom_call_target="tpu_custom_call" | custom-call | flops 169869312 | bytes 1179648 | tf_op jit(solution)/shard_map/gradient_keep/pallas_call | solution.py:323
  66.9 1.2 %collective-permute-done.21.rest_1_ = bf16[72,384]{1,0:T(8,128)(2,1)S(1)} collective-permute-done((bf16[72,384]{1,0:T(8,128)(2,1)S(1)}, bf16[72,384]{1,0:T(8,128)(2,1)S(1)}, u32[]{:S(2)}, u32[]{:S(2)}) %collective-permute-start.21) | collective-permute-done | bytes 55328 | tf_op jit(solution)/shard_map/ppermute | solution.py:340
  68.1 1.3 %gradient_rest.1 = f32[1,384,1536]{2,1,0:T(8,128)} custom-call(bf16[144,384]{1,0:T(8,128)(2,1)S(1)} %get-tuple-element.22.own_ref, bf16[72,384]{1,0:T(8,128)(2,1)S(1)} %collective-permute-done.17.rest_0_, bf16[72,384]{1,0:T(8,128)(2,1)S(1)} %collective-permute-done.21.rest_1_, f32[1,384,1536]{2,1,0:T(8,128)} %gradient_keep.1.rest_2_), custom_call_target="tpu_custom_call", output_to_operand_aliasing={{}: (3, {})} | custom-call | flops 169869312 | bytes 1179648 | tf_op jit(solution)/shard_map/gradient_rest/pallas_call | solution.py:323
  (51 shorter events, 10.7 us)
Async XLA Ops:
  0.6 22.3 %copy-start.3 = (f32[1,3072]{1,0:T(1,128)S(1)}, f32[1,3072]{1,0:T(1,128)}, u32[]{:S(2)}) copy-start(f32[1,3072]{1,0:T(1,128)} %param.12) | copy-start | bytes 36868
  3.4 20.5 %copy-start.4 = (f32[384]{0:T(512)S(1)}, f32[384]{0:T(512)}, u32[]{:S(2)}) copy-start(f32[384]{0:T(512)} %param.10) | copy-start | bytes 4612
  3.5 20.5 %copy-start = (bf16[1,1536,64]{1,2,0:T(8,128)(2,1)S(1)}, bf16[1,1536,64]{1,2,0:T(8,128)(2,1)}, u32[]{:S(2)}) copy-start(bf16[1,1536,64]{1,2,0:T(8,128)(2,1)} %param.15) | copy-start | bytes 589828
  3.5 22.9 %copy-start.1 = (bf16[384,64]{0,1:T(8,128)(2,1)S(1)}, bf16[384,64]{0,1:T(8,128)(2,1)}, u32[]{:S(2)}) copy-start(bf16[384,64]{0,1:T(8,128)(2,1)} %param.8) | copy-start | bytes 147460
  3.5 22.9 %copy-start.2 = (bf16[384,64]{0,1:T(8,128)(2,1)S(1)}, bf16[384,64]{0,1:T(8,128)(2,1)}, u32[]{:S(2)}) copy-start(bf16[384,64]{0,1:T(8,128)(2,1)} %param.9) | copy-start | bytes 147460
  3.5 5.2 %collective-permute-start = (bf16[72,384]{1,0:T(8,128)(2,1)S(1)}, bf16[72,384]{1,0:T(8,128)(2,1)S(1)}, u32[]{:S(2)}, u32[]{:S(2)}) collective-permute-start(bf16[72,384]{1,0:T(8,128)(2,1)S(1)} %get-tuple-element.24), channel_id=1, source_target_pairs={{0,1},{1,0},{2,3},{3,2},{4,5},{5,4},{6,7},{7,6},{8,9},{9,8},{10,11... | collective-permute-start | bytes 165896 | tf_op jit(solution)/shard_map/ppermute | solution.py:340
  6.5 4.8 %collective-permute-start.3 = (bf16[72,384]{1,0:T(8,128)(2,1)S(1)}, bf16[72,384]{1,0:T(8,128)(2,1)S(1)}, u32[]{:S(2)}, u32[]{:S(2)}) collective-permute-start(bf16[72,384]{1,0:T(8,128)(2,1)S(1)} %get-tuple-element.26), channel_id=1, source_target_pairs={{0,1},{1,0},{2,3},{3,2},{4,5},{5,4},{6,7},{7,6},{8,9},{9,8},{10,11... | collective-permute-start | bytes 165896 | tf_op jit(solution)/shard_map/ppermute | solution.py:340
  8.7 4.8 %collective-permute-start.1 = (bf16[72,384]{1,0:T(8,128)(2,1)S(1)}, bf16[72,384]{1,0:T(8,128)(2,1)S(1)}, u32[]{:S(2)}, u32[]{:S(2)}) collective-permute-start(bf16[72,384]{1,0:T(8,128)(2,1)S(1)} %fusion.6), channel_id=1, source_target_pairs={{0,2},{1,3},{2,0},{3,1},{4,6},{5,7},{6,4},{7,5},{8,10},{9,11},{10,... | collective-permute-start | bytes 165896 | tf_op jit(solution)/shard_map/ppermute | solution.py:340
  11.3 5.6 %collective-permute-start.4 = (bf16[72,384]{1,0:T(8,128)(2,1)S(1)}, bf16[72,384]{1,0:T(8,128)(2,1)S(1)}, u32[]{:S(2)}, u32[]{:S(2)}) collective-permute-start(bf16[72,384]{1,0:T(8,128)(2,1)S(1)} %fusion.7), channel_id=1, source_target_pairs={{0,2},{1,3},{2,0},{3,1},{4,6},{5,7},{6,4},{7,5},{8,10},{9,11},{10,... | collective-permute-start | bytes 165896 | tf_op jit(solution)/shard_map/ppermute | solution.py:340
  13.5 5.6 %collective-permute-start.2 = (bf16[72,384]{1,0:T(8,128)(2,1)S(1)}, bf16[72,384]{1,0:T(8,128)(2,1)S(1)}, u32[]{:S(2)}, u32[]{:S(2)}) collective-permute-start(bf16[72,384]{1,0:T(8,128)(2,1)S(1)} %fusion.10), channel_id=1, source_target_pairs={{0,4},{1,5},{2,6},{3,7},{4,0},{5,1},{6,2},{7,3},{8,12},{9,13},{10,... | collective-permute-start | bytes 165896 | tf_op jit(solution)/shard_map/ppermute | solution.py:340
  17.0 5.1 %collective-permute-start.5 = (bf16[72,384]{1,0:T(8,128)(2,1)S(1)}, bf16[72,384]{1,0:T(8,128)(2,1)S(1)}, u32[]{:S(2)}, u32[]{:S(2)}) collective-permute-start(bf16[72,384]{1,0:T(8,128)(2,1)S(1)} %fusion.11), channel_id=1, source_target_pairs={{0,4},{1,5},{2,6},{3,7},{4,0},{5,1},{6,2},{7,3},{8,12},{9,13},{10,... | collective-permute-start | bytes 165896 | tf_op jit(solution)/shard_map/ppermute | solution.py:340
  19.2 5.0 %collective-permute-start.6 = (bf16[72,384]{1,0:T(8,128)(2,1)S(1)}, bf16[72,384]{1,0:T(8,128)(2,1)S(1)}, u32[]{:S(2)}, u32[]{:S(2)}) collective-permute-start(bf16[72,384]{1,0:T(8,128)(2,1)S(1)} %add_convert_fusion.3.rest_0_), channel_id=1, source_target_pairs={{0,1},{1,0},{2,3},{3,2},{4,5},{5,4},{6,7},{7,6},{8,9},{9,8},{10,11... | collective-permute-start | bytes 165896 | tf_op jit(solution)/shard_map/ppermute | solution.py:340
  22.1 4.2 %collective-permute-start.7 = (bf16[72,384]{1,0:T(8,128)(2,1)S(1)}, bf16[72,384]{1,0:T(8,128)(2,1)S(1)}, u32[]{:S(2)}, u32[]{:S(2)}) collective-permute-start(bf16[72,384]{1,0:T(8,128)(2,1)S(1)} %add_convert_fusion.2.rest_1_), channel_id=1, source_target_pairs={{0,1},{1,0},{2,3},{3,2},{4,5},{5,4},{6,7},{7,6},{8,9},{9,8},{10,11... | collective-permute-start | bytes 165896 | tf_op jit(solution)/shard_map/ppermute | solution.py:340
  27.9 6.2 %collective-permute-start.10 = (bf16[64,384]{1,0:T(8,128)(2,1)S(1)}, bf16[64,384]{1,0:T(8,128)(2,1)S(1)}, u32[]{:S(2)}, u32[]{:S(2)}) collective-permute-start(bf16[64,384]{1,0:T(8,128)(2,1)S(1)} %get-tuple-element.27.own_ref), channel_id=1, source_target_pairs={{0,24},{24,0},{8,8},{16,16},{1,25},{25,1},{9,9},{17,17},{2,26},{26... | collective-permute-start | bytes 147464 | tf_op jit(solution)/shard_map/ppermute | solution.py:345
  29.8 6.0 %collective-permute-start.9 = (bf16[64,384]{1,0:T(8,128)(2,1)S(1)}, bf16[64,384]{1,0:T(8,128)(2,1)S(1)}, u32[]{:S(2)}, u32[]{:S(2)}) collective-permute-start(bf16[64,384]{1,0:T(8,128)(2,1)S(1)} %get-tuple-element.27.own_ref), channel_id=1, source_target_pairs={{0,16},{16,0},{8,8},{24,24},{1,17},{17,1},{9,9},{25,25},{2,18},{18... | collective-permute-start | bytes 147464 | tf_op jit(solution)/shard_map/ppermute | solution.py:345
  31.9 3.8 %collective-permute-start.8 = (bf16[64,384]{1,0:T(8,128)(2,1)S(1)}, bf16[64,384]{1,0:T(8,128)(2,1)S(1)}, u32[]{:S(2)}, u32[]{:S(2)}) collective-permute-start(bf16[64,384]{1,0:T(8,128)(2,1)S(1)} %get-tuple-element.27.own_ref), channel_id=1, source_target_pairs={{0,8},{8,0},{16,16},{24,24},{1,9},{9,1},{17,17},{25,25},{2,10},{10... | collective-permute-start | bytes 147464 | tf_op jit(solution)/shard_map/ppermute | solution.py:345
  38.0 6.6 %collective-permute-start.13 = (bf16[64,384]{1,0:T(8,128)(2,1)S(1)}, bf16[64,384]{1,0:T(8,128)(2,1)S(1)}, u32[]{:S(2)}, u32[]{:S(2)}) collective-permute-start(bf16[64,384]{1,0:T(8,128)(2,1)S(1)} %get-tuple-element.30.piece_ref), channel_id=1, source_target_pairs={{0,16},{16,0},{8,8},{24,24},{1,17},{17,1},{9,9},{25,25},{2,18},{18... | collective-permute-start | bytes 147464 | tf_op jit(solution)/shard_map/ppermute | solution.py:345
  40.2 4.5 %collective-permute-start.12 = (bf16[64,384]{1,0:T(8,128)(2,1)S(1)}, bf16[64,384]{1,0:T(8,128)(2,1)S(1)}, u32[]{:S(2)}, u32[]{:S(2)}) collective-permute-start(bf16[64,384]{1,0:T(8,128)(2,1)S(1)} %get-tuple-element.30.piece_ref), channel_id=1, source_target_pairs={{0,8},{8,0},{16,16},{24,24},{1,9},{9,1},{17,17},{25,25},{2,10},{10... | collective-permute-start | bytes 147464 | tf_op jit(solution)/shard_map/ppermute | solution.py:345
  42.1 5.4 %collective-permute-start.11 = (bf16[64,384]{1,0:T(8,128)(2,1)S(1)}, bf16[64,384]{1,0:T(8,128)(2,1)S(1)}, u32[]{:S(2)}, u32[]{:S(2)}) collective-permute-start(bf16[64,384]{1,0:T(8,128)(2,1)S(1)} %get-tuple-element.30.piece_ref), channel_id=1, source_target_pairs={{0,24},{24,0},{8,8},{16,16},{1,25},{25,1},{9,9},{17,17},{2,26},{26... | collective-permute-start | bytes 147464 | tf_op jit(solution)/shard_map/ppermute | solution.py:345
  48.3 4.2 %collective-permute-start.14 = (bf16[72,384]{1,0:T(8,128)(2,1)S(1)}, bf16[72,384]{1,0:T(8,128)(2,1)S(1)}, u32[]{:S(2)}, u32[]{:S(2)}) collective-permute-start(bf16[72,384]{1,0:T(8,128)(2,1)S(1)} %get-tuple-element.38), channel_id=1, source_target_pairs={{0,1},{1,0},{2,3},{3,2},{4,5},{5,4},{6,7},{7,6},{8,9},{9,8},{10,11... | collective-permute-start | bytes 165896 | tf_op jit(solution)/shard_map/ppermute | solution.py:340
  49.1 4.7 %collective-permute-start.18 = (bf16[72,384]{1,0:T(8,128)(2,1)S(1)}, bf16[72,384]{1,0:T(8,128)(2,1)S(1)}, u32[]{:S(2)}, u32[]{:S(2)}) collective-permute-start(bf16[72,384]{1,0:T(8,128)(2,1)S(1)} %get-tuple-element.40), channel_id=1, source_target_pairs={{0,1},{1,0},{2,3},{3,2},{4,5},{5,4},{6,7},{7,6},{8,9},{9,8},{10,11... | collective-permute-start | bytes 165896 | tf_op jit(solution)/shard_map/ppermute | solution.py:340
  52.5 4.4 %collective-permute-start.15 = (bf16[72,384]{1,0:T(8,128)(2,1)S(1)}, bf16[72,384]{1,0:T(8,128)(2,1)S(1)}, u32[]{:S(2)}, u32[]{:S(2)}) collective-permute-start(bf16[72,384]{1,0:T(8,128)(2,1)S(1)} %fusion.8), channel_id=1, source_target_pairs={{0,2},{1,3},{2,0},{3,1},{4,6},{5,7},{6,4},{7,5},{8,10},{9,11},{10,... | collective-permute-start | bytes 165896 | tf_op jit(solution)/shard_map/ppermute | solution.py:340
  53.8 4.7 %collective-permute-start.19 = (bf16[72,384]{1,0:T(8,128)(2,1)S(1)}, bf16[72,384]{1,0:T(8,128)(2,1)S(1)}, u32[]{:S(2)}, u32[]{:S(2)}) collective-permute-start(bf16[72,384]{1,0:T(8,128)(2,1)S(1)} %fusion.9), channel_id=1, source_target_pairs={{0,2},{1,3},{2,0},{3,1},{4,6},{5,7},{6,4},{7,5},{8,10},{9,11},{10,... | collective-permute-start | bytes 165896 | tf_op jit(solution)/shard_map/ppermute | solution.py:340
  57.0 5.7 %collective-permute-start.16 = (bf16[72,384]{1,0:T(8,128)(2,1)S(1)}, bf16[72,384]{1,0:T(8,128)(2,1)S(1)}, u32[]{:S(2)}, u32[]{:S(2)}) collective-permute-start(bf16[72,384]{1,0:T(8,128)(2,1)S(1)} %fusion.12), channel_id=1, source_target_pairs={{0,4},{1,5},{2,6},{3,7},{4,0},{5,1},{6,2},{7,3},{8,12},{9,13},{10,... | collective-permute-start | bytes 165896 | tf_op jit(solution)/shard_map/ppermute | solution.py:340
  58.5 5.4 %collective-permute-start.20 = (bf16[72,384]{1,0:T(8,128)(2,1)S(1)}, bf16[72,384]{1,0:T(8,128)(2,1)S(1)}, u32[]{:S(2)}, u32[]{:S(2)}) collective-permute-start(bf16[72,384]{1,0:T(8,128)(2,1)S(1)} %fusion.13), channel_id=1, source_target_pairs={{0,4},{1,5},{2,6},{3,7},{4,0},{5,1},{6,2},{7,3},{8,12},{9,13},{10,... | collective-permute-start | bytes 165896 | tf_op jit(solution)/shard_map/ppermute | solution.py:340
  62.7 4.2 %collective-permute-start.17 = (bf16[72,384]{1,0:T(8,128)(2,1)S(1)}, bf16[72,384]{1,0:T(8,128)(2,1)S(1)}, u32[]{:S(2)}, u32[]{:S(2)}) collective-permute-start(bf16[72,384]{1,0:T(8,128)(2,1)S(1)} %add_convert_fusion.1.rest_0_), channel_id=1, source_target_pairs={{0,1},{1,0},{2,3},{3,2},{4,5},{5,4},{6,7},{7,6},{8,9},{9,8},{10,11... | collective-permute-start | bytes 165896 | tf_op jit(solution)/shard_map/ppermute | solution.py:340
  63.9 4.2 %collective-permute-start.21 = (bf16[72,384]{1,0:T(8,128)(2,1)S(1)}, bf16[72,384]{1,0:T(8,128)(2,1)S(1)}, u32[]{:S(2)}, u32[]{:S(2)}) collective-permute-start(bf16[72,384]{1,0:T(8,128)(2,1)S(1)} %add_convert_fusion.rest_1_), channel_id=1, source_target_pairs={{0,1},{1,0},{2,3},{3,2},{4,5},{5,4},{6,7},{7,6},{8,9},{9,8},{10,11... | collective-permute-start | bytes 165896 | tf_op jit(solution)/shard_map/ppermute | solution.py:340

commit v2 on v1

--- a/solution.py
+++ b/solution.py
@@ -132,89 +132,108 @@
 def first_kernel(latent_ref, noise_ref, level_ref, gram_ref, *rest, width):
     *proj_refs, readout_ref, out_ref, mix_ref, gram_out_ref = rest
     channels, tokens = latent_ref.shape
-    wide = widen(latent_ref[...], jnp.ones((1, tokens), f32))
-    out_ref[...], unused, unused = forward(wide, gram_ref, proj_refs, readout_ref, width)
     level = level_ref[...]
     mix_ref[:channels, :] = level * noise_ref[...].astype(f32)
     mix_ref[channels:, :] = jnp.broadcast_to(level, (extra, tokens))
     gram_out_ref[...] = gram_ref[...]
 
-
-def second_kernel(source_ref, own_ref, by1_ref, by2_ref, by3_ref, mix_ref, gram_ref, *rest, width):
+    @pl.when(lax.axis_index("role") == 0)
+    def _():
+        wide = widen(latent_ref[...], jnp.ones((1, tokens), f32))
+        out_ref[...], unused, unused = forward(wide, gram_ref, proj_refs, readout_ref, width)
+
+
+def in_parts(scale, wide):
+    scaled = scale * wide
+    return jnp.concatenate([scaled, scaled - scaled.astype(bf16).astype(f32)], axis=0).astype(bf16)
+
+
+def slope_kernel(latent_ref, gram_ref, *rest, width):
+    *proj_refs, slope_ref, scaled_ref = rest
+    tile = proj_refs[0].shape[1]
+
+    @pl.when(lax.axis_index("role") == 0)
+    def _():
+        wide = widen(latent_ref[...], jnp.ones((1, latent_ref.shape[1]), f32))
+        scale, unused = norm_scale(wide, gram_ref[...], width)
+        wide16 = wide.astype(bf16)
+        for at, proj_ref in enumerate(proj_refs):
+            hidden = scale * mm(proj_ref[...], wide16, 0, 0)
+            square, bent = gelu_parts(hidden)
+            slope_ref[at * tile : (at + 1) * tile, :] = gelu_slope(hidden, square, bent)
+        scaled_ref[...] = in_parts(scale, wide)
+
+
+def second_kernel(near_ref, far_ref, mix_ref, gram_ref, *rest, width):
     proj_refs = rest[: 2 * pieces]
     readout_ref, columns_ref, generated_ref, piece_ref, flat_ref, slope_ref, scaled_ref = rest[2 * pieces :]
     role, upper = lax.axis_index("role"), lax.axis_index("fsdp") & 1
-    channels, tokens = source_ref.shape
+    channels, tokens = near_ref.shape
     half = proj_refs[0].shape[1] * pieces
     tile = half // pieces
-    level = mix_ref[channels : channels + 1, :]
-    first = role == 0
-    generated = jnp.where(
-        first,
-        own_ref[...].astype(f32),
-        jnp.where(
-            role == 3,
-            by3_ref[...].astype(f32),
-            jnp.where(role == 2, by2_ref[...].astype(f32), by1_ref[...].astype(f32)),
-        ),
-    )
+    generated = jnp.where(role < 2, near_ref[...].astype(f32), far_ref[...].astype(f32))
     generated_ref[...] = generated.astype(bf16)
-    noised = (1.0 - level) * generated + mix_ref[:channels, :]
-    latent = jnp.where(first, source_ref[...].astype(f32), noised.astype(bf16).astype(f32))
-    wide = widen(latent, jnp.where(first, 1.0, level))
-    scores, scale, seen = forward(wide, gram_ref, proj_refs, readout_ref, width, slope_ref)
-    piece_ref[...] = scores
-    logit = jnp.sum(scores.astype(f32), axis=0, keepdims=True)
-    flat_ref[...] = 1.0 / (1.0 + jnp.exp(-logit))
-
-    @pl.when(role == 3)
+
+    @pl.when(role > 0)
     def _():
-        high, low = halves(-1.0 / (1.0 + jnp.exp(logit)))
-        cot = jnp.concatenate(
-            [
-                jnp.broadcast_to(high, (channels, tokens)),
-                jnp.broadcast_to(low, (channels, tokens)),
-            ],
-            axis=0,
-        )
-        back_rows = jnp.zeros(wide.shape, f32)
-        for at, proj_ref in enumerate(proj_refs):
+        level = mix_ref[channels : channels + 1, :]
+        noised = (1.0 - level) * generated + mix_ref[:channels, :]
+        wide = widen(noised.astype(bf16), level)
+        scores, scale, seen = forward(wide, gram_ref, proj_refs, readout_ref, width, slope_ref)
+        piece_ref[...] = scores
+        logit = jnp.sum(scores.astype(f32), axis=0, keepdims=True)
+        flat_ref[...] = 1.0 / (1.0 + jnp.exp(-logit))
+        scaled_ref[...] = in_parts(scale, wide)
+
+        @pl.when(role == 3)
+        def _():
+            high, low = halves(-1.0 / (1.0 + jnp.exp(logit)))
+            cot = jnp.concatenate(
+                [
+                    jnp.broadcast_to(high, (channels, tokens)),
+                    jnp.broadcast_to(low, (channels, tokens)),
+                ],
+                axis=0,
+            )
+            back_rows = jnp.zeros(wide.shape, f32)
+            for at, proj_ref in enumerate(proj_refs):
+                back = mm(columns_ref[columns_of(at, half, upper), :], cot, 1, 0)
+                hcot = (back * slope_ref[at * tile : (at + 1) * tile, :]).astype(bf16)
+                back_rows = back_rows + mm(proj_ref[...], hcot, 1, 0)
+            inner = scale * jnp.sum(back_rows * wide, axis=0, keepdims=True)
+            latent_back = scale * back_rows[:channels] - (scale * scale * inner * (1.0 / width)) * seen[:channels]
+            piece_ref[...] = (adv_weight * (1.0 - level) * latent_back).astype(bf16)
+
+
+def pull_back(cot, tail, out_refs, first_piece):
+    upper = lax.axis_index("fsdp") & 1
+    first = lax.axis_index("role") == 0
+    rows, tile = out_refs[0].shape
+    half = tile * pieces
+    columns_ref = tail[4]
+
+    def with_slopes(slope_ref, scaled_ref):
+        scaled = scaled_ref[...]
+        for at, out_ref in enumerate(out_refs, first_piece):
             back = mm(columns_ref[columns_of(at, half, upper), :], cot, 1, 0)
             hcot = (back * slope_ref[at * tile : (at + 1) * tile, :]).astype(bf16)
-            back_rows = back_rows + mm(proj_ref[...], hcot, 1, 0)
-        inner = scale * jnp.sum(back_rows * wide, axis=0, keepdims=True)
-        latent_back = scale * back_rows[:channels] - (scale * scale * inner * (1.0 / width)) * seen[:channels]
-        piece_ref[...] = (adv_weight * (1.0 - level) * latent_back).astype(bf16)
-
-    scaled = scale * wide
-    scaled_ref[...] = jnp.concatenate([scaled, scaled - scaled.astype(bf16).astype(f32)], axis=0).astype(bf16)
-
-
-def pull_back(cot, slope_ref, scaled_ref, columns_ref, out_refs, first_piece):
-    upper = lax.axis_index("fsdp") & 1
-    rows, tile = out_refs[0].shape
-    half = tile * pieces
-    scaled = scaled_ref[...]
-    for at, out_ref in enumerate(out_refs, first_piece):
-        back = mm(columns_ref[columns_of(at, half, upper), :], cot, 1, 0)
-        hcot = (back * slope_ref[at * tile : (at + 1) * tile, :]).astype(bf16)
-        part = mm(scaled, hcot, 1, 1)
-        out_ref[...] = (part[:rows] + part[rows:]).astype(out_ref.dtype)
+            part = mm(scaled, hcot, 1, 1)
+            out_ref[...] = (part[:rows] + part[rows:]).astype(out_ref.dtype)
+
+    pl.when(first)(lambda: with_slopes(*tail[0:2]))
+    pl.when(jnp.logical_not(first))(lambda: with_slopes(*tail[2:4]))
 
 
 def send_kernel(
+    real_ref,
     adversarial_ref,
-    real_ref,
     fake_ref,
     generated_ref,
     piece_ref,
     flat_ref,
-    slope_ref,
-    scaled_ref,
-    columns_ref,
-    cot_ref,
-    *out_refs,
+    *rest,
 ):
+    tail, cot_ref, out_refs = rest[:5], rest[5], rest[6:]
     role = lax.axis_index("role")
     first = role == 0
     generated = generated_ref[...].astype(f32)
@@ -236,19 +255,18 @@
     ).astype(bf16)
     cot = jnp.concatenate([left, right], axis=0)
     cot_ref[...] = cot
-    pull_back(cot, slope_ref, scaled_ref, columns_ref, out_refs, pieces)
-
-
-def keep_kernel(cot_ref, slope_ref, scaled_ref, columns_ref, *out_refs):
-    pull_back(cot_ref[...], slope_ref, scaled_ref, columns_ref, out_refs, 0)
-
-
-def grad_kernel(own_ref, *rest, factor, keep):
-    total_refs = rest[:pieces]
-    *unused, out_ref, buffer, sems = rest[pieces:]
+    pull_back(cot, tail, out_refs, pieces)
+
+
+def keep_kernel(cot_ref, *rest):
+    pull_back(cot_ref[...], rest[:5], rest[5:], 0)
+
+
+def grad_kernel(own_ref, *rest, factor, first_piece, count):
+    total_refs = rest[:count]
+    *unused, out_ref, buffer, sems = rest[count:]
     upper = lax.axis_index("fsdp") & 1
-    half = buffer.shape[1]
-    tile = half // pieces
+    tile = buffer.shape[1] // count
     own = own_ref[...]
     copies = []
     for at, total_ref in enumerate(total_refs):
@@ -256,7 +274,7 @@
         total = total_ref[...].astype(f32)
         part = mm(own, jnp.concatenate([total, total], axis=0).astype(bf16), 0, 0)
         buffer[:, here] = part * factor
-        cols = columns_of(at if keep else at + pieces, half, upper)
+        cols = columns_of(first_piece + at, tile * pieces, upper)
         copy = pltpu.make_async_copy(buffer.at[:, here], out_ref.at[0, :, cols], sems.at[at])
         copy.start()
         copies.append(copy)
@@ -310,39 +328,35 @@
     )(embed_w, vectors, block_weight)
 
 
-def gradient(own, totals, factor, cols, buffer=None):
-    depth, half = own.shape[1], cols // 2
-    keep = buffer is None
+def gradient(own, totals, first_piece, factor, cols, buffer=None):
+    depth, tile, count = own.shape[1], cols // (2 * pieces), len(totals)
     vmem = pl.BlockSpec(memory_space=pltpu.VMEM)
     hbm = pl.BlockSpec(memory_space=pltpu.HBM)
-    specs = [vmem] * (1 + pieces)
+    specs = [vmem] * (1 + count)
     inputs = [own, *totals]
-    if not keep:
+    if buffer is not None:
         specs.append(hbm)
         inputs.append(buffer)
     return pl.pallas_call(
-        functools.partial(grad_kernel, factor=factor, keep=keep),
+        functools.partial(grad_kernel, factor=factor, first_piece=first_piece, count=count),
         out_shape=jax.ShapeDtypeStruct((1, depth, cols), f32),
         in_specs=specs,
         out_specs=hbm,
-        input_output_aliases={} if keep else {len(inputs) - 1: 0},
-        scratch_shapes=[pltpu.VMEM((depth, half), f32), pltpu.SemaphoreType.DMA((pieces,))],
+        input_output_aliases={} if buffer is None else {len(inputs) - 1: 0},
+        scratch_shapes=[pltpu.VMEM((depth, count * tile), f32), pltpu.SemaphoreType.DMA((count,))],
         compiler_params=pltpu.CompilerParams(vmem_limit_bytes=16 * 1024 * 1024),
         cost_estimate=pl.CostEstimate(
-            flops=4 * own.shape[0] * depth * half, bytes_accessed=4 * depth * half, transcendentals=0
+            flops=4 * own.shape[0] * depth * count * tile,
+            bytes_accessed=4 * depth * count * tile,
+            transcendentals=0,
         ),
-        name="gradient_keep" if keep else "gradient_rest",
+        name="gradient",
     )(*inputs)
 
 
 def swap(values, axis, n, bit):
     pairs = [(i, i ^ bit) for i in range(n)]
     return [lax.ppermute(value, axis, pairs) for value in values]
-
-
-def with_first(value, roles, other):
-    pairs = [(0, other), (other, 0)] + [(i, i) for i in range(1, roles) if i != other]
-    return lax.ppermute(value, "role", pairs)
 
 
 def add_along(mine, received, n):
@@ -398,30 +412,39 @@
         [latent_shape, shape((rows, tokens), f32), shape((rows, rows), f32)],
         (source, score_noise.T, level, gram, *proj, readout),
     )
-    by3, by2, by1 = (with_first(own_first, roles, other) for other in (3, 2, 1))
-    drawn = jnp.where(role == 0, own_first, jnp.where(role == 1, by1, jnp.where(role == 2, by2, by3)))
-    generated, piece, flat, slope, scaled = call(
+    (by1,) = swap([own_first], "role", roles, 1)
+    near = jnp.where(role == 1, by1, own_first)
+    (by2,) = swap([near], "role", roles, 2)
+    drawn = jnp.where(role < 2, near, by2)
+    slope_shapes = [shape((cols, tokens), f32), shape((2 * rows, tokens), bf16)]
+    first_slopes = call(
+        functools.partial(slope_kernel, width=width),
+        "slopes",
+        slope_shapes,
+        (source, gram, *proj),
+        cost=2 * rows * tokens * cols,
+    )
+    generated, piece, flat, *slopes = call(
         functools.partial(second_kernel, width=width),
         "score",
         [
             latent_shape,
             latent_shape,
             shape((1, tokens), f32),
-            shape((cols, tokens), f32),
-            shape((2 * rows, tokens), bf16),
+            *slope_shapes,
         ],
-        (source, own_first, by1, by2, by3, mix, gram, *proj, readout, columns),
-    )
-    real, fake, adversarial = (with_first(piece, roles, other) for other in (1, 2, 3))
+        (near, by2, mix, gram, *proj, readout, columns),
+    )
+    fake, adversarial, real = (swap([piece], "role", roles, bit)[0] for bit in (2, 3, 1))
     flat, drawn = lax.optimization_barrier((flat, drawn))
 
     cost = 4 * rows * tokens * half
-    tail = (slope, scaled, columns)
+    tail = (*first_slopes, *slopes, columns)
     cot, *send = call(
         send_kernel,
         "cotangent_send",
         [shape((2 * channels, tokens), bf16)] + [shape((rows, half // pieces), bf16)] * pieces,
-        (adversarial, real, fake, generated, piece, flat, *tail),
+        (real, adversarial, fake, generated, piece, flat, *tail),
         cost=cost,
     )
     received = swap(send, "fsdp", n, 1)
@@ -431,8 +454,9 @@
     totals = add_along(kept, received, n)
     others = swap(totals, "fsdp", n, 1)
     factor = 1.0 / math.sqrt(tokens * n)
-    grads = gradient(own_rows, totals, factor, cols)
-    grads = gradient(own_rows, others, factor, cols, grads)
+    grads = gradient(own_rows, totals, 0, factor, cols)
+    for at, other in enumerate(others, pieces):
+        grads = gradient(own_rows, [other], at, factor, cols, grads)
     return (grads, drawn.T)
 
 

time: 69.9 us -> 62.5 us (0.89)
  starting transfers between devices: 36 us -> 25.7 us
  waiting for transfers between devices: 18.3 us -> 21.2 us
    ppermute x6 -> x0, starting transfers between devices: 12 us -> none  [with_first(): return lax.ppermute(value, 'role', pairs)]
    ppermute x16 -> x21, waiting for transfers between devices: 13.8 us -> 21.2 us  [swap(): return [lax.ppermute(value, axis, pairs) for value in values]]
    ppermute x6 -> x0, waiting for transfers between devices: 4.51 us -> none  [with_first(): return lax.ppermute(value, 'role', pairs)]
    ppermute x16 -> x21, starting transfers between devices: 24.1 us -> 25.7 us  [swap(): return [lax.ppermute(value, axis, pairs) for value in values]]
    pallas_call x2 -> x3, Pallas kernels: 2.66 us -> 3.58 us  [gradient(): pl.pallas_call(functools.partial(grad_kernel, factor=factor, first_piece=...]
    pallas_call x4 -> x5, Pallas kernels: 5.22 us -> 4.65 us  [call(): pl.pallas_call(kernel, out_shape=out_shape, in_specs=[vmem] * len(inputs)...]
  transfers between devices with their start and end apart: 22 -> 21, of which waited for: 12 -> 15; matrix products, arithmetic and copies ran while one was open for 5% -> 6% of each run, Pallas kernels for 3% -> 8%
where the time goes in v2:
time: 62.5 us; the launch traced here: 62.3 us
  starting transfers between devices  25.7 us (41%)
  waiting for transfers between devices  21.2 us (34%)
  Pallas kernels  10.2 us (16%)
  other arithmetic  3.01 us (5%)
  matrix products  0.98 us (2%)
  between operations  0.9 us (1%)
    ppermute x21, starting transfers between devices, swap(): return [lax.ppermute(value, axis, pairs) for value in values]  25.7 us
    ppermute x21, waiting for transfers between devices, swap(): return [lax.ppermute(value, axis, pairs) for value in values]  21.2 us
    pallas_call x5, Pallas kernels, call(): pl.pallas_call(kernel, out_shape=out_shape, in_specs=[vmem] * len(inputs)...  4.65 us
    pallas_call x3, Pallas kernels, gradient(): pl.pallas_call(functools.partial(grad_kernel, factor=factor, first_piece=...  3.58 us
    pallas_call x1, Pallas kernels, part_of(): pl.pallas_call(part_kernel, out_shape=shapes, in_specs=[hbm, vmem, hbm],...  1.99 us
  transfers between devices with their start and end apart: 21, of which 15 were waited for; matrix products, arithmetic and copies ran while one was open for 6% of the time, Pallas kernels for 8%

profile of v2, /device:TPU:0, one launch (start us, length us, event | category | flops | bytes accessed | tf_op | source)
XLA Modules:
  0.0 62.3 jit_solution(2954820981612462620)
XLA Ops:
  1.4 2.0 %part.1 = (f32[72,384]{1,0:T(8,128)S(1)}, f32[72,384]{1,0:T(8,128)S(1)}, bf16[72,384]{1,0:T(8,128)(2,1)S(1)}, bf16[72,384]{1,0:T(8,128)(2,1)S(1)}, bf16[144,384]{1,0:T(8,128)(2,1)S(1)}) custom-call(bf16[64,3072]{1,0:T(8,128)(2,1)} %bitcast.19, f32[2,3072]{1,0:T(2,128)S(1)} %pad_maximum_fusion.vectors_ref, bf16[1,384,1536]{2,1,0:T(8,128)(2,1)} %block_ref.1), custom_call_target="tpu_custom_call" | custom-call | flops 169869312 | bytes 1179648 | tf_op jit(solution)/shard_map/part/pallas_call | solution.py:313
  3.5 3.0 %collective-permute-start = (bf16[72,384]{1,0:T(8,128)(2,1)S(1)}, bf16[72,384]{1,0:T(8,128)(2,1)S(1)}, u32[]{:S(2)}, u32[]{:S(2)}) collective-permute-start(bf16[72,384]{1,0:T(8,128)(2,1)S(1)} %get-tuple-element.26), channel_id=1, source_target_pairs={{0,1},{1,0},{2,3},{3,2},{4,5},{5,4},{6,7},{7,6},{8,9},{9,8},{10,11... | collective-permute-start | bytes 165896 | tf_op jit(solution)/shard_map/ppermute | solution.py:359
  6.6 1.0 %bitcast_convert_fusion = f32[64,3072]{1,0:T(8,128)S(1)} fusion(bf16[1,64,3072]{2,1,0:T(8,128)(2,1)} %param.11), kind=kLoop, calls=%fused_computation.31 | loop fusion | flops 196608 | bytes 1179648 | tf_op jit(solution)/shard_map/convert_element_type | solution.py:401
  7.7 0.9 %collective-permute-done = bf16[72,384]{1,0:T(8,128)(2,1)S(1)} collective-permute-done((bf16[72,384]{1,0:T(8,128)(2,1)S(1)}, bf16[72,384]{1,0:T(8,128)(2,1)S(1)}, u32[]{:S(2)}, u32[]{:S(2)}) %collective-permute-start) | collective-permute-done | bytes 55328 | tf_op jit(solution)/shard_map/ppermute | solution.py:359
  8.7 2.6 %collective-permute-start.1 = (bf16[72,384]{1,0:T(8,128)(2,1)S(1)}, bf16[72,384]{1,0:T(8,128)(2,1)S(1)}, u32[]{:S(2)}, u32[]{:S(2)}) collective-permute-start(bf16[72,384]{1,0:T(8,128)(2,1)S(1)} %fusion.6), channel_id=1, source_target_pairs={{0,2},{1,3},{2,0},{3,1},{4,6},{5,7},{6,4},{7,5},{8,10},{9,11},{10,... | collective-permute-start | bytes 165896 | tf_op jit(solution)/shard_map/ppermute | solution.py:359
  11.3 1.0 %collective-permute-start.4 = (bf16[72,384]{1,0:T(8,128)(2,1)S(1)}, bf16[72,384]{1,0:T(8,128)(2,1)S(1)}, u32[]{:S(2)}, u32[]{:S(2)}) collective-permute-start(bf16[72,384]{1,0:T(8,128)(2,1)S(1)} %fusion.7), channel_id=1, source_target_pairs={{0,2},{1,3},{2,0},{3,1},{4,6},{5,7},{6,4},{7,5},{8,10},{9,11},{10,... | collective-permute-start | bytes 165896 | tf_op jit(solution)/shard_map/ppermute | solution.py:359
  12.3 1.1 %collective-permute-done.1 = bf16[72,384]{1,0:T(8,128)(2,1)S(1)} collective-permute-done((bf16[72,384]{1,0:T(8,128)(2,1)S(1)}, bf16[72,384]{1,0:T(8,128)(2,1)S(1)}, u32[]{:S(2)}, u32[]{:S(2)}) %collective-permute-start.1) | collective-permute-done | bytes 55328 | tf_op jit(solution)/shard_map/ppermute | solution.py:359
  13.5 3.5 %collective-permute-start.2 = (bf16[72,384]{1,0:T(8,128)(2,1)S(1)}, bf16[72,384]{1,0:T(8,128)(2,1)S(1)}, u32[]{:S(2)}, u32[]{:S(2)}) collective-permute-start(bf16[72,384]{1,0:T(8,128)(2,1)S(1)} %fusion.10), channel_id=1, source_target_pairs={{0,4},{1,5},{2,6},{3,7},{4,0},{5,1},{6,2},{7,3},{8,12},{9,13},{10,... | collective-permute-start | bytes 165896 | tf_op jit(solution)/shard_map/ppermute | solution.py:359
  17.0 1.3 %collective-permute-start.5 = (bf16[72,384]{1,0:T(8,128)(2,1)S(1)}, bf16[72,384]{1,0:T(8,128)(2,1)S(1)}, u32[]{:S(2)}, u32[]{:S(2)}) collective-permute-start(bf16[72,384]{1,0:T(8,128)(2,1)S(1)} %fusion.11), channel_id=1, source_target_pairs={{0,4},{1,5},{2,6},{3,7},{4,0},{5,1},{6,2},{7,3},{8,12},{9,13},{10,... | collective-permute-start | bytes 165896 | tf_op jit(solution)/shard_map/ppermute | solution.py:359
  18.2 0.9 %collective-permute-done.2 = bf16[72,384]{1,0:T(8,128)(2,1)S(1)} collective-permute-done((bf16[72,384]{1,0:T(8,128)(2,1)S(1)}, bf16[72,384]{1,0:T(8,128)(2,1)S(1)}, u32[]{:S(2)}, u32[]{:S(2)}) %collective-permute-start.2) | collective-permute-done | bytes 55328 | tf_op jit(solution)/shard_map/ppermute | solution.py:359
  19.2 2.2 %collective-permute-start.6 = (bf16[72,384]{1,0:T(8,128)(2,1)S(1)}, bf16[72,384]{1,0:T(8,128)(2,1)S(1)}, u32[]{:S(2)}, u32[]{:S(2)}) collective-permute-start(bf16[72,384]{1,0:T(8,128)(2,1)S(1)} %add_convert_fusion.3.rest_0_), channel_id=1, source_target_pairs={{0,1},{1,0},{2,3},{3,2},{4,5},{5,4},{6,7},{7,6},{8,9},{9,8},{10,11... | collective-permute-start | bytes 165896 | tf_op jit(solution)/shard_map/ppermute | solution.py:359
  22.9 1.0 %fusion.gram_ref = f32[72,72]{1,0:T(8,128)S(1)} fusion(f32[3,3072]{1,0:T(4,128)S(1)} %broadcast_in_dim.15, f32[64,3072]{1,0:T(8,128)S(1)} %bitcast_convert_fusion, f32[72]{0:T(128)S(1)} %pad.4.clone), kind=kOutput, calls=%fused_computation | convolution fusion | flops 191545344 | bytes 844320 | tf_op jit(solution)/shard_map/dot_general | solution.py:403
  23.9 2.4 %collective-permute-done.7.rest_3_ = bf16[72,384]{1,0:T(8,128)(2,1)S(1)} collective-permute-done((bf16[72,384]{1,0:T(8,128)(2,1)S(1)}, bf16[72,384]{1,0:T(8,128)(2,1)S(1)}, u32[]{:S(2)}, u32[]{:S(2)}) %collective-permute-start.7) | collective-permute-done | bytes 55328 | tf_op jit(solution)/shard_map/ppermute | solution.py:359
  26.4 1.5 %generator.1 = (bf16[64,384]{1,0:T(8,128)(2,1)S(1)}, f32[72,384]{1,0:T(8,128)S(1)}, f32[72,72]{1,0:T(8,128)S(1)}) custom-call(bf16[64,384]{1,0:T(8,128)(2,1)S(1)} %bitcast.16, bf16[64,384]{1,0:T(8,128)(2,1)S(1)} %bitcast.15, f32[1,384]{1,0:T(1,128)S(1)} %broadcast_in_dim.13.level_ref, f32[72,72]{1,0:T(8,128)S(1)} %fusion.gram_ref, ...), custom_call_target="tpu_custom_call" | custom-call | tf_op jit(solution)/shard_map/generator/pallas_call | solution.py:288
  28.2 1.0 %collective-permute-done.8 = bf16[64,384]{1,0:T(8,128)(2,1)S(1)} collective-permute-done((bf16[64,384]{1,0:T(8,128)(2,1)S(1)}, bf16[64,384]{1,0:T(8,128)(2,1)S(1)}, u32[]{:S(2)}, u32[]{:S(2)}) %collective-permute-start.8) | collective-permute-done | bytes 49184 | tf_op jit(solution)/shard_map/ppermute | solution.py:359
  29.5 1.6 %slopes.1 = (f32[1536,384]{1,0:T(8,128)S(1)}, bf16[144,384]{1,0:T(8,128)(2,1)S(1)}) custom-call(bf16[64,384]{1,0:T(8,128)(2,1)S(1)} %bitcast.17, f32[72,72]{1,0:T(8,128)S(1)} %get-tuple-element.31.gram_ref, bf16[72,384]{1,0:T(8,128)(2,1)S(1)} %add_convert_fusion.3.rest_0_, bf16[72,384]{1,0:T(8,128)(2,1)S(1)} %add_convert_fusion.2.rest_1_, ...), custom_call_target="tpu_custom_call" | custom-call | flops 84934656 | bytes 84934 | tf_op jit(solution)/shard_map/slopes/pallas_call | solution.py:288
  31.1 2.2 %collective-permute-done.9.far_ref = bf16[64,384]{1,0:T(8,128)(2,1)S(1)} collective-permute-done((bf16[64,384]{1,0:T(8,128)(2,1)S(1)}, bf16[64,384]{1,0:T(8,128)(2,1)S(1)}, u32[]{:S(2)}, u32[]{:S(2)}) %collective-permute-start.9) | collective-permute-done | bytes 49184 | tf_op jit(solution)/shard_map/ppermute | solution.py:359
  33.4 2.3 %collective-permute-start.12 = (bf16[64,384]{1,0:T(8,128)(2,1)S(1)}, bf16[64,384]{1,0:T(8,128)(2,1)S(1)}, u32[]{:S(2)}, u32[]{:S(2)}) collective-permute-start(bf16[64,384]{1,0:T(8,128)(2,1)S(1)} %get-tuple-element.32.piece_ref), channel_id=1, source_target_pairs={{0,16},{8,24},{16,0},{24,8},{1,17},{9,25},{17,1},{25,9},{2,18},{10... | collective-permute-start | bytes 147464 | tf_op jit(solution)/shard_map/ppermute | solution.py:359
  36.7 1.6 %collective-permute-done.12.fake_ref = bf16[64,384]{1,0:T(8,128)(2,1)S(1)} collective-permute-done((bf16[64,384]{1,0:T(8,128)(2,1)S(1)}, bf16[64,384]{1,0:T(8,128)(2,1)S(1)}, u32[]{:S(2)}, u32[]{:S(2)}) %collective-permute-start.12) | collective-permute-done | bytes 49184 | tf_op jit(solution)/shard_map/ppermute | solution.py:359
  38.2 1.3 %collective-permute-done.11.adversarial_ref = bf16[64,384]{1,0:T(8,128)(2,1)S(1)} collective-permute-done((bf16[64,384]{1,0:T(8,128)(2,1)S(1)}, bf16[64,384]{1,0:T(8,128)(2,1)S(1)}, u32[]{:S(2)}, u32[]{:S(2)}) %collective-permute-start.11) | collective-permute-done | bytes 49184 | tf_op jit(solution)/shard_map/ppermute | solution.py:359
  41.1 1.3 %collective-permute-start.13 = (bf16[72,384]{1,0:T(8,128)(2,1)S(1)}, bf16[72,384]{1,0:T(8,128)(2,1)S(1)}, u32[]{:S(2)}, u32[]{:S(2)}) collective-permute-start(bf16[72,384]{1,0:T(8,128)(2,1)S(1)} %get-tuple-element.42), channel_id=1, source_target_pairs={{0,1},{1,0},{2,3},{3,2},{4,5},{5,4},{6,7},{7,6},{8,9},{9,8},{10,11... | collective-permute-start | bytes 165896 | tf_op jit(solution)/shard_map/ppermute | solution.py:359
  43.1 1.7 %collective-permute-done.17 = bf16[72,384]{1,0:T(8,128)(2,1)S(1)} collective-permute-done((bf16[72,384]{1,0:T(8,128)(2,1)S(1)}, bf16[72,384]{1,0:T(8,128)(2,1)S(1)}, u32[]{:S(2)}, u32[]{:S(2)}) %collective-permute-start.17) | collective-permute-done | bytes 55328 | tf_op jit(solution)/shard_map/ppermute | solution.py:359
  44.8 1.5 %collective-permute-start.18 = (bf16[72,384]{1,0:T(8,128)(2,1)S(1)}, bf16[72,384]{1,0:T(8,128)(2,1)S(1)}, u32[]{:S(2)}, u32[]{:S(2)}) collective-permute-start(bf16[72,384]{1,0:T(8,128)(2,1)S(1)} %fusion.9), channel_id=1, source_target_pairs={{0,2},{1,3},{2,0},{3,1},{4,6},{5,7},{6,4},{7,5},{8,10},{9,11},{10,... | collective-permute-start | bytes 165896 | tf_op jit(solution)/shard_map/ppermute | solution.py:359
  47.0 2.0 %collective-permute-done.18 = bf16[72,384]{1,0:T(8,128)(2,1)S(1)} collective-permute-done((bf16[72,384]{1,0:T(8,128)(2,1)S(1)}, bf16[72,384]{1,0:T(8,128)(2,1)S(1)}, u32[]{:S(2)}, u32[]{:S(2)}) %collective-permute-start.18) | collective-permute-done | bytes 55328 | tf_op jit(solution)/shard_map/ppermute | solution.py:359
  49.1 1.6 %collective-permute-start.19 = (bf16[72,384]{1,0:T(8,128)(2,1)S(1)}, bf16[72,384]{1,0:T(8,128)(2,1)S(1)}, u32[]{:S(2)}, u32[]{:S(2)}) collective-permute-start(bf16[72,384]{1,0:T(8,128)(2,1)S(1)} %fusion.13), channel_id=1, source_target_pairs={{0,4},{1,5},{2,6},{3,7},{4,0},{5,1},{6,2},{7,3},{8,12},{9,13},{10,... | collective-permute-start | bytes 165896 | tf_op jit(solution)/shard_map/ppermute | solution.py:359
  51.2 1.4 %collective-permute-start.15 = (bf16[72,384]{1,0:T(8,128)(2,1)S(1)}, bf16[72,384]{1,0:T(8,128)(2,1)S(1)}, u32[]{:S(2)}, u32[]{:S(2)}) collective-permute-start(bf16[72,384]{1,0:T(8,128)(2,1)S(1)} %fusion.12), channel_id=1, source_target_pairs={{0,4},{1,5},{2,6},{3,7},{4,0},{5,1},{6,2},{7,3},{8,12},{9,13},{10,... | collective-permute-start | bytes 165896 | tf_op jit(solution)/shard_map/ppermute | solution.py:359
  52.6 1.6 %collective-permute-done.19 = bf16[72,384]{1,0:T(8,128)(2,1)S(1)} collective-permute-done((bf16[72,384]{1,0:T(8,128)(2,1)S(1)}, bf16[72,384]{1,0:T(8,128)(2,1)S(1)}, u32[]{:S(2)}, u32[]{:S(2)}) %collective-permute-start.19) | collective-permute-done | bytes 55328 | tf_op jit(solution)/shard_map/ppermute | solution.py:359
  55.1 1.8 %collective-permute-done.15 = bf16[72,384]{1,0:T(8,128)(2,1)S(1)} collective-permute-done((bf16[72,384]{1,0:T(8,128)(2,1)S(1)}, bf16[72,384]{1,0:T(8,128)(2,1)S(1)}, u32[]{:S(2)}, u32[]{:S(2)}) %collective-permute-start.15) | collective-permute-done | bytes 55328 | tf_op jit(solution)/shard_map/ppermute | solution.py:359
  57.3 1.3 %gradient.3.rest_1_ = f32[1,384,1536]{2,1,0:T(8,128)} custom-call(bf16[144,384]{1,0:T(8,128)(2,1)S(1)} %get-tuple-element.24.own_ref, bf16[72,384]{1,0:T(8,128)(2,1)S(1)} %add_convert_fusion.rest_0_, bf16[72,384]{1,0:T(8,128)(2,1)S(1)} %add_convert_fusion.1.rest_1_), custom_call_target="tpu_custom_call" | custom-call | flops 169869312 | bytes 1179648 | tf_op jit(solution)/shard_map/gradient/pallas_call | solution.py:340
  58.6 1.1 %gradient.4.rest_1_ = f32[1,384,1536]{2,1,0:T(8,128)} custom-call(bf16[144,384]{1,0:T(8,128)(2,1)S(1)} %get-tuple-element.24.own_ref, bf16[72,384]{1,0:T(8,128)(2,1)S(1)} %collective-permute-done.20.rest_0_, f32[1,384,1536]{2,1,0:T(8,128)} %gradient.3.rest_1_), custom_call_target="tpu_custom_call", output_to_operand_aliasing={{}: (2, {})} | custom-call | flops 84934656 | bytes 589824 | tf_op jit(solution)/shard_map/gradient/pallas_call | solution.py:340
  59.8 1.4 %collective-permute-done.16.rest_0_ = bf16[72,384]{1,0:T(8,128)(2,1)S(1)} collective-permute-done((bf16[72,384]{1,0:T(8,128)(2,1)S(1)}, bf16[72,384]{1,0:T(8,128)(2,1)S(1)}, u32[]{:S(2)}, u32[]{:S(2)}) %collective-permute-start.16) | collective-permute-done | bytes 55328 | tf_op jit(solution)/shard_map/ppermute | solution.py:359
  61.2 1.1 %gradient.5 = f32[1,384,1536]{2,1,0:T(8,128)} custom-call(bf16[144,384]{1,0:T(8,128)(2,1)S(1)} %get-tuple-element.24.own_ref, bf16[72,384]{1,0:T(8,128)(2,1)S(1)} %collective-permute-done.16.rest_0_, f32[1,384,1536]{2,1,0:T(8,128)} %gradient.4.rest_1_), custom_call_target="tpu_custom_call", output_to_operand_aliasing={{}: (2, {})} | custom-call | flops 84934656 | bytes 589824 | tf_op jit(solution)/shard_map/gradient/pallas_call | solution.py:340
  (52 shorter events, 9.1 us)
Async XLA Ops:
  0.6 22.3 %copy-start.3 = (f32[1,3072]{1,0:T(1,128)S(1)}, f32[1,3072]{1,0:T(1,128)}, u32[]{:S(2)}) copy-start(f32[1,3072]{1,0:T(1,128)} %param.12) | copy-start | bytes 36868
  3.4 20.5 %copy-start.4 = (f32[384]{0:T(512)S(1)}, f32[384]{0:T(512)}, u32[]{:S(2)}) copy-start(f32[384]{0:T(512)} %param.10) | copy-start | bytes 4612
  3.5 22.9 %copy-start = (bf16[1,1536,64]{1,2,0:T(8,128)(2,1)S(1)}, bf16[1,1536,64]{1,2,0:T(8,128)(2,1)}, u32[]{:S(2)}) copy-start(bf16[1,1536,64]{1,2,0:T(8,128)(2,1)} %param.15) | copy-start | bytes 589828
  3.5 22.9 %copy-start.1 = (bf16[384,64]{0,1:T(8,128)(2,1)S(1)}, bf16[384,64]{0,1:T(8,128)(2,1)}, u32[]{:S(2)}) copy-start(bf16[384,64]{0,1:T(8,128)(2,1)} %param.9) | copy-start | bytes 147460
  3.5 22.9 %copy-start.2 = (bf16[384,64]{0,1:T(8,128)(2,1)S(1)}, bf16[384,64]{0,1:T(8,128)(2,1)}, u32[]{:S(2)}) copy-start(bf16[384,64]{0,1:T(8,128)(2,1)} %param.8) | copy-start | bytes 147460
  3.5 5.2 %collective-permute-start = (bf16[72,384]{1,0:T(8,128)(2,1)S(1)}, bf16[72,384]{1,0:T(8,128)(2,1)S(1)}, u32[]{:S(2)}, u32[]{:S(2)}) collective-permute-start(bf16[72,384]{1,0:T(8,128)(2,1)S(1)} %get-tuple-element.26), channel_id=1, source_target_pairs={{0,1},{1,0},{2,3},{3,2},{4,5},{5,4},{6,7},{7,6},{8,9},{9,8},{10,11... | collective-permute-start | bytes 165896 | tf_op jit(solution)/shard_map/ppermute | solution.py:359
  6.5 4.8 %collective-permute-start.3 = (bf16[72,384]{1,0:T(8,128)(2,1)S(1)}, bf16[72,384]{1,0:T(8,128)(2,1)S(1)}, u32[]{:S(2)}, u32[]{:S(2)}) collective-permute-start(bf16[72,384]{1,0:T(8,128)(2,1)S(1)} %get-tuple-element.28), channel_id=1, source_target_pairs={{0,1},{1,0},{2,3},{3,2},{4,5},{5,4},{6,7},{7,6},{8,9},{9,8},{10,11... | collective-permute-start | bytes 165896 | tf_op jit(solution)/shard_map/ppermute | solution.py:359
  8.7 4.8 %collective-permute-start.1 = (bf16[72,384]{1,0:T(8,128)(2,1)S(1)}, bf16[72,384]{1,0:T(8,128)(2,1)S(1)}, u32[]{:S(2)}, u32[]{:S(2)}) collective-permute-start(bf16[72,384]{1,0:T(8,128)(2,1)S(1)} %fusion.6), channel_id=1, source_target_pairs={{0,2},{1,3},{2,0},{3,1},{4,6},{5,7},{6,4},{7,5},{8,10},{9,11},{10,... | collective-permute-start | bytes 165896 | tf_op jit(solution)/shard_map/ppermute | solution.py:359
  11.3 5.6 %collective-permute-start.4 = (bf16[72,384]{1,0:T(8,128)(2,1)S(1)}, bf16[72,384]{1,0:T(8,128)(2,1)S(1)}, u32[]{:S(2)}, u32[]{:S(2)}) collective-permute-start(bf16[72,384]{1,0:T(8,128)(2,1)S(1)} %fusion.7), channel_id=1, source_target_pairs={{0,2},{1,3},{2,0},{3,1},{4,6},{5,7},{6,4},{7,5},{8,10},{9,11},{10,... | collective-permute-start | bytes 165896 | tf_op jit(solution)/shard_map/ppermute | solution.py:359
  13.5 5.6 %collective-permute-start.2 = (bf16[72,384]{1,0:T(8,128)(2,1)S(1)}, bf16[72,384]{1,0:T(8,128)(2,1)S(1)}, u32[]{:S(2)}, u32[]{:S(2)}) collective-permute-start(bf16[72,384]{1,0:T(8,128)(2,1)S(1)} %fusion.10), channel_id=1, source_target_pairs={{0,4},{1,5},{2,6},{3,7},{4,0},{5,1},{6,2},{7,3},{8,12},{9,13},{10,... | collective-permute-start | bytes 165896 | tf_op jit(solution)/shard_map/ppermute | solution.py:359
  17.0 5.1 %collective-permute-start.5 = (bf16[72,384]{1,0:T(8,128)(2,1)S(1)}, bf16[72,384]{1,0:T(8,128)(2,1)S(1)}, u32[]{:S(2)}, u32[]{:S(2)}) collective-permute-start(bf16[72,384]{1,0:T(8,128)(2,1)S(1)} %fusion.11), channel_id=1, source_target_pairs={{0,4},{1,5},{2,6},{3,7},{4,0},{5,1},{6,2},{7,3},{8,12},{9,13},{10,... | collective-permute-start | bytes 165896 | tf_op jit(solution)/shard_map/ppermute | solution.py:359
  19.2 4.8 %collective-permute-start.6 = (bf16[72,384]{1,0:T(8,128)(2,1)S(1)}, bf16[72,384]{1,0:T(8,128)(2,1)S(1)}, u32[]{:S(2)}, u32[]{:S(2)}) collective-permute-start(bf16[72,384]{1,0:T(8,128)(2,1)S(1)} %add_convert_fusion.3.rest_0_), channel_id=1, source_target_pairs={{0,1},{1,0},{2,3},{3,2},{4,5},{5,4},{6,7},{7,6},{8,9},{9,8},{10,11... | collective-permute-start | bytes 165896 | tf_op jit(solution)/shard_map/ppermute | solution.py:359
  22.1 4.2 %collective-permute-start.7 = (bf16[72,384]{1,0:T(8,128)(2,1)S(1)}, bf16[72,384]{1,0:T(8,128)(2,1)S(1)}, u32[]{:S(2)}, u32[]{:S(2)}) collective-permute-start(bf16[72,384]{1,0:T(8,128)(2,1)S(1)} %add_convert_fusion.2.rest_1_), channel_id=1, source_target_pairs={{0,1},{1,0},{2,3},{3,2},{4,5},{5,4},{6,7},{7,6},{8,9},{9,8},{10,11... | collective-permute-start | bytes 165896 | tf_op jit(solution)/shard_map/ppermute | solution.py:359
  27.9 1.3 %collective-permute-start.8 = (bf16[64,384]{1,0:T(8,128)(2,1)S(1)}, bf16[64,384]{1,0:T(8,128)(2,1)S(1)}, u32[]{:S(2)}, u32[]{:S(2)}) collective-permute-start(bf16[64,384]{1,0:T(8,128)(2,1)S(1)} %get-tuple-element.29), channel_id=1, source_target_pairs={{0,8},{8,0},{16,24},{24,16},{1,9},{9,1},{17,25},{25,17},{2,10},{10... | collective-permute-start | bytes 147464 | tf_op jit(solution)/shard_map/ppermute | solution.py:359
  29.2 4.2 %collective-permute-start.9 = (bf16[64,384]{1,0:T(8,128)(2,1)S(1)}, bf16[64,384]{1,0:T(8,128)(2,1)S(1)}, u32[]{:S(2)}, u32[]{:S(2)}) collective-permute-start(bf16[64,384]{1,0:T(8,128)(2,1)S(1)} %broadcast_select_fusion.1.near_ref), channel_id=1, source_target_pairs={{0,16},{8,24},{16,0},{24,8},{1,17},{9,25},{17,1},{25,9},{2,18},{10... | collective-permute-start | bytes 147464 | tf_op jit(solution)/shard_map/ppermute | solution.py:359
  33.4 4.8 %collective-permute-start.12 = (bf16[64,384]{1,0:T(8,128)(2,1)S(1)}, bf16[64,384]{1,0:T(8,128)(2,1)S(1)}, u32[]{:S(2)}, u32[]{:S(2)}) collective-permute-start(bf16[64,384]{1,0:T(8,128)(2,1)S(1)} %get-tuple-element.32.piece_ref), channel_id=1, source_target_pairs={{0,16},{8,24},{16,0},{24,8},{1,17},{9,25},{17,1},{25,9},{2,18},{10... | collective-permute-start | bytes 147464 | tf_op jit(solution)/shard_map/ppermute | solution.py:359
  35.7 3.8 %collective-permute-start.11 = (bf16[64,384]{1,0:T(8,128)(2,1)S(1)}, bf16[64,384]{1,0:T(8,128)(2,1)S(1)}, u32[]{:S(2)}, u32[]{:S(2)}) collective-permute-start(bf16[64,384]{1,0:T(8,128)(2,1)S(1)} %get-tuple-element.32.piece_ref), channel_id=1, source_target_pairs={{0,24},{8,16},{16,8},{24,0},{1,25},{9,17},{17,9},{25,1},{2,26},{10... | collective-permute-start | bytes 147464 | tf_op jit(solution)/shard_map/ppermute | solution.py:359
  36.0 3.5 %collective-permute-start.10 = (bf16[64,384]{1,0:T(8,128)(2,1)S(1)}, bf16[64,384]{1,0:T(8,128)(2,1)S(1)}, u32[]{:S(2)}, u32[]{:S(2)}) collective-permute-start(bf16[64,384]{1,0:T(8,128)(2,1)S(1)} %get-tuple-element.32.piece_ref), channel_id=1, source_target_pairs={{0,8},{8,0},{16,24},{24,16},{1,9},{9,1},{17,25},{25,17},{2,10},{10... | collective-permute-start | bytes 147464 | tf_op jit(solution)/shard_map/ppermute | solution.py:359
  40.3 4.5 %collective-permute-start.17 = (bf16[72,384]{1,0:T(8,128)(2,1)S(1)}, bf16[72,384]{1,0:T(8,128)(2,1)S(1)}, u32[]{:S(2)}, u32[]{:S(2)}) collective-permute-start(bf16[72,384]{1,0:T(8,128)(2,1)S(1)} %get-tuple-element.44), channel_id=1, source_target_pairs={{0,1},{1,0},{2,3},{3,2},{4,5},{5,4},{6,7},{7,6},{8,9},{9,8},{10,11... | collective-permute-start | bytes 165896 | tf_op jit(solution)/shard_map/ppermute | solution.py:359
  41.1 5.3 %collective-permute-start.13 = (bf16[72,384]{1,0:T(8,128)(2,1)S(1)}, bf16[72,384]{1,0:T(8,128)(2,1)S(1)}, u32[]{:S(2)}, u32[]{:S(2)}) collective-permute-start(bf16[72,384]{1,0:T(8,128)(2,1)S(1)} %get-tuple-element.42), channel_id=1, source_target_pairs={{0,1},{1,0},{2,3},{3,2},{4,5},{5,4},{6,7},{7,6},{8,9},{9,8},{10,11... | collective-permute-start | bytes 165896 | tf_op jit(solution)/shard_map/ppermute | solution.py:359
  44.8 4.2 %collective-permute-start.18 = (bf16[72,384]{1,0:T(8,128)(2,1)S(1)}, bf16[72,384]{1,0:T(8,128)(2,1)S(1)}, u32[]{:S(2)}, u32[]{:S(2)}) collective-permute-start(bf16[72,384]{1,0:T(8,128)(2,1)S(1)} %fusion.9), channel_id=1, source_target_pairs={{0,2},{1,3},{2,0},{3,1},{4,6},{5,7},{6,4},{7,5},{8,10},{9,11},{10,... | collective-permute-start | bytes 165896 | tf_op jit(solution)/shard_map/ppermute | solution.py:359
  46.4 4.8 %collective-permute-start.14 = (bf16[72,384]{1,0:T(8,128)(2,1)S(1)}, bf16[72,384]{1,0:T(8,128)(2,1)S(1)}, u32[]{:S(2)}, u32[]{:S(2)}) collective-permute-start(bf16[72,384]{1,0:T(8,128)(2,1)S(1)} %fusion.8), channel_id=1, source_target_pairs={{0,2},{1,3},{2,0},{3,1},{4,6},{5,7},{6,4},{7,5},{8,10},{9,11},{10,... | collective-permute-start | bytes 165896 | tf_op jit(solution)/shard_map/ppermute | solution.py:359
  49.1 5.1 %collective-permute-start.19 = (bf16[72,384]{1,0:T(8,128)(2,1)S(1)}, bf16[72,384]{1,0:T(8,128)(2,1)S(1)}, u32[]{:S(2)}, u32[]{:S(2)}) collective-permute-start(bf16[72,384]{1,0:T(8,128)(2,1)S(1)} %fusion.13), channel_id=1, source_target_pairs={{0,4},{1,5},{2,6},{3,7},{4,0},{5,1},{6,2},{7,3},{8,12},{9,13},{10,... | collective-permute-start | bytes 165896 | tf_op jit(solution)/shard_map/ppermute | solution.py:359
  51.2 5.7 %collective-permute-start.15 = (bf16[72,384]{1,0:T(8,128)(2,1)S(1)}, bf16[72,384]{1,0:T(8,128)(2,1)S(1)}, u32[]{:S(2)}, u32[]{:S(2)}) collective-permute-start(bf16[72,384]{1,0:T(8,128)(2,1)S(1)} %fusion.12), channel_id=1, source_target_pairs={{0,4},{1,5},{2,6},{3,7},{4,0},{5,1},{6,2},{7,3},{8,12},{9,13},{10,... | collective-permute-start | bytes 165896 | tf_op jit(solution)/shard_map/ppermute | solution.py:359
  54.3 4.4 %collective-permute-start.20 = (bf16[72,384]{1,0:T(8,128)(2,1)S(1)}, bf16[72,384]{1,0:T(8,128)(2,1)S(1)}, u32[]{:S(2)}, u32[]{:S(2)}) collective-permute-start(bf16[72,384]{1,0:T(8,128)(2,1)S(1)} %add_convert_fusion.rest_0_), channel_id=1, source_target_pairs={{0,1},{1,0},{2,3},{3,2},{4,5},{5,4},{6,7},{7,6},{8,9},{9,8},{10,11... | collective-permute-start | bytes 165896 | tf_op jit(solution)/shard_map/ppermute | solution.py:359
  57.0 4.2 %collective-permute-start.16 = (bf16[72,384]{1,0:T(8,128)(2,1)S(1)}, bf16[72,384]{1,0:T(8,128)(2,1)S(1)}, u32[]{:S(2)}, u32[]{:S(2)}) collective-permute-start(bf16[72,384]{1,0:T(8,128)(2,1)S(1)} %add_convert_fusion.1.rest_1_), channel_id=1, source_target_pairs={{0,1},{1,0},{2,3},{3,2},{4,5},{5,4},{6,7},{7,6},{8,9},{9,8},{10,11... | collective-permute-start | bytes 165896 | tf_op jit(solution)/shard_map/ppermute | solution.py:359

commit v3 on v2

--- a/solution.py
+++ b/solution.py
@@ -12,7 +12,7 @@
 f32 = jnp.float32
 bf16 = jnp.bfloat16
 extra = 8
-pieces = 2
+chains = 2
 part_limit = 54528
 curve = math.sqrt(2.0 / math.pi)
 bend = 0.044715
@@ -29,20 +29,13 @@
     )
 
 
-def gelu_parts(hidden):
+def gelu_gate(hidden):
     square = hidden * hidden
-    bent = jnp.tanh(curve * hidden * (1.0 + bend * square))
-    return square, bent
-
-
-def gelu_value(hidden, bent):
-    return 0.5 * hidden * (1.0 + bent)
-
-
-def gelu_slope(hidden, square, bent):
-    return 0.5 * (1.0 + bent) + (0.5 * curve) * hidden * (1.0 - bent * bent) * (
-        1.0 + (3.0 * bend) * square
-    )
+    return 0.5 + 0.5 * jnp.tanh(hidden * (curve + (curve * bend) * square)), square
+
+
+def gelu_slope(hidden, square, gate):
+    return gate + (gate - gate * gate) * (hidden * (2.0 * curve + (6.0 * curve * bend) * square))
 
 
 def level_rows(level):
@@ -69,27 +62,26 @@
     return lax.rsqrt(square * (1.0 / width) + 1e-06), seen
 
 
-def columns_of(at, half, upper):
-    tile = half // pieces
-    base = upper * half if at < pieces else (1 - upper) * half
-    return pl.ds(pl.multiple_of(base + (at % pieces) * tile, tile), tile)
+def columns_of(at, tile):
+    chain = at % chains
+    kept = (lax.axis_index("fsdp") >> chain) & 1
+    base = 2 * tile * chain + tile * (kept if at < chains else 1 - kept)
+    return pl.ds(pl.multiple_of(base, tile), tile)
 
 
 def part_kernel(embed_ref, vectors_ref, block_ref, *rest):
     *outs, embed, buffer, sems = rest
     place = lax.axis_index("fsdp")
-    upper = place & 1
     depth, cols = buffer.shape
-    half = cols // 2
-    tile = half // pieces
+    tile = cols // (2 * chains)
     own = slice(None)
     if embed_ref.shape[1] != depth:
         own = pl.ds(pl.multiple_of(place * depth, depth), depth)
-    small = pltpu.make_async_copy(embed_ref.at[:, own], embed, sems.at[2 * pieces])
-    order = [*range(pieces, 2 * pieces), *range(pieces)]
+    small = pltpu.make_async_copy(embed_ref.at[:, own], embed, sems.at[2 * chains])
+    order = [*range(chains, 2 * chains), *range(chains)]
     large = [
         pltpu.make_async_copy(
-            block_ref.at[0, :, columns_of(at, half, upper)],
+            block_ref.at[0, :, columns_of(at, tile)],
             buffer.at[:, at * tile : (at + 1) * tile],
             sems.at[at],
         )
@@ -105,31 +97,39 @@
     gained = jnp.concatenate([embed[...].astype(f32) * gain, stamped], axis=0)
     rows = gained.shape[0]
     both = jnp.concatenate([gained, gained - gained.astype(bf16).astype(f32)], axis=0).astype(bf16)
-    outs[2 * pieces][...] = both
+    outs[2 * chains][...] = both
     for at, copy in zip(order, large):
         copy.wait()
         part = mm(both, buffer[:, at * tile : (at + 1) * tile], 1, 0)
         outs[at][...] = (part[:rows] + part[rows:]).astype(outs[at].dtype)
 
 
-def forward(wide, gram_ref, proj_refs, readout_ref, width, slope_ref=None):
-    upper = lax.axis_index("fsdp") & 1
-    half = proj_refs[0].shape[1] * pieces
-    tile = half // pieces
-    scale, seen = norm_scale(wide, gram_ref[...], width)
-    wide16 = wide.astype(bf16)
-    total = jnp.zeros((readout_ref.shape[0], wide.shape[1]), f32)
-    for at, proj_ref in enumerate(proj_refs):
+def network(wide16, scale, proj_refs, first_piece, readout_ref, slope_ref=None):
+    tile = proj_refs[0].shape[1]
+    total = jnp.zeros((readout_ref.shape[0], wide16.shape[1]), f32)
+    for at, proj_ref in enumerate(proj_refs, first_piece):
         hidden = scale * mm(proj_ref[...], wide16, 0, 0)
-        square, bent = gelu_parts(hidden)
-        activated = gelu_value(hidden, bent).astype(bf16)
-        total = total + mm(readout_ref[:, columns_of(at, half, upper)], activated, 1, 0)
+        gate, square = gelu_gate(hidden)
+        activated = (hidden * gate).astype(bf16)
+        total = total + mm(readout_ref[:, columns_of(at, tile)], activated, 1, 0)
         if slope_ref is not None:
-            slope_ref[at * tile : (at + 1) * tile, :] = gelu_slope(hidden, square, bent)
-    return total.astype(bf16), scale, seen
-
-
-def first_kernel(latent_ref, noise_ref, level_ref, gram_ref, *rest, width):
+            slope_ref[at * tile : (at + 1) * tile, :] = gelu_slope(hidden, square, gate)
+    return total
+
+
+def early_kernel(latent_ref, gram_ref, *rest, width):
+    *proj_refs, readout_ref, total_ref = rest
+    channels, tokens = latent_ref.shape
+
+    @pl.when(lax.axis_index("role") == 0)
+    def _():
+        wide = widen(latent_ref[...], jnp.ones((1, tokens), f32))
+        scale, unused = norm_scale(wide, gram_ref[...], width)
+        total_ref[:channels, :] = network(wide.astype(bf16), scale, proj_refs, 0, readout_ref)
+        total_ref[channels:, :] = jnp.broadcast_to(scale, (extra, tokens))
+
+
+def late_kernel(latent_ref, noise_ref, level_ref, gram_ref, total_ref, *rest):
     *proj_refs, readout_ref, out_ref, mix_ref, gram_out_ref = rest
     channels, tokens = latent_ref.shape
     level = level_ref[...]
@@ -139,8 +139,10 @@
 
     @pl.when(lax.axis_index("role") == 0)
     def _():
-        wide = widen(latent_ref[...], jnp.ones((1, tokens), f32))
-        out_ref[...], unused, unused = forward(wide, gram_ref, proj_refs, readout_ref, width)
+        wide16 = widen(latent_ref[...], jnp.ones((1, tokens), f32)).astype(bf16)
+        scale = total_ref[channels : channels + 1, :]
+        total = network(wide16, scale, proj_refs, chains, readout_ref)
+        out_ref[...] = (total_ref[:channels, :] + total).astype(bf16)
 
 
 def in_parts(scale, wide):
@@ -159,19 +161,18 @@
         wide16 = wide.astype(bf16)
         for at, proj_ref in enumerate(proj_refs):
             hidden = scale * mm(proj_ref[...], wide16, 0, 0)
-            square, bent = gelu_parts(hidden)
-            slope_ref[at * tile : (at + 1) * tile, :] = gelu_slope(hidden, square, bent)
+            gate, square = gelu_gate(hidden)
+            slope_ref[at * tile : (at + 1) * tile, :] = gelu_slope(hidden, square, gate)
         scaled_ref[...] = in_parts(scale, wide)
 
 
-def second_kernel(near_ref, far_ref, mix_ref, gram_ref, *rest, width):
-    proj_refs = rest[: 2 * pieces]
-    readout_ref, columns_ref, generated_ref, piece_ref, flat_ref, slope_ref, scaled_ref = rest[2 * pieces :]
-    role, upper = lax.axis_index("role"), lax.axis_index("fsdp") & 1
-    channels, tokens = near_ref.shape
-    half = proj_refs[0].shape[1] * pieces
-    tile = half // pieces
-    generated = jnp.where(role < 2, near_ref[...].astype(f32), far_ref[...].astype(f32))
+def second_kernel(even_ref, odd_ref, mix_ref, gram_ref, *rest, width):
+    proj_refs = rest[: 2 * chains]
+    readout_ref, columns_ref, generated_ref, piece_ref, flat_ref, slope_ref, scaled_ref = rest[2 * chains :]
+    role = lax.axis_index("role")
+    channels, tokens = even_ref.shape
+    tile = proj_refs[0].shape[1]
+    generated = jnp.where((role & 1) == 0, even_ref[...].astype(f32), odd_ref[...].astype(f32))
     generated_ref[...] = generated.astype(bf16)
 
     @pl.when(role > 0)
@@ -179,7 +180,8 @@
         level = mix_ref[channels : channels + 1, :]
         noised = (1.0 - level) * generated + mix_ref[:channels, :]
         wide = widen(noised.astype(bf16), level)
-        scores, scale, seen = forward(wide, gram_ref, proj_refs, readout_ref, width, slope_ref)
+        scale, seen = norm_scale(wide, gram_ref[...], width)
+        scores = network(wide.astype(bf16), scale, proj_refs, 0, readout_ref, slope_ref).astype(bf16)
         piece_ref[...] = scores
         logit = jnp.sum(scores.astype(f32), axis=0, keepdims=True)
         flat_ref[...] = 1.0 / (1.0 + jnp.exp(-logit))
@@ -197,7 +199,7 @@
             )
             back_rows = jnp.zeros(wide.shape, f32)
             for at, proj_ref in enumerate(proj_refs):
-                back = mm(columns_ref[columns_of(at, half, upper), :], cot, 1, 0)
+                back = mm(columns_ref[columns_of(at, tile), :], cot, 1, 0)
                 hcot = (back * slope_ref[at * tile : (at + 1) * tile, :]).astype(bf16)
                 back_rows = back_rows + mm(proj_ref[...], hcot, 1, 0)
             inner = scale * jnp.sum(back_rows * wide, axis=0, keepdims=True)
@@ -206,16 +208,14 @@
 
 
 def pull_back(cot, tail, out_refs, first_piece):
-    upper = lax.axis_index("fsdp") & 1
     first = lax.axis_index("role") == 0
     rows, tile = out_refs[0].shape
-    half = tile * pieces
     columns_ref = tail[4]
 
     def with_slopes(slope_ref, scaled_ref):
         scaled = scaled_ref[...]
         for at, out_ref in enumerate(out_refs, first_piece):
-            back = mm(columns_ref[columns_of(at, half, upper), :], cot, 1, 0)
+            back = mm(columns_ref[columns_of(at, tile), :], cot, 1, 0)
             hcot = (back * slope_ref[at * tile : (at + 1) * tile, :]).astype(bf16)
             part = mm(scaled, hcot, 1, 1)
             out_ref[...] = (part[:rows] + part[rows:]).astype(out_ref.dtype)
@@ -255,7 +255,7 @@
     ).astype(bf16)
     cot = jnp.concatenate([left, right], axis=0)
     cot_ref[...] = cot
-    pull_back(cot, tail, out_refs, pieces)
+    pull_back(cot, tail, out_refs, chains)
 
 
 def keep_kernel(cot_ref, *rest):
@@ -265,7 +265,6 @@
 def grad_kernel(own_ref, *rest, factor, first_piece, count):
     total_refs = rest[:count]
     *unused, out_ref, buffer, sems = rest[count:]
-    upper = lax.axis_index("fsdp") & 1
     tile = buffer.shape[1] // count
     own = own_ref[...]
     copies = []
@@ -274,7 +273,7 @@
         total = total_ref[...].astype(f32)
         part = mm(own, jnp.concatenate([total, total], axis=0).astype(bf16), 0, 0)
         buffer[:, here] = part * factor
-        cols = columns_of(first_piece + at, tile * pieces, upper)
+        cols = columns_of(first_piece + at, tile)
         copy = pltpu.make_async_copy(buffer.at[:, here], out_ref.at[0, :, cols], sems.at[at])
         copy.start()
         copies.append(copy)
@@ -300,13 +299,13 @@
 def part_of(embed_w, vectors, block_weight):
     depth, cols = block_weight.shape[1:]
     channels = embed_w.shape[0]
-    rows, half = channels + extra, cols // 2
+    rows, tile = channels + extra, cols // (2 * chains)
     if depth % 128 != 0:
         embed_w, vectors = (
             lax.dynamic_slice_in_dim(value, lax.axis_index("fsdp") * depth, depth, 1)
             for value in (embed_w, vectors)
         )
-    shapes = [jax.ShapeDtypeStruct((rows, half // pieces), dtype) for dtype in (f32, bf16) for at in range(pieces)]
+    shapes = [jax.ShapeDtypeStruct((rows, tile), dtype) for dtype in (f32, bf16) for at in range(chains)]
     shapes.append(jax.ShapeDtypeStruct((2 * rows, depth), bf16))
     vmem = pl.BlockSpec(memory_space=pltpu.VMEM)
     hbm = pl.BlockSpec(memory_space=pltpu.HBM)
@@ -318,18 +317,18 @@
         scratch_shapes=[
             pltpu.VMEM((channels, depth), bf16),
             pltpu.VMEM((depth, cols), bf16),
-            pltpu.SemaphoreType.DMA((2 * pieces + 1,)),
+            pltpu.SemaphoreType.DMA((2 * chains + 1,)),
         ],
         compiler_params=pltpu.CompilerParams(vmem_limit_bytes=part_limit * 1024),
         cost_estimate=pl.CostEstimate(
-            flops=8 * rows * depth * half, bytes_accessed=4 * depth * half, transcendentals=0
+            flops=4 * rows * depth * cols, bytes_accessed=2 * depth * cols, transcendentals=0
         ),
         name="part",
     )(embed_w, vectors, block_weight)
 
 
 def gradient(own, totals, first_piece, factor, cols, buffer=None):
-    depth, tile, count = own.shape[1], cols // (2 * pieces), len(totals)
+    depth, tile, count = own.shape[1], cols // (2 * chains), len(totals)
     vmem = pl.BlockSpec(memory_space=pltpu.VMEM)
     hbm = pl.BlockSpec(memory_space=pltpu.HBM)
     specs = [vmem] * (1 + count)
@@ -354,19 +353,21 @@
     )(*inputs)
 
 
-def swap(values, axis, n, bit):
-    pairs = [(i, i ^ bit) for i in range(n)]
-    return [lax.ppermute(value, axis, pairs) for value in values]
-
-
-def add_along(mine, received, n):
-    mine = [value + part.astype(f32) for value, part in zip(mine, received)]
-    bit = 2
-    while bit < n:
-        parts = swap([value.astype(bf16) for value in mine], "fsdp", n, bit)
-        mine = [value + part.astype(f32) for value, part in zip(mine, parts)]
-        bit *= 2
-    return [value.astype(bf16) for value in mine]
+def swap(value, axis, n, bit):
+    return lax.ppermute(value, axis, [(i, i ^ bit) for i in range(n)])
+
+
+def add_all(kept, sent, n):
+    bits = [1 << at for at in range(n.bit_length() - 1)]
+    orders = [[1, *reversed(bits[1:])], [2, 1, *bits[2:]]]
+    mine = []
+    for value, part, order in zip(kept, sent, orders):
+        for step, bit in enumerate(order):
+            outgoing = value.astype(bf16) if step else part
+            value = value + swap(outgoing, "fsdp", n, bit).astype(f32)
+        mine.append(value.astype(bf16))
+    others = [swap(value, "fsdp", n, order[0]) for value, order in zip(mine, orders)]
+    return mine, others
 
 
 def shards(
@@ -387,15 +388,14 @@
     channels, width = embed_w.shape
     tokens = source_noise.shape[0]
     rows = channels + extra
-    half = cols // 2
+    tile = cols // (2 * chains)
     shape = jax.ShapeDtypeStruct
     roles = lax.axis_size("role")
 
     vectors = jnp.concatenate([time_vector, norm_gain], axis=0)
     *parts, own_rows = part_of(embed_w, vectors, block_weight)
-    received = swap(parts[pieces:], "fsdp", n, 1)
-    mine = add_along(parts[:pieces], received, n)
-    proj = mine + swap(mine, "fsdp", n, 1)
+    mine, others = add_all(parts[:chains], parts[chains:], n)
+    proj = mine + others
 
     tall = jnp.concatenate(
         [embed_w.astype(f32), jnp.broadcast_to(time_vector, (3, width)), jnp.zeros((extra - 3, width), f32)]
@@ -406,23 +406,31 @@
     source = source_noise.T
     latent_shape = shape((channels, tokens), bf16)
 
+    cost = 2 * rows * tokens * cols
+    total = call(
+        functools.partial(early_kernel, width=width),
+        "generator_early",
+        shape((rows, tokens), f32),
+        (source, gram, *mine, readout),
+        cost=cost,
+    )
     own_first, mix, gram = call(
-        functools.partial(first_kernel, width=width),
-        "generator",
+        late_kernel,
+        "generator_late",
         [latent_shape, shape((rows, tokens), f32), shape((rows, rows), f32)],
-        (source, score_noise.T, level, gram, *proj, readout),
-    )
-    (by1,) = swap([own_first], "role", roles, 1)
-    near = jnp.where(role == 1, by1, own_first)
-    (by2,) = swap([near], "role", roles, 2)
-    drawn = jnp.where(role < 2, near, by2)
+        (source, score_noise.T, level, gram, total, *others, readout),
+    )
+    by2 = swap(own_first, "role", roles, 2)
+    even = jnp.where(role == 2, by2, own_first)
+    by1 = swap(even, "role", roles, 1)
+    drawn = jnp.where(role % 2 == 0, even, by1)
     slope_shapes = [shape((cols, tokens), f32), shape((2 * rows, tokens), bf16)]
     first_slopes = call(
         functools.partial(slope_kernel, width=width),
         "slopes",
         slope_shapes,
         (source, gram, *proj),
-        cost=2 * rows * tokens * cols,
+        cost=cost,
     )
     generated, piece, flat, *slopes = call(
         functools.partial(second_kernel, width=width),
@@ -433,29 +441,26 @@
             shape((1, tokens), f32),
             *slope_shapes,
         ],
-        (near, by2, mix, gram, *proj, readout, columns),
-    )
-    fake, adversarial, real = (swap([piece], "role", roles, bit)[0] for bit in (2, 3, 1))
+        (even, by1, mix, gram, *proj, readout, columns),
+    )
+    fake, adversarial, real = (swap(piece, "role", roles, bit) for bit in (2, 3, 1))
     flat, drawn = lax.optimization_barrier((flat, drawn))
 
-    cost = 4 * rows * tokens * half
     tail = (*first_slopes, *slopes, columns)
     cot, *send = call(
         send_kernel,
         "cotangent_send",
-        [shape((2 * channels, tokens), bf16)] + [shape((rows, half // pieces), bf16)] * pieces,
+        [shape((2 * channels, tokens), bf16)] + [shape((rows, tile), bf16)] * chains,
         (real, adversarial, fake, generated, piece, flat, *tail),
         cost=cost,
     )
-    received = swap(send, "fsdp", n, 1)
     kept = call(
-        keep_kernel, "cotangent_keep", [shape((rows, half // pieces), f32)] * pieces, (cot, *tail), cost=cost
-    )
-    totals = add_along(kept, received, n)
-    others = swap(totals, "fsdp", n, 1)
+        keep_kernel, "cotangent_keep", [shape((rows, tile), f32)] * chains, (cot, *tail), cost=cost
+    )
+    totals, others = add_all(kept, send, n)
     factor = 1.0 / math.sqrt(tokens * n)
     grads = gradient(own_rows, totals, 0, factor, cols)
-    for at, other in enumerate(others, pieces):
+    for at, other in enumerate(others, chains):
         grads = gradient(own_rows, [other], at, factor, cols, grads)
     return (grads, drawn.T)
 

time: 62.5 us -> 62 us (level)
  waiting for transfers between devices: 21.2 us -> 11.9 us
  starting transfers between devices: 25.7 us -> 34.4 us
    ppermute x21, waiting for transfers between devices: 21.2 us -> 11.9 us  [swap(): return lax.ppermute(value, axis, [(i, i ^ bit) for i in range(n)])]
    ppermute x21, starting transfers between devices: 25.7 us -> 34.4 us  [swap(): return lax.ppermute(value, axis, [(i, i ^ bit) for i in range(n)])]
    pallas_call x5 -> x6, Pallas kernels: 4.65 us -> 4.61 us  [call(): pl.pallas_call(kernel, out_shape=out_shape, in_specs=[vmem] * len(inputs)...]
  transfers between devices with their start and end apart: 21 -> 21, of which waited for: 15 -> 12; matrix products, arithmetic and copies ran while one was open for 6% -> 6% of each run, Pallas kernels for 8% -> 9%
where the time goes in v3:
time: 62 us; the launch traced here: 61.8 us
  starting transfers between devices  34.4 us (55%)
  waiting for transfers between devices  11.9 us (19%)
  Pallas kernels  10.2 us (16%)
  other arithmetic  3.01 us (5%)
  matrix products  0.98 us (2%)
  between operations  0.92 us (1%)
    ppermute x21, starting transfers between devices, swap(): return lax.ppermute(value, axis, [(i, i ^ bit) for i in range(n)])  34.4 us
    ppermute x21, waiting for transfers between devices, swap(): return lax.ppermute(value, axis, [(i, i ^ bit) for i in range(n)])  11.9 us
    pallas_call x6, Pallas kernels, call(): pl.pallas_call(kernel, out_shape=out_shape, in_specs=[vmem] * len(inputs)...  4.61 us
    pallas_call x3, Pallas kernels, gradient(): pl.pallas_call(functools.partial(grad_kernel, factor=factor, first_piece=...  3.57 us
    pallas_call x1, Pallas kernels, part_of(): pl.pallas_call(part_kernel, out_shape=shapes, in_specs=[hbm, vmem, hbm],...  1.99 us
  transfers between devices with their start and end apart: 21, of which 12 were waited for; matrix products, arithmetic and copies ran while one was open for 6% of the time, Pallas kernels for 9%

profile of v3, /device:TPU:0, one launch (start us, length us, event | category | flops | bytes accessed | tf_op | source)
XLA Modules:
  0.0 61.8 jit_solution(17854117205966234652)
XLA Ops:
  0.6 0.8 %pad_maximum_fusion.vectors_ref = f32[2,3072]{1,0:T(2,128)S(1)} fusion(f32[1,3072]{1,0:T(1,128)} %param.13, f32[1,3072]{1,0:T(1,128)} %param.12), kind=kLoop, calls=%fused_computation.29 | loop fusion | flops 6144 | bytes 49152 | tf_op jit(solution)/shard_map/concatenate | solution.py:395
  1.4 2.0 %part.1 = (f32[72,384]{1,0:T(8,128)S(1)}, f32[72,384]{1,0:T(8,128)S(1)}, bf16[72,384]{1,0:T(8,128)(2,1)S(1)}, bf16[72,384]{1,0:T(8,128)(2,1)S(1)}, bf16[144,384]{1,0:T(8,128)(2,1)S(1)}) custom-call(bf16[64,3072]{1,0:T(8,128)(2,1)} %bitcast.22, f32[2,3072]{1,0:T(2,128)S(1)} %pad_maximum_fusion.vectors_ref, bf16[1,384,1536]{2,1,0:T(8,128)(2,1)} %block_ref.1), custom_call_target="tpu_custom_call" | custom-call | flops 169869312 | bytes 1179648 | tf_op jit(solution)/shard_map/part/pallas_call | solution.py:312
  3.5 3.0 %collective-permute-start = (bf16[72,384]{1,0:T(8,128)(2,1)S(1)}, bf16[72,384]{1,0:T(8,128)(2,1)S(1)}, u32[]{:S(2)}, u32[]{:S(2)}) collective-permute-start(bf16[72,384]{1,0:T(8,128)(2,1)S(1)} %get-tuple-element.26), channel_id=1, source_target_pairs={{0,1},{1,0},{2,3},{3,2},{4,5},{5,4},{6,7},{7,6},{8,9},{9,8},{10,11... | collective-permute-start | bytes 165896 | tf_op jit(solution)/shard_map/ppermute | solution.py:357
  6.5 1.6 %collective-permute-start.3 = (bf16[72,384]{1,0:T(8,128)(2,1)S(1)}, bf16[72,384]{1,0:T(8,128)(2,1)S(1)}, u32[]{:S(2)}, u32[]{:S(2)}) collective-permute-start(bf16[72,384]{1,0:T(8,128)(2,1)S(1)} %get-tuple-element.28), channel_id=1, source_target_pairs={{0,2},{1,3},{2,0},{3,1},{4,6},{5,7},{6,4},{7,5},{8,10},{9,11},{10,... | collective-permute-start | bytes 165896 | tf_op jit(solution)/shard_map/ppermute | solution.py:357
  8.1 1.0 %bitcast_convert_fusion = f32[64,3072]{1,0:T(8,128)S(1)} fusion(bf16[1,64,3072]{2,1,0:T(8,128)(2,1)} %param.11), kind=kLoop, calls=%fused_computation.31 | loop fusion | flops 196608 | bytes 1179648 | tf_op jit(solution)/shard_map/convert_element_type | solution.py:401
  9.3 2.7 %collective-permute-start.1 = (bf16[72,384]{1,0:T(8,128)(2,1)S(1)}, bf16[72,384]{1,0:T(8,128)(2,1)S(1)}, u32[]{:S(2)}, u32[]{:S(2)}) collective-permute-start(bf16[72,384]{1,0:T(8,128)(2,1)S(1)} %fusion.6), channel_id=1, source_target_pairs={{0,4},{1,5},{2,6},{3,7},{4,0},{5,1},{6,2},{7,3},{8,12},{9,13},{10,... | collective-permute-start | bytes 165896 | tf_op jit(solution)/shard_map/ppermute | solution.py:357
  11.9 1.5 %collective-permute-start.4 = (bf16[72,384]{1,0:T(8,128)(2,1)S(1)}, bf16[72,384]{1,0:T(8,128)(2,1)S(1)}, u32[]{:S(2)}, u32[]{:S(2)}) collective-permute-start(bf16[72,384]{1,0:T(8,128)(2,1)S(1)} %fusion.7), channel_id=1, source_target_pairs={{0,1},{1,0},{2,3},{3,2},{4,5},{5,4},{6,7},{7,6},{8,9},{9,8},{10,11... | collective-permute-start | bytes 165896 | tf_op jit(solution)/shard_map/ppermute | solution.py:357
  13.4 0.9 %collective-permute-done.1 = bf16[72,384]{1,0:T(8,128)(2,1)S(1)} collective-permute-done((bf16[72,384]{1,0:T(8,128)(2,1)S(1)}, bf16[72,384]{1,0:T(8,128)(2,1)S(1)}, u32[]{:S(2)}, u32[]{:S(2)}) %collective-permute-start.1) | collective-permute-done | bytes 55328 | tf_op jit(solution)/shard_map/ppermute | solution.py:357
  14.4 1.6 %collective-permute-start.2 = (bf16[72,384]{1,0:T(8,128)(2,1)S(1)}, bf16[72,384]{1,0:T(8,128)(2,1)S(1)}, u32[]{:S(2)}, u32[]{:S(2)}) collective-permute-start(bf16[72,384]{1,0:T(8,128)(2,1)S(1)} %fusion.10), channel_id=1, source_target_pairs={{0,2},{1,3},{2,0},{3,1},{4,6},{5,7},{6,4},{7,5},{8,10},{9,11},{10,... | collective-permute-start | bytes 165896 | tf_op jit(solution)/shard_map/ppermute | solution.py:357
  16.2 3.1 %collective-permute-start.5 = (bf16[72,384]{1,0:T(8,128)(2,1)S(1)}, bf16[72,384]{1,0:T(8,128)(2,1)S(1)}, u32[]{:S(2)}, u32[]{:S(2)}) collective-permute-start(bf16[72,384]{1,0:T(8,128)(2,1)S(1)} %fusion.11), channel_id=1, source_target_pairs={{0,4},{1,5},{2,6},{3,7},{4,0},{5,1},{6,2},{7,3},{8,12},{9,13},{10,... | collective-permute-start | bytes 165896 | tf_op jit(solution)/shard_map/ppermute | solution.py:357
  19.3 1.5 %collective-permute-start.6 = (bf16[72,384]{1,0:T(8,128)(2,1)S(1)}, bf16[72,384]{1,0:T(8,128)(2,1)S(1)}, u32[]{:S(2)}, u32[]{:S(2)}) collective-permute-start(bf16[72,384]{1,0:T(8,128)(2,1)S(1)} %add_convert_fusion.3.rest_0_), channel_id=1, source_target_pairs={{0,1},{1,0},{2,3},{3,2},{4,5},{5,4},{6,7},{7,6},{8,9},{9,8},{10,11... | collective-permute-start | bytes 165896 | tf_op jit(solution)/shard_map/ppermute | solution.py:357
  21.4 1.7 %collective-permute-start.7 = (bf16[72,384]{1,0:T(8,128)(2,1)S(1)}, bf16[72,384]{1,0:T(8,128)(2,1)S(1)}, u32[]{:S(2)}, u32[]{:S(2)}) collective-permute-start(bf16[72,384]{1,0:T(8,128)(2,1)S(1)} %add_convert_fusion.2.rest_1_), channel_id=1, source_target_pairs={{0,2},{1,3},{2,0},{3,1},{4,6},{5,7},{6,4},{7,5},{8,10},{9,11},{10,... | collective-permute-start | bytes 165896 | tf_op jit(solution)/shard_map/ppermute | solution.py:357
  23.2 1.0 %fusion.gram_ref = f32[72,72]{1,0:T(8,128)S(1)} fusion(f32[3,3072]{1,0:T(4,128)S(1)} %broadcast_in_dim.15, f32[64,3072]{1,0:T(8,128)S(1)} %bitcast_convert_fusion, f32[72]{0:T(128)S(1)} %pad.4.clone), kind=kOutput, calls=%fused_computation | convolution fusion | flops 191545344 | bytes 844320 | tf_op jit(solution)/shard_map/dot_general | solution.py:403
  24.2 0.9 %generator_early.1.total_ref = f32[72,384]{1,0:T(8,128)S(1)} custom-call(bf16[64,384]{1,0:T(8,128)(2,1)S(1)} %bitcast.17, f32[72,72]{1,0:T(8,128)S(1)} %fusion.gram_ref, bf16[72,384]{1,0:T(8,128)(2,1)S(1)} %add_convert_fusion.3.rest_0_, bf16[72,384]{1,0:T(8,128)(2,1)S(1)} %add_convert_fusion.2.rest_1_, bf16[64,1536]{1,0:T(8,128)(2,1)S(1)} %bitcast.14), custom_call_target="tpu_custom_call" | custom-call | flops 84934656 | bytes 84934 | tf_op jit(solution)/shard_map/generator_early/pallas_call | solution.py:287
  26.4 0.8 %collective-permute-start.8 = (bf16[64,384]{1,0:T(8,128)(2,1)S(1)}, bf16[64,384]{1,0:T(8,128)(2,1)S(1)}, u32[]{:S(2)}, u32[]{:S(2)}) collective-permute-start(bf16[64,384]{1,0:T(8,128)(2,1)S(1)} %get-tuple-element.29), channel_id=1, source_target_pairs={{0,16},{8,24},{16,0},{24,8},{1,17},{9,25},{17,1},{25,9},{2,18},{10... | collective-permute-start | bytes 147464 | tf_op jit(solution)/shard_map/ppermute | solution.py:357
  27.5 3.1 %collective-permute-done.8 = bf16[64,384]{1,0:T(8,128)(2,1)S(1)} collective-permute-done((bf16[64,384]{1,0:T(8,128)(2,1)S(1)}, bf16[64,384]{1,0:T(8,128)(2,1)S(1)}, u32[]{:S(2)}, u32[]{:S(2)}) %collective-permute-start.8) | collective-permute-done | bytes 49184 | tf_op jit(solution)/shard_map/ppermute | solution.py:357
  30.9 1.5 %slopes.1 = (f32[1536,384]{1,0:T(8,128)S(1)}, bf16[144,384]{1,0:T(8,128)(2,1)S(1)}) custom-call(bf16[64,384]{1,0:T(8,128)(2,1)S(1)} %bitcast.19, f32[72,72]{1,0:T(8,128)S(1)} %get-tuple-element.31.gram_ref, bf16[72,384]{1,0:T(8,128)(2,1)S(1)} %add_convert_fusion.3.rest_0_, bf16[72,384]{1,0:T(8,128)(2,1)S(1)} %add_convert_fusion.2.rest_1_, ...), custom_call_target="tpu_custom_call" | custom-call | flops 84934656 | bytes 84934 | tf_op jit(solution)/shard_map/slopes/pallas_call | solution.py:287
  32.4 2.3 %collective-permute-start.12 = (bf16[64,384]{1,0:T(8,128)(2,1)S(1)}, bf16[64,384]{1,0:T(8,128)(2,1)S(1)}, u32[]{:S(2)}, u32[]{:S(2)}) collective-permute-start(bf16[64,384]{1,0:T(8,128)(2,1)S(1)} %get-tuple-element.32.piece_ref), channel_id=1, source_target_pairs={{0,16},{8,24},{16,0},{24,8},{1,17},{9,25},{17,1},{25,9},{2,18},{10... | collective-permute-start | bytes 147464 | tf_op jit(solution)/shard_map/ppermute | solution.py:357
  34.7 0.9 %collective-permute-start.11 = (bf16[64,384]{1,0:T(8,128)(2,1)S(1)}, bf16[64,384]{1,0:T(8,128)(2,1)S(1)}, u32[]{:S(2)}, u32[]{:S(2)}) collective-permute-start(bf16[64,384]{1,0:T(8,128)(2,1)S(1)} %get-tuple-element.32.piece_ref), channel_id=1, source_target_pairs={{0,24},{8,16},{16,8},{24,0},{1,25},{9,17},{17,9},{25,1},{2,26},{10... | collective-permute-start | bytes 147464 | tf_op jit(solution)/shard_map/ppermute | solution.py:357
  36.9 1.4 %collective-permute-done.11.adversarial_ref = bf16[64,384]{1,0:T(8,128)(2,1)S(1)} collective-permute-done((bf16[64,384]{1,0:T(8,128)(2,1)S(1)}, bf16[64,384]{1,0:T(8,128)(2,1)S(1)}, u32[]{:S(2)}, u32[]{:S(2)}) %collective-permute-start.11) | collective-permute-done | bytes 49184 | tf_op jit(solution)/shard_map/ppermute | solution.py:357
  39.1 1.6 %collective-permute-start.17 = (bf16[72,384]{1,0:T(8,128)(2,1)S(1)}, bf16[72,384]{1,0:T(8,128)(2,1)S(1)}, u32[]{:S(2)}, u32[]{:S(2)}) collective-permute-start(bf16[72,384]{1,0:T(8,128)(2,1)S(1)} %get-tuple-element.44), channel_id=1, source_target_pairs={{0,1},{1,0},{2,3},{3,2},{4,5},{5,4},{6,7},{7,6},{8,9},{9,8},{10,11... | collective-permute-start | bytes 165896 | tf_op jit(solution)/shard_map/ppermute | solution.py:357
  40.6 1.4 %collective-permute-start.13 = (bf16[72,384]{1,0:T(8,128)(2,1)S(1)}, bf16[72,384]{1,0:T(8,128)(2,1)S(1)}, u32[]{:S(2)}, u32[]{:S(2)}) collective-permute-start(bf16[72,384]{1,0:T(8,128)(2,1)S(1)} %get-tuple-element.42), channel_id=1, source_target_pairs={{0,2},{1,3},{2,0},{3,1},{4,6},{5,7},{6,4},{7,5},{8,10},{9,11},{10,... | collective-permute-start | bytes 165896 | tf_op jit(solution)/shard_map/ppermute | solution.py:357
  42.8 1.0 %collective-permute-done.17 = bf16[72,384]{1,0:T(8,128)(2,1)S(1)} collective-permute-done((bf16[72,384]{1,0:T(8,128)(2,1)S(1)}, bf16[72,384]{1,0:T(8,128)(2,1)S(1)}, u32[]{:S(2)}, u32[]{:S(2)}) %collective-permute-start.17) | collective-permute-done | bytes 55328 | tf_op jit(solution)/shard_map/ppermute | solution.py:357
  43.8 3.0 %collective-permute-start.18 = (bf16[72,384]{1,0:T(8,128)(2,1)S(1)}, bf16[72,384]{1,0:T(8,128)(2,1)S(1)}, u32[]{:S(2)}, u32[]{:S(2)}) collective-permute-start(bf16[72,384]{1,0:T(8,128)(2,1)S(1)} %fusion.9), channel_id=1, source_target_pairs={{0,4},{1,5},{2,6},{3,7},{4,0},{5,1},{6,2},{7,3},{8,12},{9,13},{10,... | collective-permute-start | bytes 165896 | tf_op jit(solution)/shard_map/ppermute | solution.py:357
  46.9 1.5 %collective-permute-start.14 = (bf16[72,384]{1,0:T(8,128)(2,1)S(1)}, bf16[72,384]{1,0:T(8,128)(2,1)S(1)}, u32[]{:S(2)}, u32[]{:S(2)}) collective-permute-start(bf16[72,384]{1,0:T(8,128)(2,1)S(1)} %fusion.8), channel_id=1, source_target_pairs={{0,1},{1,0},{2,3},{3,2},{4,5},{5,4},{6,7},{7,6},{8,9},{9,8},{10,11... | collective-permute-start | bytes 165896 | tf_op jit(solution)/shard_map/ppermute | solution.py:357
  48.3 1.8 %collective-permute-done.18 = bf16[72,384]{1,0:T(8,128)(2,1)S(1)} collective-permute-done((bf16[72,384]{1,0:T(8,128)(2,1)S(1)}, bf16[72,384]{1,0:T(8,128)(2,1)S(1)}, u32[]{:S(2)}, u32[]{:S(2)}) %collective-permute-start.18) | collective-permute-done | bytes 55328 | tf_op jit(solution)/shard_map/ppermute | solution.py:357
  51.1 2.7 %collective-permute-start.15 = (bf16[72,384]{1,0:T(8,128)(2,1)S(1)}, bf16[72,384]{1,0:T(8,128)(2,1)S(1)}, u32[]{:S(2)}, u32[]{:S(2)}) collective-permute-start(bf16[72,384]{1,0:T(8,128)(2,1)S(1)} %fusion.12), channel_id=1, source_target_pairs={{0,4},{1,5},{2,6},{3,7},{4,0},{5,1},{6,2},{7,3},{8,12},{9,13},{10,... | collective-permute-start | bytes 165896 | tf_op jit(solution)/shard_map/ppermute | solution.py:357
  54.4 2.0 %collective-permute-start.20 = (bf16[72,384]{1,0:T(8,128)(2,1)S(1)}, bf16[72,384]{1,0:T(8,128)(2,1)S(1)}, u32[]{:S(2)}, u32[]{:S(2)}) collective-permute-start(bf16[72,384]{1,0:T(8,128)(2,1)S(1)} %add_convert_fusion.rest_0_), channel_id=1, source_target_pairs={{0,1},{1,0},{2,3},{3,2},{4,5},{5,4},{6,7},{7,6},{8,9},{9,8},{10,11... | collective-permute-start | bytes 165896 | tf_op jit(solution)/shard_map/ppermute | solution.py:357
  56.5 1.1 %collective-permute-start.16 = (bf16[72,384]{1,0:T(8,128)(2,1)S(1)}, bf16[72,384]{1,0:T(8,128)(2,1)S(1)}, u32[]{:S(2)}, u32[]{:S(2)}) collective-permute-start(bf16[72,384]{1,0:T(8,128)(2,1)S(1)} %add_convert_fusion.1.rest_1_), channel_id=1, source_target_pairs={{0,2},{1,3},{2,0},{3,1},{4,6},{5,7},{6,4},{7,5},{8,10},{9,11},{10,... | collective-permute-start | bytes 165896 | tf_op jit(solution)/shard_map/ppermute | solution.py:357
  57.5 1.3 %gradient.3.rest_1_ = f32[1,384,1536]{2,1,0:T(8,128)} custom-call(bf16[144,384]{1,0:T(8,128)(2,1)S(1)} %get-tuple-element.24.own_ref, bf16[72,384]{1,0:T(8,128)(2,1)S(1)} %add_convert_fusion.rest_0_, bf16[72,384]{1,0:T(8,128)(2,1)S(1)} %add_convert_fusion.1.rest_1_), custom_call_target="tpu_custom_call" | custom-call | flops 169869312 | bytes 1179648 | tf_op jit(solution)/shard_map/gradient/pallas_call | solution.py:339
  58.9 1.1 %gradient.4.rest_1_ = f32[1,384,1536]{2,1,0:T(8,128)} custom-call(bf16[144,384]{1,0:T(8,128)(2,1)S(1)} %get-tuple-element.24.own_ref, bf16[72,384]{1,0:T(8,128)(2,1)S(1)} %collective-permute-done.20.rest_0_, f32[1,384,1536]{2,1,0:T(8,128)} %gradient.3.rest_1_), custom_call_target="tpu_custom_call", output_to_operand_aliasing={{}: (2, {})} | custom-call | flops 84934656 | bytes 589824 | tf_op jit(solution)/shard_map/gradient/pallas_call | solution.py:339
  60.7 1.1 %gradient.5 = f32[1,384,1536]{2,1,0:T(8,128)} custom-call(bf16[144,384]{1,0:T(8,128)(2,1)S(1)} %get-tuple-element.24.own_ref, bf16[72,384]{1,0:T(8,128)(2,1)S(1)} %collective-permute-done.16.rest_0_, f32[1,384,1536]{2,1,0:T(8,128)} %gradient.4.rest_1_), custom_call_target="tpu_custom_call", output_to_operand_aliasing={{}: (2, {})} | custom-call | flops 84934656 | bytes 589824 | tf_op jit(solution)/shard_map/gradient/pallas_call | solution.py:339
  (53 shorter events, 8.1 us)
Async XLA Ops:
  0.6 22.5 %copy-start.3 = (f32[1,3072]{1,0:T(1,128)S(1)}, f32[1,3072]{1,0:T(1,128)}, u32[]{:S(2)}) copy-start(f32[1,3072]{1,0:T(1,128)} %param.12) | copy-start | bytes 36868
  3.4 20.7 %copy-start.4 = (f32[384]{0:T(512)S(1)}, f32[384]{0:T(512)}, u32[]{:S(2)}) copy-start(f32[384]{0:T(512)} %param.10) | copy-start | bytes 4612
  3.4 20.7 %copy-start = (bf16[1,1536,64]{1,2,0:T(8,128)(2,1)S(1)}, bf16[1,1536,64]{1,2,0:T(8,128)(2,1)}, u32[]{:S(2)}) copy-start(bf16[1,1536,64]{1,2,0:T(8,128)(2,1)} %param.15) | copy-start | bytes 589828
  3.5 20.7 %copy-start.1 = (bf16[384,64]{0,1:T(8,128)(2,1)S(1)}, bf16[384,64]{0,1:T(8,128)(2,1)}, u32[]{:S(2)}) copy-start(bf16[384,64]{0,1:T(8,128)(2,1)} %param.8) | copy-start | bytes 147460
  3.5 22.2 %copy-start.2 = (bf16[384,64]{0,1:T(8,128)(2,1)S(1)}, bf16[384,64]{0,1:T(8,128)(2,1)}, u32[]{:S(2)}) copy-start(bf16[384,64]{0,1:T(8,128)(2,1)} %param.9) | copy-start | bytes 147460
  3.5 5.7 %collective-permute-start = (bf16[72,384]{1,0:T(8,128)(2,1)S(1)}, bf16[72,384]{1,0:T(8,128)(2,1)S(1)}, u32[]{:S(2)}, u32[]{:S(2)}) collective-permute-start(bf16[72,384]{1,0:T(8,128)(2,1)S(1)} %get-tuple-element.26), channel_id=1, source_target_pairs={{0,1},{1,0},{2,3},{3,2},{4,5},{5,4},{6,7},{7,6},{8,9},{9,8},{10,11... | collective-permute-start | bytes 165896 | tf_op jit(solution)/shard_map/ppermute | solution.py:357
  6.5 5.4 %collective-permute-start.3 = (bf16[72,384]{1,0:T(8,128)(2,1)S(1)}, bf16[72,384]{1,0:T(8,128)(2,1)S(1)}, u32[]{:S(2)}, u32[]{:S(2)}) collective-permute-start(bf16[72,384]{1,0:T(8,128)(2,1)S(1)} %get-tuple-element.28), channel_id=1, source_target_pairs={{0,2},{1,3},{2,0},{3,1},{4,6},{5,7},{6,4},{7,5},{8,10},{9,11},{10,... | collective-permute-start | bytes 165896 | tf_op jit(solution)/shard_map/ppermute | solution.py:357
  9.3 5.1 %collective-permute-start.1 = (bf16[72,384]{1,0:T(8,128)(2,1)S(1)}, bf16[72,384]{1,0:T(8,128)(2,1)S(1)}, u32[]{:S(2)}, u32[]{:S(2)}) collective-permute-start(bf16[72,384]{1,0:T(8,128)(2,1)S(1)} %fusion.6), channel_id=1, source_target_pairs={{0,4},{1,5},{2,6},{3,7},{4,0},{5,1},{6,2},{7,3},{8,12},{9,13},{10,... | collective-permute-start | bytes 165896 | tf_op jit(solution)/shard_map/ppermute | solution.py:357
  11.9 4.2 %collective-permute-start.4 = (bf16[72,384]{1,0:T(8,128)(2,1)S(1)}, bf16[72,384]{1,0:T(8,128)(2,1)S(1)}, u32[]{:S(2)}, u32[]{:S(2)}) collective-permute-start(bf16[72,384]{1,0:T(8,128)(2,1)S(1)} %fusion.7), channel_id=1, source_target_pairs={{0,1},{1,0},{2,3},{3,2},{4,5},{5,4},{6,7},{7,6},{8,9},{9,8},{10,11... | collective-permute-start | bytes 165896 | tf_op jit(solution)/shard_map/ppermute | solution.py:357
  14.4 4.8 %collective-permute-start.2 = (bf16[72,384]{1,0:T(8,128)(2,1)S(1)}, bf16[72,384]{1,0:T(8,128)(2,1)S(1)}, u32[]{:S(2)}, u32[]{:S(2)}) collective-permute-start(bf16[72,384]{1,0:T(8,128)(2,1)S(1)} %fusion.10), channel_id=1, source_target_pairs={{0,2},{1,3},{2,0},{3,1},{4,6},{5,7},{6,4},{7,5},{8,10},{9,11},{10,... | collective-permute-start | bytes 165896 | tf_op jit(solution)/shard_map/ppermute | solution.py:357
  16.2 5.2 %collective-permute-start.5 = (bf16[72,384]{1,0:T(8,128)(2,1)S(1)}, bf16[72,384]{1,0:T(8,128)(2,1)S(1)}, u32[]{:S(2)}, u32[]{:S(2)}) collective-permute-start(bf16[72,384]{1,0:T(8,128)(2,1)S(1)} %fusion.11), channel_id=1, source_target_pairs={{0,4},{1,5},{2,6},{3,7},{4,0},{5,1},{6,2},{7,3},{8,12},{9,13},{10,... | collective-permute-start | bytes 165896 | tf_op jit(solution)/shard_map/ppermute | solution.py:357
  19.3 5.8 %collective-permute-start.6 = (bf16[72,384]{1,0:T(8,128)(2,1)S(1)}, bf16[72,384]{1,0:T(8,128)(2,1)S(1)}, u32[]{:S(2)}, u32[]{:S(2)}) collective-permute-start(bf16[72,384]{1,0:T(8,128)(2,1)S(1)} %add_convert_fusion.3.rest_0_), channel_id=1, source_target_pairs={{0,1},{1,0},{2,3},{3,2},{4,5},{5,4},{6,7},{7,6},{8,9},{9,8},{10,11... | collective-permute-start | bytes 165896 | tf_op jit(solution)/shard_map/ppermute | solution.py:357
  21.4 4.2 %collective-permute-start.7 = (bf16[72,384]{1,0:T(8,128)(2,1)S(1)}, bf16[72,384]{1,0:T(8,128)(2,1)S(1)}, u32[]{:S(2)}, u32[]{:S(2)}) collective-permute-start(bf16[72,384]{1,0:T(8,128)(2,1)S(1)} %add_convert_fusion.2.rest_1_), channel_id=1, source_target_pairs={{0,2},{1,3},{2,0},{3,1},{4,6},{5,7},{6,4},{7,5},{8,10},{9,11},{10,... | collective-permute-start | bytes 165896 | tf_op jit(solution)/shard_map/ppermute | solution.py:357
  26.4 4.2 %collective-permute-start.8 = (bf16[64,384]{1,0:T(8,128)(2,1)S(1)}, bf16[64,384]{1,0:T(8,128)(2,1)S(1)}, u32[]{:S(2)}, u32[]{:S(2)}) collective-permute-start(bf16[64,384]{1,0:T(8,128)(2,1)S(1)} %get-tuple-element.29), channel_id=1, source_target_pairs={{0,16},{8,24},{16,0},{24,8},{1,17},{9,25},{17,1},{25,9},{2,18},{10... | collective-permute-start | bytes 147464 | tf_op jit(solution)/shard_map/ppermute | solution.py:357
  30.6 1.8 %collective-permute-start.9 = (bf16[64,384]{1,0:T(8,128)(2,1)S(1)}, bf16[64,384]{1,0:T(8,128)(2,1)S(1)}, u32[]{:S(2)}, u32[]{:S(2)}) collective-permute-start(bf16[64,384]{1,0:T(8,128)(2,1)S(1)} %broadcast_select_fusion.1.even_ref), channel_id=1, source_target_pairs={{0,8},{8,0},{16,24},{24,16},{1,9},{9,1},{17,25},{25,17},{2,10},{10... | collective-permute-start | bytes 147464 | tf_op jit(solution)/shard_map/ppermute | solution.py:357
  32.4 4.5 %collective-permute-start.12 = (bf16[64,384]{1,0:T(8,128)(2,1)S(1)}, bf16[64,384]{1,0:T(8,128)(2,1)S(1)}, u32[]{:S(2)}, u32[]{:S(2)}) collective-permute-start(bf16[64,384]{1,0:T(8,128)(2,1)S(1)} %get-tuple-element.32.piece_ref), channel_id=1, source_target_pairs={{0,16},{8,24},{16,0},{24,8},{1,17},{9,25},{17,1},{25,9},{2,18},{10... | collective-permute-start | bytes 147464 | tf_op jit(solution)/shard_map/ppermute | solution.py:357
  34.7 3.5 %collective-permute-start.11 = (bf16[64,384]{1,0:T(8,128)(2,1)S(1)}, bf16[64,384]{1,0:T(8,128)(2,1)S(1)}, u32[]{:S(2)}, u32[]{:S(2)}) collective-permute-start(bf16[64,384]{1,0:T(8,128)(2,1)S(1)} %get-tuple-element.32.piece_ref), channel_id=1, source_target_pairs={{0,24},{8,16},{16,8},{24,0},{1,25},{9,17},{17,9},{25,1},{2,26},{10... | collective-permute-start | bytes 147464 | tf_op jit(solution)/shard_map/ppermute | solution.py:357
  35.6 2.6 %collective-permute-start.10 = (bf16[64,384]{1,0:T(8,128)(2,1)S(1)}, bf16[64,384]{1,0:T(8,128)(2,1)S(1)}, u32[]{:S(2)}, u32[]{:S(2)}) collective-permute-start(bf16[64,384]{1,0:T(8,128)(2,1)S(1)} %get-tuple-element.32.piece_ref), channel_id=1, source_target_pairs={{0,8},{8,0},{16,24},{24,16},{1,9},{9,1},{17,25},{25,17},{2,10},{10... | collective-permute-start | bytes 147464 | tf_op jit(solution)/shard_map/ppermute | solution.py:357
  39.1 4.8 %collective-permute-start.17 = (bf16[72,384]{1,0:T(8,128)(2,1)S(1)}, bf16[72,384]{1,0:T(8,128)(2,1)S(1)}, u32[]{:S(2)}, u32[]{:S(2)}) collective-permute-start(bf16[72,384]{1,0:T(8,128)(2,1)S(1)} %get-tuple-element.44), channel_id=1, source_target_pairs={{0,1},{1,0},{2,3},{3,2},{4,5},{5,4},{6,7},{7,6},{8,9},{9,8},{10,11... | collective-permute-start | bytes 165896 | tf_op jit(solution)/shard_map/ppermute | solution.py:357
  40.6 6.2 %collective-permute-start.13 = (bf16[72,384]{1,0:T(8,128)(2,1)S(1)}, bf16[72,384]{1,0:T(8,128)(2,1)S(1)}, u32[]{:S(2)}, u32[]{:S(2)}) collective-permute-start(bf16[72,384]{1,0:T(8,128)(2,1)S(1)} %get-tuple-element.42), channel_id=1, source_target_pairs={{0,2},{1,3},{2,0},{3,1},{4,6},{5,7},{6,4},{7,5},{8,10},{9,11},{10,... | collective-permute-start | bytes 165896 | tf_op jit(solution)/shard_map/ppermute | solution.py:357
  43.8 6.3 %collective-permute-start.18 = (bf16[72,384]{1,0:T(8,128)(2,1)S(1)}, bf16[72,384]{1,0:T(8,128)(2,1)S(1)}, u32[]{:S(2)}, u32[]{:S(2)}) collective-permute-start(bf16[72,384]{1,0:T(8,128)(2,1)S(1)} %fusion.9), channel_id=1, source_target_pairs={{0,4},{1,5},{2,6},{3,7},{4,0},{5,1},{6,2},{7,3},{8,12},{9,13},{10,... | collective-permute-start | bytes 165896 | tf_op jit(solution)/shard_map/ppermute | solution.py:357
  46.9 4.2 %collective-permute-start.14 = (bf16[72,384]{1,0:T(8,128)(2,1)S(1)}, bf16[72,384]{1,0:T(8,128)(2,1)S(1)}, u32[]{:S(2)}, u32[]{:S(2)}) collective-permute-start(bf16[72,384]{1,0:T(8,128)(2,1)S(1)} %fusion.8), channel_id=1, source_target_pairs={{0,1},{1,0},{2,3},{3,2},{4,5},{5,4},{6,7},{7,6},{8,9},{9,8},{10,11... | collective-permute-start | bytes 165896 | tf_op jit(solution)/shard_map/ppermute | solution.py:357
  50.2 4.2 %collective-permute-start.19 = (bf16[72,384]{1,0:T(8,128)(2,1)S(1)}, bf16[72,384]{1,0:T(8,128)(2,1)S(1)}, u32[]{:S(2)}, u32[]{:S(2)}) collective-permute-start(bf16[72,384]{1,0:T(8,128)(2,1)S(1)} %fusion.13), channel_id=1, source_target_pairs={{0,2},{1,3},{2,0},{3,1},{4,6},{5,7},{6,4},{7,5},{8,10},{9,11},{10,... | collective-permute-start | bytes 165896 | tf_op jit(solution)/shard_map/ppermute | solution.py:357
  51.1 5.3 %collective-permute-start.15 = (bf16[72,384]{1,0:T(8,128)(2,1)S(1)}, bf16[72,384]{1,0:T(8,128)(2,1)S(1)}, u32[]{:S(2)}, u32[]{:S(2)}) collective-permute-start(bf16[72,384]{1,0:T(8,128)(2,1)S(1)} %fusion.12), channel_id=1, source_target_pairs={{0,4},{1,5},{2,6},{3,7},{4,0},{5,1},{6,2},{7,3},{8,12},{9,13},{10,... | collective-permute-start | bytes 165896 | tf_op jit(solution)/shard_map/ppermute | solution.py:357
  54.4 4.4 %collective-permute-start.20 = (bf16[72,384]{1,0:T(8,128)(2,1)S(1)}, bf16[72,384]{1,0:T(8,128)(2,1)S(1)}, u32[]{:S(2)}, u32[]{:S(2)}) collective-permute-start(bf16[72,384]{1,0:T(8,128)(2,1)S(1)} %add_convert_fusion.rest_0_), channel_id=1, source_target_pairs={{0,1},{1,0},{2,3},{3,2},{4,5},{5,4},{6,7},{7,6},{8,9},{9,8},{10,11... | collective-permute-start | bytes 165896 | tf_op jit(solution)/shard_map/ppermute | solution.py:357
  56.5 4.2 %collective-permute-start.16 = (bf16[72,384]{1,0:T(8,128)(2,1)S(1)}, bf16[72,384]{1,0:T(8,128)(2,1)S(1)}, u32[]{:S(2)}, u32[]{:S(2)}) collective-permute-start(bf16[72,384]{1,0:T(8,128)(2,1)S(1)} %add_convert_fusion.1.rest_1_), channel_id=1, source_target_pairs={{0,2},{1,3},{2,0},{3,1},{4,6},{5,7},{6,4},{7,5},{8,10},{9,11},{10,... | collective-permute-start | bytes 165896 | tf_op jit(solution)/shard_map/ppermute | solution.py:357

commit v4 on v3

--- a/solution.py
+++ b/solution.py
@@ -63,9 +63,8 @@
 
 
 def columns_of(at, tile):
-    chain = at % chains
-    kept = (lax.axis_index("fsdp") >> chain) & 1
-    base = 2 * tile * chain + tile * (kept if at < chains else 1 - kept)
+    kept = lax.axis_index("fsdp") & 1
+    base = tile * ((at % chains) + chains * (kept if at < chains else 1 - kept))
     return pl.ds(pl.multiple_of(base, tile), tile)
 
 
@@ -104,17 +103,32 @@
         outs[at][...] = (part[:rows] + part[rows:]).astype(outs[at].dtype)
 
 
-def network(wide16, scale, proj_refs, first_piece, readout_ref, slope_ref=None):
+def network(wide16, scale, proj_refs, first_piece, readout_ref):
     tile = proj_refs[0].shape[1]
     total = jnp.zeros((readout_ref.shape[0], wide16.shape[1]), f32)
     for at, proj_ref in enumerate(proj_refs, first_piece):
         hidden = scale * mm(proj_ref[...], wide16, 0, 0)
+        gate, unused = gelu_gate(hidden)
+        activated = (hidden * gate).astype(bf16)
+        total = total + mm(readout_ref[:, columns_of(at, tile)], activated, 1, 0)
+    return total
+
+
+def network_by_rows(wide, scale, turned_ref, tile, readout_ref, slope_ref):
+    total = jnp.zeros((readout_ref.shape[0], wide.shape[1]), f32)
+    wide16 = lanes_of_zeros(wide).astype(bf16)
+    for at in range(2 * chains):
+        rows = slice(at * tile, (at + 1) * tile)
+        hidden = scale * mm(turned_ref[rows, :], wide16, 1, 0)
         gate, square = gelu_gate(hidden)
         activated = (hidden * gate).astype(bf16)
         total = total + mm(readout_ref[:, columns_of(at, tile)], activated, 1, 0)
-        if slope_ref is not None:
-            slope_ref[at * tile : (at + 1) * tile, :] = gelu_slope(hidden, square, gate)
+        slope_ref[rows, :] = gelu_slope(hidden, square, gate)
     return total
+
+
+def lanes_of_zeros(wide, lanes=128):
+    return jnp.concatenate([wide, jnp.zeros((lanes - wide.shape[0], wide.shape[1]), f32)], axis=0)
 
 
 def early_kernel(latent_ref, gram_ref, *rest, width):
@@ -150,29 +164,35 @@
     return jnp.concatenate([scaled, scaled - scaled.astype(bf16).astype(f32)], axis=0).astype(bf16)
 
 
-def slope_kernel(latent_ref, gram_ref, *rest, width):
-    *proj_refs, slope_ref, scaled_ref = rest
+def slope_kernel(latent_ref, gram_ref, own_ref, *rest, width):
+    *proj_refs, own_turned_ref, turned_ref, slope_ref, scaled_ref = rest
+    own_turned_ref[...] = lanes_of_zeros(own_ref[...].astype(f32), 256).T.astype(bf16)
     tile = proj_refs[0].shape[1]
+    for at, proj_ref in enumerate(proj_refs):
+        turned = lanes_of_zeros(proj_ref[...].astype(f32)).T
+        turned_ref[at * tile : (at + 1) * tile, :] = turned.astype(bf16)
 
     @pl.when(lax.axis_index("role") == 0)
     def _():
         wide = widen(latent_ref[...], jnp.ones((1, latent_ref.shape[1]), f32))
         scale, unused = norm_scale(wide, gram_ref[...], width)
-        wide16 = wide.astype(bf16)
-        for at, proj_ref in enumerate(proj_refs):
-            hidden = scale * mm(proj_ref[...], wide16, 0, 0)
+        wide16 = lanes_of_zeros(wide).astype(bf16)
+        for at in range(2 * chains):
+            hidden = scale * mm(turned_ref[at * tile : (at + 1) * tile, :], wide16, 1, 0)
             gate, square = gelu_gate(hidden)
             slope_ref[at * tile : (at + 1) * tile, :] = gelu_slope(hidden, square, gate)
         scaled_ref[...] = in_parts(scale, wide)
 
 
-def second_kernel(even_ref, odd_ref, mix_ref, gram_ref, *rest, width):
+def second_kernel(own_ref, by2_ref, by3_ref, by1_ref, mix_ref, gram_ref, *rest, width):
     proj_refs = rest[: 2 * chains]
-    readout_ref, columns_ref, generated_ref, piece_ref, flat_ref, slope_ref, scaled_ref = rest[2 * chains :]
+    turned_ref, readout_ref, columns_ref, generated_ref, piece_ref, flat_ref, slope_ref, scaled_ref = rest[2 * chains :]
     role = lax.axis_index("role")
-    channels, tokens = even_ref.shape
+    channels, tokens = own_ref.shape
     tile = proj_refs[0].shape[1]
-    generated = jnp.where((role & 1) == 0, even_ref[...].astype(f32), odd_ref[...].astype(f32))
+    low = jnp.where(role == 0, own_ref[...].astype(f32), by1_ref[...].astype(f32))
+    high = jnp.where(role == 2, by2_ref[...].astype(f32), by3_ref[...].astype(f32))
+    generated = jnp.where(role < 2, low, high)
     generated_ref[...] = generated.astype(bf16)
 
     @pl.when(role > 0)
@@ -181,7 +201,7 @@
         noised = (1.0 - level) * generated + mix_ref[:channels, :]
         wide = widen(noised.astype(bf16), level)
         scale, seen = norm_scale(wide, gram_ref[...], width)
-        scores = network(wide.astype(bf16), scale, proj_refs, 0, readout_ref, slope_ref).astype(bf16)
+        scores = network_by_rows(wide, scale, turned_ref, tile, readout_ref, slope_ref).astype(bf16)
         piece_ref[...] = scores
         logit = jnp.sum(scores.astype(f32), axis=0, keepdims=True)
         flat_ref[...] = 1.0 / (1.0 + jnp.exp(-logit))
@@ -225,9 +245,9 @@
 
 
 def send_kernel(
+    fake_ref,
+    adversarial_ref,
     real_ref,
-    adversarial_ref,
-    fake_ref,
     generated_ref,
     piece_ref,
     flat_ref,
@@ -271,7 +291,7 @@
     for at, total_ref in enumerate(total_refs):
         here = slice(at * tile, (at + 1) * tile)
         total = total_ref[...].astype(f32)
-        part = mm(own, jnp.concatenate([total, total], axis=0).astype(bf16), 0, 0)
+        part = mm(own, lanes_of_zeros(jnp.concatenate([total, total], axis=0), 256).astype(bf16), 1, 0)
         buffer[:, here] = part * factor
         cols = columns_of(first_piece + at, tile)
         copy = pltpu.make_async_copy(buffer.at[:, here], out_ref.at[0, :, cols], sems.at[at])
@@ -328,7 +348,7 @@
 
 
 def gradient(own, totals, first_piece, factor, cols, buffer=None):
-    depth, tile, count = own.shape[1], cols // (2 * chains), len(totals)
+    depth, tile, count = own.shape[0], cols // (2 * chains), len(totals)
     vmem = pl.BlockSpec(memory_space=pltpu.VMEM)
     hbm = pl.BlockSpec(memory_space=pltpu.HBM)
     specs = [vmem] * (1 + count)
@@ -345,7 +365,7 @@
         scratch_shapes=[pltpu.VMEM((depth, count * tile), f32), pltpu.SemaphoreType.DMA((count,))],
         compiler_params=pltpu.CompilerParams(vmem_limit_bytes=16 * 1024 * 1024),
         cost_estimate=pl.CostEstimate(
-            flops=4 * own.shape[0] * depth * count * tile,
+            flops=2 * own.shape[1] * depth * count * tile,
             bytes_accessed=4 * depth * count * tile,
             transcendentals=0,
         ),
@@ -359,15 +379,13 @@
 
 def add_all(kept, sent, n):
     bits = [1 << at for at in range(n.bit_length() - 1)]
-    orders = [[1, *reversed(bits[1:])], [2, 1, *bits[2:]]]
     mine = []
-    for value, part, order in zip(kept, sent, orders):
-        for step, bit in enumerate(order):
-            outgoing = value.astype(bf16) if step else part
+    for value, part in zip(kept, sent):
+        for bit in bits:
+            outgoing = part if bit == 1 else value.astype(bf16)
             value = value + swap(outgoing, "fsdp", n, bit).astype(f32)
         mine.append(value.astype(bf16))
-    others = [swap(value, "fsdp", n, order[0]) for value, order in zip(mine, orders)]
-    return mine, others
+    return mine, [swap(value, "fsdp", n, 1) for value in mine]
 
 
 def shards(
@@ -420,16 +438,14 @@
         [latent_shape, shape((rows, tokens), f32), shape((rows, rows), f32)],
         (source, score_noise.T, level, gram, total, *others, readout),
     )
-    by2 = swap(own_first, "role", roles, 2)
-    even = jnp.where(role == 2, by2, own_first)
-    by1 = swap(even, "role", roles, 1)
-    drawn = jnp.where(role % 2 == 0, even, by1)
+    by2, by3, by1 = (swap(own_first, "role", roles, bit) for bit in (2, 3, 1))
+    drawn = jnp.where(role == 0, own_first, jnp.where(role == 1, by1, jnp.where(role == 2, by2, by3)))
     slope_shapes = [shape((cols, tokens), f32), shape((2 * rows, tokens), bf16)]
-    first_slopes = call(
+    own_turned, turned, *first_slopes = call(
         functools.partial(slope_kernel, width=width),
         "slopes",
-        slope_shapes,
-        (source, gram, *proj),
+        [shape((depth, 256), bf16), shape((cols, 128), bf16), *slope_shapes],
+        (source, gram, own_rows, *proj),
         cost=cost,
     )
     generated, piece, flat, *slopes = call(
@@ -441,7 +457,7 @@
             shape((1, tokens), f32),
             *slope_shapes,
         ],
-        (even, by1, mix, gram, *proj, readout, columns),
+        (own_first, by2, by3, by1, mix, gram, *proj, turned, readout, columns),
     )
     fake, adversarial, real = (swap(piece, "role", roles, bit) for bit in (2, 3, 1))
     flat, drawn = lax.optimization_barrier((flat, drawn))
@@ -451,7 +467,7 @@
         send_kernel,
         "cotangent_send",
         [shape((2 * channels, tokens), bf16)] + [shape((rows, tile), bf16)] * chains,
-        (real, adversarial, fake, generated, piece, flat, *tail),
+        (fake, adversarial, real, generated, piece, flat, *tail),
         cost=cost,
     )
     kept = call(
@@ -459,9 +475,9 @@
     )
     totals, others = add_all(kept, send, n)
     factor = 1.0 / math.sqrt(tokens * n)
-    grads = gradient(own_rows, totals, 0, factor, cols)
+    grads = gradient(own_turned, totals, 0, factor, cols)
     for at, other in enumerate(others, chains):
-        grads = gradient(own_rows, [other], at, factor, cols, grads)
+        grads = gradient(own_turned, [other], at, factor, cols, grads)
     return (grads, drawn.T)
 
 

time: 62 us -> 61.7 us (level)
  starting transfers between devices: 34.4 us -> 30.1 us
  waiting for transfers between devices: 11.9 us -> 15.9 us
    ppermute x21 -> x22, starting transfers between devices: 34.4 us -> 30.1 us  [swap(): return lax.ppermute(value, axis, [(i, i ^ bit) for i in range(n)])]
    ppermute x21 -> x22, waiting for transfers between devices: 11.9 us -> 15.9 us  [swap(): return lax.ppermute(value, axis, [(i, i ^ bit) for i in range(n)])]
  transfers between devices with their start and end apart: 21 -> 22, of which waited for: 12 -> 14; matrix products, arithmetic and copies ran while one was open for 6% -> 6% of each run, Pallas kernels for 9% -> 9%
where the time goes in v4:
time: 61.7 us; the launch traced here: 61.5 us
  starting transfers between devices  30.1 us (49%)
  waiting for transfers between devices  15.9 us (26%)
  Pallas kernels  10.3 us (17%)
  other arithmetic  3 us (5%)
  matrix products  0.98 us (2%)
  between operations  0.87 us (1%)
    ppermute x22, starting transfers between devices, swap(): return lax.ppermute(value, axis, [(i, i ^ bit) for i in range(n)])  30.1 us
    ppermute x22, waiting for transfers between devices, swap(): return lax.ppermute(value, axis, [(i, i ^ bit) for i in range(n)])  15.9 us
    pallas_call x6, Pallas kernels, call(): pl.pallas_call(kernel, out_shape=out_shape, in_specs=[vmem] * len(inputs)...  4.87 us
    pallas_call x3, Pallas kernels, gradient(): pl.pallas_call(functools.partial(grad_kernel, factor=factor, first_piece=...  3.43 us
    pallas_call x1, Pallas kernels, part_of(): pl.pallas_call(part_kernel, out_shape=shapes, in_specs=[hbm, vmem, hbm],...  1.99 us
  transfers between devices with their start and end apart: 22, of which 14 were waited for; matrix products, arithmetic and copies ran while one was open for 6% of the time, Pallas kernels for 9%

profile of v4, /device:TPU:0, one launch (start us, length us, event | category | flops | bytes accessed | tf_op | source)
XLA Modules:
  0.0 61.5 jit_solution(4628594255933865859)
XLA Ops:
  1.4 2.0 %part.1 = (f32[72,384]{1,0:T(8,128)S(1)}, f32[72,384]{1,0:T(8,128)S(1)}, bf16[72,384]{1,0:T(8,128)(2,1)S(1)}, bf16[72,384]{1,0:T(8,128)(2,1)S(1)}, bf16[144,384]{1,0:T(8,128)(2,1)S(1)}) custom-call(bf16[64,3072]{1,0:T(8,128)(2,1)} %bitcast.22, f32[2,3072]{1,0:T(2,128)S(1)} %pad_maximum_fusion.vectors_ref, bf16[1,384,1536]{2,1,0:T(8,128)(2,1)} %block_ref.1), custom_call_target="tpu_custom_call" | custom-call | flops 169869312 | bytes 1179648 | tf_op jit(solution)/shard_map/part/pallas_call | solution.py:332
  3.5 3.0 %collective-permute-start = (bf16[72,384]{1,0:T(8,128)(2,1)S(1)}, bf16[72,384]{1,0:T(8,128)(2,1)S(1)}, u32[]{:S(2)}, u32[]{:S(2)}) collective-permute-start(bf16[72,384]{1,0:T(8,128)(2,1)S(1)} %get-tuple-element.27), channel_id=1, source_target_pairs={{0,1},{1,0},{2,3},{3,2},{4,5},{5,4},{6,7},{7,6},{8,9},{9,8},{10,11... | collective-permute-start | bytes 165896 | tf_op jit(solution)/shard_map/ppermute | solution.py:377
  6.6 1.0 %bitcast_convert_fusion = f32[64,3072]{1,0:T(8,128)S(1)} fusion(bf16[1,64,3072]{2,1,0:T(8,128)(2,1)} %param.11), kind=kLoop, calls=%fused_computation.30 | loop fusion | flops 196608 | bytes 1179648 | tf_op jit(solution)/shard_map/convert_element_type | solution.py:419
  7.7 0.9 %collective-permute-done = bf16[72,384]{1,0:T(8,128)(2,1)S(1)} collective-permute-done((bf16[72,384]{1,0:T(8,128)(2,1)S(1)}, bf16[72,384]{1,0:T(8,128)(2,1)S(1)}, u32[]{:S(2)}, u32[]{:S(2)}) %collective-permute-start) | collective-permute-done | bytes 55328 | tf_op jit(solution)/shard_map/ppermute | solution.py:377
  8.7 2.6 %collective-permute-start.1 = (bf16[72,384]{1,0:T(8,128)(2,1)S(1)}, bf16[72,384]{1,0:T(8,128)(2,1)S(1)}, u32[]{:S(2)}, u32[]{:S(2)}) collective-permute-start(bf16[72,384]{1,0:T(8,128)(2,1)S(1)} %fusion.6), channel_id=1, source_target_pairs={{0,2},{1,3},{2,0},{3,1},{4,6},{5,7},{6,4},{7,5},{8,10},{9,11},{10,... | collective-permute-start | bytes 165896 | tf_op jit(solution)/shard_map/ppermute | solution.py:377
  11.3 1.0 %collective-permute-start.4 = (bf16[72,384]{1,0:T(8,128)(2,1)S(1)}, bf16[72,384]{1,0:T(8,128)(2,1)S(1)}, u32[]{:S(2)}, u32[]{:S(2)}) collective-permute-start(bf16[72,384]{1,0:T(8,128)(2,1)S(1)} %fusion.7), channel_id=1, source_target_pairs={{0,2},{1,3},{2,0},{3,1},{4,6},{5,7},{6,4},{7,5},{8,10},{9,11},{10,... | collective-permute-start | bytes 165896 | tf_op jit(solution)/shard_map/ppermute | solution.py:377
  12.3 1.1 %collective-permute-done.1 = bf16[72,384]{1,0:T(8,128)(2,1)S(1)} collective-permute-done((bf16[72,384]{1,0:T(8,128)(2,1)S(1)}, bf16[72,384]{1,0:T(8,128)(2,1)S(1)}, u32[]{:S(2)}, u32[]{:S(2)}) %collective-permute-start.1) | collective-permute-done | bytes 55328 | tf_op jit(solution)/shard_map/ppermute | solution.py:377
  13.5 3.4 %collective-permute-start.2 = (bf16[72,384]{1,0:T(8,128)(2,1)S(1)}, bf16[72,384]{1,0:T(8,128)(2,1)S(1)}, u32[]{:S(2)}, u32[]{:S(2)}) collective-permute-start(bf16[72,384]{1,0:T(8,128)(2,1)S(1)} %fusion.10), channel_id=1, source_target_pairs={{0,4},{1,5},{2,6},{3,7},{4,0},{5,1},{6,2},{7,3},{8,12},{9,13},{10,... | collective-permute-start | bytes 165896 | tf_op jit(solution)/shard_map/ppermute | solution.py:377
  16.9 1.3 %collective-permute-start.5 = (bf16[72,384]{1,0:T(8,128)(2,1)S(1)}, bf16[72,384]{1,0:T(8,128)(2,1)S(1)}, u32[]{:S(2)}, u32[]{:S(2)}) collective-permute-start(bf16[72,384]{1,0:T(8,128)(2,1)S(1)} %fusion.11), channel_id=1, source_target_pairs={{0,4},{1,5},{2,6},{3,7},{4,0},{5,1},{6,2},{7,3},{8,12},{9,13},{10,... | collective-permute-start | bytes 165896 | tf_op jit(solution)/shard_map/ppermute | solution.py:377
  18.2 0.9 %collective-permute-done.2 = bf16[72,384]{1,0:T(8,128)(2,1)S(1)} collective-permute-done((bf16[72,384]{1,0:T(8,128)(2,1)S(1)}, bf16[72,384]{1,0:T(8,128)(2,1)S(1)}, u32[]{:S(2)}, u32[]{:S(2)}) %collective-permute-start.2) | collective-permute-done | bytes 55328 | tf_op jit(solution)/shard_map/ppermute | solution.py:377
  19.1 2.2 %collective-permute-start.6 = (bf16[72,384]{1,0:T(8,128)(2,1)S(1)}, bf16[72,384]{1,0:T(8,128)(2,1)S(1)}, u32[]{:S(2)}, u32[]{:S(2)}) collective-permute-start(bf16[72,384]{1,0:T(8,128)(2,1)S(1)} %add_convert_fusion.3.rest_0_), channel_id=1, source_target_pairs={{0,1},{1,0},{2,3},{3,2},{4,5},{5,4},{6,7},{7,6},{8,9},{9,8},{10,11... | collective-permute-start | bytes 165896 | tf_op jit(solution)/shard_map/ppermute | solution.py:377
  22.9 1.0 %fusion.gram_ref = f32[72,72]{1,0:T(8,128)S(1)} fusion(f32[3,3072]{1,0:T(4,128)S(1)} %broadcast_in_dim.15, f32[64,3072]{1,0:T(8,128)S(1)} %bitcast_convert_fusion, f32[72]{0:T(128)S(1)} %pad.6.clone), kind=kOutput, calls=%fused_computation | convolution fusion | flops 191545344 | bytes 844320 | tf_op jit(solution)/shard_map/dot_general | solution.py:421
  24.2 0.9 %generator_early.1.total_ref = f32[72,384]{1,0:T(8,128)S(1)} custom-call(bf16[64,384]{1,0:T(8,128)(2,1)S(1)} %bitcast.17, f32[72,72]{1,0:T(8,128)S(1)} %fusion.gram_ref, bf16[72,384]{1,0:T(8,128)(2,1)S(1)} %add_convert_fusion.3.rest_0_, bf16[72,384]{1,0:T(8,128)(2,1)S(1)} %add_convert_fusion.2.rest_1_, bf16[64,1536]{1,0:T(8,128)(2,1)S(1)} %bitcast.14), custom_call_target="tpu_custom_call" | custom-call | flops 84934656 | bytes 84934 | tf_op jit(solution)/shard_map/generator_early/pallas_call | solution.py:307
  25.0 1.3 %collective-permute-done.7.rest_1_.rest_3_ = bf16[72,384]{1,0:T(8,128)(2,1)S(1)} collective-permute-done((bf16[72,384]{1,0:T(8,128)(2,1)S(1)}, bf16[72,384]{1,0:T(8,128)(2,1)S(1)}, u32[]{:S(2)}, u32[]{:S(2)}) %collective-permute-start.7) | collective-permute-done | bytes 55328 | tf_op jit(solution)/shard_map/ppermute | solution.py:377
  27.9 1.4 %collective-permute-start.10 = (bf16[64,384]{1,0:T(8,128)(2,1)S(1)}, bf16[64,384]{1,0:T(8,128)(2,1)S(1)}, u32[]{:S(2)}, u32[]{:S(2)}) collective-permute-start(bf16[64,384]{1,0:T(8,128)(2,1)S(1)} %get-tuple-element.33.own_ref), channel_id=1, source_target_pairs={{0,8},{8,0},{16,24},{24,16},{1,9},{9,1},{17,25},{25,17},{2,10},{10... | collective-permute-start | bytes 147464 | tf_op jit(solution)/shard_map/ppermute | solution.py:377
  29.5 1.7 %slopes.1 = (bf16[384,256]{1,0:T(8,128)(2,1)S(1)}, bf16[1536,128]{1,0:T(8,128)(2,1)S(1)}, f32[1536,384]{1,0:T(8,128)S(1)}, bf16[144,384]{1,0:T(8,128)(2,1)S(1)}) custom-call(bf16[64,384]{1,0:T(8,128)(2,1)S(1)} %bitcast.19, f32[72,72]{1,0:T(8,128)S(1)} %get-tuple-element.30.gram_ref, bf16[144,384]{1,0:T(8,128)(2,1)S(1)} %get-tuple-element.31.own_ref, ...), custom_call_target="tpu_custom_call" | custom-call | flops 84934656 | bytes 84934 | tf_op jit(solution)/shard_map/slopes/pallas_call | solution.py:307
  32.0 3.2 %collective-permute-start.11 = (bf16[64,384]{1,0:T(8,128)(2,1)S(1)}, bf16[64,384]{1,0:T(8,128)(2,1)S(1)}, u32[]{:S(2)}, u32[]{:S(2)}) collective-permute-start(bf16[64,384]{1,0:T(8,128)(2,1)S(1)} %get-tuple-element.36.piece_ref), channel_id=1, source_target_pairs={{0,16},{8,24},{16,0},{24,8},{1,17},{9,25},{17,1},{25,9},{2,18},{10... | collective-permute-start | bytes 147464 | tf_op jit(solution)/shard_map/ppermute | solution.py:377
  36.6 0.9 %collective-permute-done.11.fake_ref = bf16[64,384]{1,0:T(8,128)(2,1)S(1)} collective-permute-done((bf16[64,384]{1,0:T(8,128)(2,1)S(1)}, bf16[64,384]{1,0:T(8,128)(2,1)S(1)}, u32[]{:S(2)}, u32[]{:S(2)}) %collective-permute-start.11) | collective-permute-done | bytes 49184 | tf_op jit(solution)/shard_map/ppermute | solution.py:377
  37.5 1.2 %collective-permute-done.12.adversarial_ref = bf16[64,384]{1,0:T(8,128)(2,1)S(1)} collective-permute-done((bf16[64,384]{1,0:T(8,128)(2,1)S(1)}, bf16[64,384]{1,0:T(8,128)(2,1)S(1)}, u32[]{:S(2)}, u32[]{:S(2)}) %collective-permute-start.12) | collective-permute-done | bytes 49184 | tf_op jit(solution)/shard_map/ppermute | solution.py:377
  40.3 1.3 %collective-permute-start.14 = (bf16[72,384]{1,0:T(8,128)(2,1)S(1)}, bf16[72,384]{1,0:T(8,128)(2,1)S(1)}, u32[]{:S(2)}, u32[]{:S(2)}) collective-permute-start(bf16[72,384]{1,0:T(8,128)(2,1)S(1)} %get-tuple-element.46), channel_id=1, source_target_pairs={{0,1},{1,0},{2,3},{3,2},{4,5},{5,4},{6,7},{7,6},{8,9},{9,8},{10,11... | collective-permute-start | bytes 165896 | tf_op jit(solution)/shard_map/ppermute | solution.py:377
  42.3 2.0 %collective-permute-done.18 = bf16[72,384]{1,0:T(8,128)(2,1)S(1)} collective-permute-done((bf16[72,384]{1,0:T(8,128)(2,1)S(1)}, bf16[72,384]{1,0:T(8,128)(2,1)S(1)}, u32[]{:S(2)}, u32[]{:S(2)}) %collective-permute-start.18) | collective-permute-done | bytes 55328 | tf_op jit(solution)/shard_map/ppermute | solution.py:377
  44.3 1.3 %collective-permute-start.19 = (bf16[72,384]{1,0:T(8,128)(2,1)S(1)}, bf16[72,384]{1,0:T(8,128)(2,1)S(1)}, u32[]{:S(2)}, u32[]{:S(2)}) collective-permute-start(bf16[72,384]{1,0:T(8,128)(2,1)S(1)} %fusion.9), channel_id=1, source_target_pairs={{0,2},{1,3},{2,0},{3,1},{4,6},{5,7},{6,4},{7,5},{8,10},{9,11},{10,... | collective-permute-start | bytes 165896 | tf_op jit(solution)/shard_map/ppermute | solution.py:377
  45.6 0.9 %collective-permute-start.15 = (bf16[72,384]{1,0:T(8,128)(2,1)S(1)}, bf16[72,384]{1,0:T(8,128)(2,1)S(1)}, u32[]{:S(2)}, u32[]{:S(2)}) collective-permute-start(bf16[72,384]{1,0:T(8,128)(2,1)S(1)} %fusion.8), channel_id=1, source_target_pairs={{0,2},{1,3},{2,0},{3,1},{4,6},{5,7},{6,4},{7,5},{8,10},{9,11},{10,... | collective-permute-start | bytes 165896 | tf_op jit(solution)/shard_map/ppermute | solution.py:377
  46.6 2.4 %collective-permute-done.19 = bf16[72,384]{1,0:T(8,128)(2,1)S(1)} collective-permute-done((bf16[72,384]{1,0:T(8,128)(2,1)S(1)}, bf16[72,384]{1,0:T(8,128)(2,1)S(1)}, u32[]{:S(2)}, u32[]{:S(2)}) %collective-permute-start.19) | collective-permute-done | bytes 55328 | tf_op jit(solution)/shard_map/ppermute | solution.py:377
  49.0 1.5 %collective-permute-start.20 = (bf16[72,384]{1,0:T(8,128)(2,1)S(1)}, bf16[72,384]{1,0:T(8,128)(2,1)S(1)}, u32[]{:S(2)}, u32[]{:S(2)}) collective-permute-start(bf16[72,384]{1,0:T(8,128)(2,1)S(1)} %fusion.13), channel_id=1, source_target_pairs={{0,4},{1,5},{2,6},{3,7},{4,0},{5,1},{6,2},{7,3},{8,12},{9,13},{10,... | collective-permute-start | bytes 165896 | tf_op jit(solution)/shard_map/ppermute | solution.py:377
  50.5 1.6 %collective-permute-start.16 = (bf16[72,384]{1,0:T(8,128)(2,1)S(1)}, bf16[72,384]{1,0:T(8,128)(2,1)S(1)}, u32[]{:S(2)}, u32[]{:S(2)}) collective-permute-start(bf16[72,384]{1,0:T(8,128)(2,1)S(1)} %fusion.12), channel_id=1, source_target_pairs={{0,4},{1,5},{2,6},{3,7},{4,0},{5,1},{6,2},{7,3},{8,12},{9,13},{10,... | collective-permute-start | bytes 165896 | tf_op jit(solution)/shard_map/ppermute | solution.py:377
  52.1 2.9 %collective-permute-done.20 = bf16[72,384]{1,0:T(8,128)(2,1)S(1)} collective-permute-done((bf16[72,384]{1,0:T(8,128)(2,1)S(1)}, bf16[72,384]{1,0:T(8,128)(2,1)S(1)}, u32[]{:S(2)}, u32[]{:S(2)}) %collective-permute-start.20) | collective-permute-done | bytes 55328 | tf_op jit(solution)/shard_map/ppermute | solution.py:377
  55.0 1.1 %collective-permute-start.21 = (bf16[72,384]{1,0:T(8,128)(2,1)S(1)}, bf16[72,384]{1,0:T(8,128)(2,1)S(1)}, u32[]{:S(2)}, u32[]{:S(2)}) collective-permute-start(bf16[72,384]{1,0:T(8,128)(2,1)S(1)} %add_convert_fusion.rest_0_), channel_id=1, source_target_pairs={{0,1},{1,0},{2,3},{3,2},{4,5},{5,4},{6,7},{7,6},{8,9},{9,8},{10,11... | collective-permute-start | bytes 165896 | tf_op jit(solution)/shard_map/ppermute | solution.py:377
  56.2 1.0 %collective-permute-start.17 = (bf16[72,384]{1,0:T(8,128)(2,1)S(1)}, bf16[72,384]{1,0:T(8,128)(2,1)S(1)}, u32[]{:S(2)}, u32[]{:S(2)}) collective-permute-start(bf16[72,384]{1,0:T(8,128)(2,1)S(1)} %add_convert_fusion.1.rest_1_), channel_id=1, source_target_pairs={{0,1},{1,0},{2,3},{3,2},{4,5},{5,4},{6,7},{7,6},{8,9},{9,8},{10,11... | collective-permute-start | bytes 165896 | tf_op jit(solution)/shard_map/ppermute | solution.py:377
  57.2 1.3 %gradient.3.rest_1_ = f32[1,384,1536]{2,1,0:T(8,128)} custom-call(bf16[384,256]{1,0:T(8,128)(2,1)S(1)} %get-tuple-element.32.own_ref, bf16[72,384]{1,0:T(8,128)(2,1)S(1)} %add_convert_fusion.rest_0_, bf16[72,384]{1,0:T(8,128)(2,1)S(1)} %add_convert_fusion.1.rest_1_), custom_call_target="tpu_custom_call" | custom-call | flops 150994944 | bytes 1179648 | tf_op jit(solution)/shard_map/gradient/pallas_call | solution.py:359
  59.2 1.1 %gradient.4.rest_1_ = f32[1,384,1536]{2,1,0:T(8,128)} custom-call(bf16[384,256]{1,0:T(8,128)(2,1)S(1)} %get-tuple-element.32.own_ref, bf16[72,384]{1,0:T(8,128)(2,1)S(1)} %collective-permute-done.21.rest_0_, f32[1,384,1536]{2,1,0:T(8,128)} %gradient.3.rest_1_), custom_call_target="tpu_custom_call", output_to_operand_aliasing={{}: (2, {})} | custom-call | flops 75497472 | bytes 589824 | tf_op jit(solution)/shard_map/gradient/pallas_call | solution.py:359
  60.4 1.1 %gradient.5 = f32[1,384,1536]{2,1,0:T(8,128)} custom-call(bf16[384,256]{1,0:T(8,128)(2,1)S(1)} %get-tuple-element.32.own_ref, bf16[72,384]{1,0:T(8,128)(2,1)S(1)} %collective-permute-done.17.rest_0_, f32[1,384,1536]{2,1,0:T(8,128)} %gradient.4.rest_1_), custom_call_target="tpu_custom_call", output_to_operand_aliasing={{}: (2, {})} | custom-call | flops 75497472 | bytes 589824 | tf_op jit(solution)/shard_map/gradient/pallas_call | solution.py:359
  (54 shorter events, 10.1 us)
Async XLA Ops:
  0.6 22.3 %copy-start.3 = (f32[1,3072]{1,0:T(1,128)S(1)}, f32[1,3072]{1,0:T(1,128)}, u32[]{:S(2)}) copy-start(f32[1,3072]{1,0:T(1,128)} %param.12) | copy-start | bytes 36868
  3.4 20.5 %copy-start.4 = (f32[384]{0:T(512)S(1)}, f32[384]{0:T(512)}, u32[]{:S(2)}) copy-start(f32[384]{0:T(512)} %param.10) | copy-start | bytes 4612
  3.5 20.5 %copy-start = (bf16[1,1536,64]{1,2,0:T(8,128)(2,1)S(1)}, bf16[1,1536,64]{1,2,0:T(8,128)(2,1)}, u32[]{:S(2)}) copy-start(bf16[1,1536,64]{1,2,0:T(8,128)(2,1)} %param.15) | copy-start | bytes 589828
  3.5 20.7 %copy-start.1 = (bf16[384,64]{0,1:T(8,128)(2,1)S(1)}, bf16[384,64]{0,1:T(8,128)(2,1)}, u32[]{:S(2)}) copy-start(bf16[384,64]{0,1:T(8,128)(2,1)} %param.8) | copy-start | bytes 147460
  3.5 5.2 %collective-permute-start = (bf16[72,384]{1,0:T(8,128)(2,1)S(1)}, bf16[72,384]{1,0:T(8,128)(2,1)S(1)}, u32[]{:S(2)}, u32[]{:S(2)}) collective-permute-start(bf16[72,384]{1,0:T(8,128)(2,1)S(1)} %get-tuple-element.27), channel_id=1, source_target_pairs={{0,1},{1,0},{2,3},{3,2},{4,5},{5,4},{6,7},{7,6},{8,9},{9,8},{10,11... | collective-permute-start | bytes 165896 | tf_op jit(solution)/shard_map/ppermute | solution.py:377
  6.5 19.8 %copy-start.2 = (bf16[384,64]{0,1:T(8,128)(2,1)S(1)}, bf16[384,64]{0,1:T(8,128)(2,1)}, u32[]{:S(2)}) copy-start(bf16[384,64]{0,1:T(8,128)(2,1)} %param.9) | copy-start | bytes 147460
  6.5 4.8 %collective-permute-start.3 = (bf16[72,384]{1,0:T(8,128)(2,1)S(1)}, bf16[72,384]{1,0:T(8,128)(2,1)S(1)}, u32[]{:S(2)}, u32[]{:S(2)}) collective-permute-start(bf16[72,384]{1,0:T(8,128)(2,1)S(1)} %get-tuple-element.29), channel_id=1, source_target_pairs={{0,1},{1,0},{2,3},{3,2},{4,5},{5,4},{6,7},{7,6},{8,9},{9,8},{10,11... | collective-permute-start | bytes 165896 | tf_op jit(solution)/shard_map/ppermute | solution.py:377
  8.7 4.8 %collective-permute-start.1 = (bf16[72,384]{1,0:T(8,128)(2,1)S(1)}, bf16[72,384]{1,0:T(8,128)(2,1)S(1)}, u32[]{:S(2)}, u32[]{:S(2)}) collective-permute-start(bf16[72,384]{1,0:T(8,128)(2,1)S(1)} %fusion.6), channel_id=1, source_target_pairs={{0,2},{1,3},{2,0},{3,1},{4,6},{5,7},{6,4},{7,5},{8,10},{9,11},{10,... | collective-permute-start | bytes 165896 | tf_op jit(solution)/shard_map/ppermute | solution.py:377
  11.3 5.6 %collective-permute-start.4 = (bf16[72,384]{1,0:T(8,128)(2,1)S(1)}, bf16[72,384]{1,0:T(8,128)(2,1)S(1)}, u32[]{:S(2)}, u32[]{:S(2)}) collective-permute-start(bf16[72,384]{1,0:T(8,128)(2,1)S(1)} %fusion.7), channel_id=1, source_target_pairs={{0,2},{1,3},{2,0},{3,1},{4,6},{5,7},{6,4},{7,5},{8,10},{9,11},{10,... | collective-permute-start | bytes 165896 | tf_op jit(solution)/shard_map/ppermute | solution.py:377
  13.5 5.6 %collective-permute-start.2 = (bf16[72,384]{1,0:T(8,128)(2,1)S(1)}, bf16[72,384]{1,0:T(8,128)(2,1)S(1)}, u32[]{:S(2)}, u32[]{:S(2)}) collective-permute-start(bf16[72,384]{1,0:T(8,128)(2,1)S(1)} %fusion.10), channel_id=1, source_target_pairs={{0,4},{1,5},{2,6},{3,7},{4,0},{5,1},{6,2},{7,3},{8,12},{9,13},{10,... | collective-permute-start | bytes 165896 | tf_op jit(solution)/shard_map/ppermute | solution.py:377
  16.9 5.1 %collective-permute-start.5 = (bf16[72,384]{1,0:T(8,128)(2,1)S(1)}, bf16[72,384]{1,0:T(8,128)(2,1)S(1)}, u32[]{:S(2)}, u32[]{:S(2)}) collective-permute-start(bf16[72,384]{1,0:T(8,128)(2,1)S(1)} %fusion.11), channel_id=1, source_target_pairs={{0,4},{1,5},{2,6},{3,7},{4,0},{5,1},{6,2},{7,3},{8,12},{9,13},{10,... | collective-permute-start | bytes 165896 | tf_op jit(solution)/shard_map/ppermute | solution.py:377
  19.1 5.9 %collective-permute-start.6 = (bf16[72,384]{1,0:T(8,128)(2,1)S(1)}, bf16[72,384]{1,0:T(8,128)(2,1)S(1)}, u32[]{:S(2)}, u32[]{:S(2)}) collective-permute-start(bf16[72,384]{1,0:T(8,128)(2,1)S(1)} %add_convert_fusion.3.rest_0_), channel_id=1, source_target_pairs={{0,1},{1,0},{2,3},{3,2},{4,5},{5,4},{6,7},{7,6},{8,9},{9,8},{10,11... | collective-permute-start | bytes 165896 | tf_op jit(solution)/shard_map/ppermute | solution.py:377
  22.1 4.2 %collective-permute-start.7 = (bf16[72,384]{1,0:T(8,128)(2,1)S(1)}, bf16[72,384]{1,0:T(8,128)(2,1)S(1)}, u32[]{:S(2)}, u32[]{:S(2)}) collective-permute-start(bf16[72,384]{1,0:T(8,128)(2,1)S(1)} %add_convert_fusion.2.rest_1_), channel_id=1, source_target_pairs={{0,1},{1,0},{2,3},{3,2},{4,5},{5,4},{6,7},{7,6},{8,9},{9,8},{10,11... | collective-permute-start | bytes 165896 | tf_op jit(solution)/shard_map/ppermute | solution.py:377
  27.1 4.5 %collective-permute-start.8 = (bf16[64,384]{1,0:T(8,128)(2,1)S(1)}, bf16[64,384]{1,0:T(8,128)(2,1)S(1)}, u32[]{:S(2)}, u32[]{:S(2)}) collective-permute-start(bf16[64,384]{1,0:T(8,128)(2,1)S(1)} %get-tuple-element.33.own_ref), channel_id=1, source_target_pairs={{0,16},{8,24},{16,0},{24,8},{1,17},{9,25},{17,1},{25,9},{2,18},{10... | collective-permute-start | bytes 147464 | tf_op jit(solution)/shard_map/ppermute | solution.py:377
  27.9 4.0 %collective-permute-start.9 = (bf16[64,384]{1,0:T(8,128)(2,1)S(1)}, bf16[64,384]{1,0:T(8,128)(2,1)S(1)}, u32[]{:S(2)}, u32[]{:S(2)}) collective-permute-start(bf16[64,384]{1,0:T(8,128)(2,1)S(1)} %get-tuple-element.33.own_ref), channel_id=1, source_target_pairs={{0,24},{8,16},{16,8},{24,0},{1,25},{9,17},{17,9},{25,1},{2,26},{10... | collective-permute-start | bytes 147464 | tf_op jit(solution)/shard_map/ppermute | solution.py:377
  27.9 4.0 %collective-permute-start.10 = (bf16[64,384]{1,0:T(8,128)(2,1)S(1)}, bf16[64,384]{1,0:T(8,128)(2,1)S(1)}, u32[]{:S(2)}, u32[]{:S(2)}) collective-permute-start(bf16[64,384]{1,0:T(8,128)(2,1)S(1)} %get-tuple-element.33.own_ref), channel_id=1, source_target_pairs={{0,8},{8,0},{16,24},{24,16},{1,9},{9,1},{17,25},{25,17},{2,10},{10... | collective-permute-start | bytes 147464 | tf_op jit(solution)/shard_map/ppermute | solution.py:377
  32.0 5.5 %collective-permute-start.11 = (bf16[64,384]{1,0:T(8,128)(2,1)S(1)}, bf16[64,384]{1,0:T(8,128)(2,1)S(1)}, u32[]{:S(2)}, u32[]{:S(2)}) collective-permute-start(bf16[64,384]{1,0:T(8,128)(2,1)S(1)} %get-tuple-element.36.piece_ref), channel_id=1, source_target_pairs={{0,16},{8,24},{16,0},{24,8},{1,17},{9,25},{17,1},{25,9},{2,18},{10... | collective-permute-start | bytes 147464 | tf_op jit(solution)/shard_map/ppermute | solution.py:377
  35.2 3.5 %collective-permute-start.12 = (bf16[64,384]{1,0:T(8,128)(2,1)S(1)}, bf16[64,384]{1,0:T(8,128)(2,1)S(1)}, u32[]{:S(2)}, u32[]{:S(2)}) collective-permute-start(bf16[64,384]{1,0:T(8,128)(2,1)S(1)} %get-tuple-element.36.piece_ref), channel_id=1, source_target_pairs={{0,24},{8,16},{16,8},{24,0},{1,25},{9,17},{17,9},{25,1},{2,26},{10... | collective-permute-start | bytes 147464 | tf_op jit(solution)/shard_map/ppermute | solution.py:377
  35.9 2.8 %collective-permute-start.13 = (bf16[64,384]{1,0:T(8,128)(2,1)S(1)}, bf16[64,384]{1,0:T(8,128)(2,1)S(1)}, u32[]{:S(2)}, u32[]{:S(2)}) collective-permute-start(bf16[64,384]{1,0:T(8,128)(2,1)S(1)} %get-tuple-element.36.piece_ref), channel_id=1, source_target_pairs={{0,8},{8,0},{16,24},{24,16},{1,9},{9,1},{17,25},{25,17},{2,10},{10... | collective-permute-start | bytes 147464 | tf_op jit(solution)/shard_map/ppermute | solution.py:377
  39.5 4.8 %collective-permute-start.18 = (bf16[72,384]{1,0:T(8,128)(2,1)S(1)}, bf16[72,384]{1,0:T(8,128)(2,1)S(1)}, u32[]{:S(2)}, u32[]{:S(2)}) collective-permute-start(bf16[72,384]{1,0:T(8,128)(2,1)S(1)} %get-tuple-element.48), channel_id=1, source_target_pairs={{0,1},{1,0},{2,3},{3,2},{4,5},{5,4},{6,7},{7,6},{8,9},{9,8},{10,11... | collective-permute-start | bytes 165896 | tf_op jit(solution)/shard_map/ppermute | solution.py:377
  40.3 5.3 %collective-permute-start.14 = (bf16[72,384]{1,0:T(8,128)(2,1)S(1)}, bf16[72,384]{1,0:T(8,128)(2,1)S(1)}, u32[]{:S(2)}, u32[]{:S(2)}) collective-permute-start(bf16[72,384]{1,0:T(8,128)(2,1)S(1)} %get-tuple-element.46), channel_id=1, source_target_pairs={{0,1},{1,0},{2,3},{3,2},{4,5},{5,4},{6,7},{7,6},{8,9},{9,8},{10,11... | collective-permute-start | bytes 165896 | tf_op jit(solution)/shard_map/ppermute | solution.py:377
  44.3 4.7 %collective-permute-start.19 = (bf16[72,384]{1,0:T(8,128)(2,1)S(1)}, bf16[72,384]{1,0:T(8,128)(2,1)S(1)}, u32[]{:S(2)}, u32[]{:S(2)}) collective-permute-start(bf16[72,384]{1,0:T(8,128)(2,1)S(1)} %fusion.9), channel_id=1, source_target_pairs={{0,2},{1,3},{2,0},{3,1},{4,6},{5,7},{6,4},{7,5},{8,10},{9,11},{10,... | collective-permute-start | bytes 165896 | tf_op jit(solution)/shard_map/ppermute | solution.py:377
  45.6 4.9 %collective-permute-start.15 = (bf16[72,384]{1,0:T(8,128)(2,1)S(1)}, bf16[72,384]{1,0:T(8,128)(2,1)S(1)}, u32[]{:S(2)}, u32[]{:S(2)}) collective-permute-start(bf16[72,384]{1,0:T(8,128)(2,1)S(1)} %fusion.8), channel_id=1, source_target_pairs={{0,2},{1,3},{2,0},{3,1},{4,6},{5,7},{6,4},{7,5},{8,10},{9,11},{10,... | collective-permute-start | bytes 165896 | tf_op jit(solution)/shard_map/ppermute | solution.py:377
  49.0 6.0 %collective-permute-start.20 = (bf16[72,384]{1,0:T(8,128)(2,1)S(1)}, bf16[72,384]{1,0:T(8,128)(2,1)S(1)}, u32[]{:S(2)}, u32[]{:S(2)}) collective-permute-start(bf16[72,384]{1,0:T(8,128)(2,1)S(1)} %fusion.13), channel_id=1, source_target_pairs={{0,4},{1,5},{2,6},{3,7},{4,0},{5,1},{6,2},{7,3},{8,12},{9,13},{10,... | collective-permute-start | bytes 165896 | tf_op jit(solution)/shard_map/ppermute | solution.py:377
  50.5 5.6 %collective-permute-start.16 = (bf16[72,384]{1,0:T(8,128)(2,1)S(1)}, bf16[72,384]{1,0:T(8,128)(2,1)S(1)}, u32[]{:S(2)}, u32[]{:S(2)}) collective-permute-start(bf16[72,384]{1,0:T(8,128)(2,1)S(1)} %fusion.12), channel_id=1, source_target_pairs={{0,4},{1,5},{2,6},{3,7},{4,0},{5,1},{6,2},{7,3},{8,12},{9,13},{10,... | collective-permute-start | bytes 165896 | tf_op jit(solution)/shard_map/ppermute | solution.py:377
  55.0 4.2 %collective-permute-start.21 = (bf16[72,384]{1,0:T(8,128)(2,1)S(1)}, bf16[72,384]{1,0:T(8,128)(2,1)S(1)}, u32[]{:S(2)}, u32[]{:S(2)}) collective-permute-start(bf16[72,384]{1,0:T(8,128)(2,1)S(1)} %add_convert_fusion.rest_0_), channel_id=1, source_target_pairs={{0,1},{1,0},{2,3},{3,2},{4,5},{5,4},{6,7},{7,6},{8,9},{9,8},{10,11... | collective-permute-start | bytes 165896 | tf_op jit(solution)/shard_map/ppermute | solution.py:377
  56.2 4.2 %collective-permute-start.17 = (bf16[72,384]{1,0:T(8,128)(2,1)S(1)}, bf16[72,384]{1,0:T(8,128)(2,1)S(1)}, u32[]{:S(2)}, u32[]{:S(2)}) collective-permute-start(bf16[72,384]{1,0:T(8,128)(2,1)S(1)} %add_convert_fusion.1.rest_1_), channel_id=1, source_target_pairs={{0,1},{1,0},{2,3},{3,2},{4,5},{5,4},{6,7},{7,6},{8,9},{9,8},{10,11... | collective-permute-start | bytes 165896 | tf_op jit(solution)/shard_map/ppermute | solution.py:377

commit v5 on v4

--- a/solution.py
+++ b/solution.py
@@ -103,27 +103,16 @@
         outs[at][...] = (part[:rows] + part[rows:]).astype(outs[at].dtype)
 
 
-def network(wide16, scale, proj_refs, first_piece, readout_ref):
+def network(wide16, scale, proj_refs, first_piece, readout_ref, slope_ref=None):
     tile = proj_refs[0].shape[1]
     total = jnp.zeros((readout_ref.shape[0], wide16.shape[1]), f32)
     for at, proj_ref in enumerate(proj_refs, first_piece):
         hidden = scale * mm(proj_ref[...], wide16, 0, 0)
-        gate, unused = gelu_gate(hidden)
-        activated = (hidden * gate).astype(bf16)
-        total = total + mm(readout_ref[:, columns_of(at, tile)], activated, 1, 0)
-    return total
-
-
-def network_by_rows(wide, scale, turned_ref, tile, readout_ref, slope_ref):
-    total = jnp.zeros((readout_ref.shape[0], wide.shape[1]), f32)
-    wide16 = lanes_of_zeros(wide).astype(bf16)
-    for at in range(2 * chains):
-        rows = slice(at * tile, (at + 1) * tile)
-        hidden = scale * mm(turned_ref[rows, :], wide16, 1, 0)
         gate, square = gelu_gate(hidden)
         activated = (hidden * gate).astype(bf16)
         total = total + mm(readout_ref[:, columns_of(at, tile)], activated, 1, 0)
-        slope_ref[rows, :] = gelu_slope(hidden, square, gate)
+        if slope_ref is not None:
+            slope_ref[at * tile : (at + 1) * tile, :] = gelu_slope(hidden, square, gate)
     return total
 
 
@@ -159,34 +148,24 @@
         out_ref[...] = (total_ref[:channels, :] + total).astype(bf16)
 
 
-def in_parts(scale, wide):
-    scaled = scale * wide
-    return jnp.concatenate([scaled, scaled - scaled.astype(bf16).astype(f32)], axis=0).astype(bf16)
-
-
-def slope_kernel(latent_ref, gram_ref, own_ref, *rest, width):
-    *proj_refs, own_turned_ref, turned_ref, slope_ref, scaled_ref = rest
+def slope_kernel(latent_ref, scaled_in_ref, gram_ref, own_ref, *rest, width):
+    *proj_refs, own_turned_ref, slope_ref, scaled_ref = rest
     own_turned_ref[...] = lanes_of_zeros(own_ref[...].astype(f32), 256).T.astype(bf16)
-    tile = proj_refs[0].shape[1]
+    rows, tile = proj_refs[0].shape
+    wide = widen(latent_ref[...], jnp.ones((1, latent_ref.shape[1]), f32))
+    scale, unused = norm_scale(wide, gram_ref[...], width)
+    scaled = jnp.where(lax.axis_index("role") == 0, scale * wide, scaled_in_ref[...])
+    high, low = halves(scaled)
+    scaled_ref[...] = jnp.concatenate([scaled, scaled - high.astype(f32)], axis=0).astype(bf16)
     for at, proj_ref in enumerate(proj_refs):
-        turned = lanes_of_zeros(proj_ref[...].astype(f32)).T
-        turned_ref[at * tile : (at + 1) * tile, :] = turned.astype(bf16)
-
-    @pl.when(lax.axis_index("role") == 0)
-    def _():
-        wide = widen(latent_ref[...], jnp.ones((1, latent_ref.shape[1]), f32))
-        scale, unused = norm_scale(wide, gram_ref[...], width)
-        wide16 = lanes_of_zeros(wide).astype(bf16)
-        for at in range(2 * chains):
-            hidden = scale * mm(turned_ref[at * tile : (at + 1) * tile, :], wide16, 1, 0)
-            gate, square = gelu_gate(hidden)
-            slope_ref[at * tile : (at + 1) * tile, :] = gelu_slope(hidden, square, gate)
-        scaled_ref[...] = in_parts(scale, wide)
-
-
-def second_kernel(own_ref, by2_ref, by3_ref, by1_ref, mix_ref, gram_ref, *rest, width):
+        hidden = mm(proj_ref[...], high, 0, 0) + mm(proj_ref[...], low, 0, 0)
+        gate, square = gelu_gate(hidden)
+        slope_ref[at * tile : (at + 1) * tile, :] = gelu_slope(hidden, square, gate)
+
+
+def second_kernel(own_ref, by1_ref, by3_ref, by2_ref, mix_ref, gram_ref, *rest, width):
     proj_refs = rest[: 2 * chains]
-    turned_ref, readout_ref, columns_ref, generated_ref, piece_ref, flat_ref, slope_ref, scaled_ref = rest[2 * chains :]
+    readout_ref, columns_ref, generated_ref, piece_ref, flat_ref, scaled_ref, slope_ref = rest[2 * chains :]
     role = lax.axis_index("role")
     channels, tokens = own_ref.shape
     tile = proj_refs[0].shape[1]
@@ -195,65 +174,63 @@
     generated = jnp.where(role < 2, low, high)
     generated_ref[...] = generated.astype(bf16)
 
-    @pl.when(role > 0)
-    def _():
+    def score(slope_ref):
         level = mix_ref[channels : channels + 1, :]
         noised = (1.0 - level) * generated + mix_ref[:channels, :]
         wide = widen(noised.astype(bf16), level)
         scale, seen = norm_scale(wide, gram_ref[...], width)
-        scores = network_by_rows(wide, scale, turned_ref, tile, readout_ref, slope_ref).astype(bf16)
-        piece_ref[...] = scores
+        scaled_ref[...] = scale * wide
+        scores = network(wide.astype(bf16), scale, proj_refs, 0, readout_ref, slope_ref).astype(bf16)
+        return level, wide, scale, seen, scores
+
+    @pl.when((role == 1) | (role == 2))
+    def _():
+        piece_ref[...] = score(None)[4]
+
+    @pl.when(role == 3)
+    def _():
+        level, wide, scale, seen, scores = score(slope_ref)
         logit = jnp.sum(scores.astype(f32), axis=0, keepdims=True)
         flat_ref[...] = 1.0 / (1.0 + jnp.exp(-logit))
-        scaled_ref[...] = in_parts(scale, wide)
-
-        @pl.when(role == 3)
-        def _():
-            high, low = halves(-1.0 / (1.0 + jnp.exp(logit)))
-            cot = jnp.concatenate(
-                [
-                    jnp.broadcast_to(high, (channels, tokens)),
-                    jnp.broadcast_to(low, (channels, tokens)),
-                ],
-                axis=0,
-            )
-            back_rows = jnp.zeros(wide.shape, f32)
-            for at, proj_ref in enumerate(proj_refs):
-                back = mm(columns_ref[columns_of(at, tile), :], cot, 1, 0)
-                hcot = (back * slope_ref[at * tile : (at + 1) * tile, :]).astype(bf16)
-                back_rows = back_rows + mm(proj_ref[...], hcot, 1, 0)
-            inner = scale * jnp.sum(back_rows * wide, axis=0, keepdims=True)
-            latent_back = scale * back_rows[:channels] - (scale * scale * inner * (1.0 / width)) * seen[:channels]
-            piece_ref[...] = (adv_weight * (1.0 - level) * latent_back).astype(bf16)
-
-
-def pull_back(cot, tail, out_refs, first_piece):
-    first = lax.axis_index("role") == 0
-    rows, tile = out_refs[0].shape
-    columns_ref = tail[4]
-
-    def with_slopes(slope_ref, scaled_ref):
-        scaled = scaled_ref[...]
-        for at, out_ref in enumerate(out_refs, first_piece):
+        high, low = halves(-1.0 / (1.0 + jnp.exp(logit)))
+        cot = jnp.concatenate(
+            [
+                jnp.broadcast_to(high, (channels, tokens)),
+                jnp.broadcast_to(low, (channels, tokens)),
+            ],
+            axis=0,
+        )
+        back_rows = jnp.zeros(wide.shape, f32)
+        for at, proj_ref in enumerate(proj_refs):
             back = mm(columns_ref[columns_of(at, tile), :], cot, 1, 0)
             hcot = (back * slope_ref[at * tile : (at + 1) * tile, :]).astype(bf16)
-            part = mm(scaled, hcot, 1, 1)
-            out_ref[...] = (part[:rows] + part[rows:]).astype(out_ref.dtype)
-
-    pl.when(first)(lambda: with_slopes(*tail[0:2]))
-    pl.when(jnp.logical_not(first))(lambda: with_slopes(*tail[2:4]))
+            back_rows = back_rows + mm(proj_ref[...], hcot, 1, 0)
+        inner = scale * jnp.sum(back_rows * wide, axis=0, keepdims=True)
+        latent_back = scale * back_rows[:channels] - (scale * scale * inner * (1.0 / width)) * seen[:channels]
+        piece_ref[...] = (adv_weight * (1.0 - level) * latent_back).astype(bf16)
+
+
+def pull_back(cot, tail, out_refs, first_piece):
+    slope_ref, scaled_ref, columns_ref = tail
+    rows, tile = out_refs[0].shape
+    scaled = scaled_ref[...]
+    for at, out_ref in enumerate(out_refs, first_piece):
+        back = mm(columns_ref[columns_of(at, tile), :], cot, 1, 0)
+        hcot = (back * slope_ref[at * tile : (at + 1) * tile, :]).astype(bf16)
+        part = mm(scaled, hcot, 1, 1)
+        out_ref[...] = (part[:rows] + part[rows:]).astype(out_ref.dtype)
 
 
 def send_kernel(
+    real_ref,
+    adversarial_ref,
     fake_ref,
-    adversarial_ref,
-    real_ref,
     generated_ref,
     piece_ref,
     flat_ref,
     *rest,
 ):
-    tail, cot_ref, out_refs = rest[:5], rest[5], rest[6:]
+    tail, cot_ref, out_refs = rest[:3], rest[3], rest[4:]
     role = lax.axis_index("role")
     first = role == 0
     generated = generated_ref[...].astype(f32)
@@ -279,7 +256,7 @@
 
 
 def keep_kernel(cot_ref, *rest):
-    pull_back(cot_ref[...], rest[:5], rest[5:], 0)
+    pull_back(cot_ref[...], rest[:3], rest[3:], 0)
 
 
 def grad_kernel(own_ref, *rest, factor, first_piece, count):
@@ -440,34 +417,29 @@
     )
     by2, by3, by1 = (swap(own_first, "role", roles, bit) for bit in (2, 3, 1))
     drawn = jnp.where(role == 0, own_first, jnp.where(role == 1, by1, jnp.where(role == 2, by2, by3)))
-    slope_shapes = [shape((cols, tokens), f32), shape((2 * rows, tokens), bf16)]
-    own_turned, turned, *first_slopes = call(
+    generated, piece, flat, scaled = call(
+        functools.partial(second_kernel, width=width),
+        "score",
+        [latent_shape, latent_shape, shape((1, tokens), f32), shape((rows, tokens), f32)],
+        (own_first, by1, by3, by2, mix, gram, *proj, readout, columns),
+        scratch=[pltpu.VMEM((cols, tokens), f32)],
+    )
+    fake, adversarial, real = (swap(piece, "role", roles, bit) for bit in (2, 3, 1))
+    own_turned, slope, scaled = call(
         functools.partial(slope_kernel, width=width),
         "slopes",
-        [shape((depth, 256), bf16), shape((cols, 128), bf16), *slope_shapes],
-        (source, gram, own_rows, *proj),
+        [shape((depth, 256), bf16), shape((cols, tokens), f32), shape((2 * rows, tokens), bf16)],
+        (source, scaled, gram, own_rows, *proj),
         cost=cost,
     )
-    generated, piece, flat, *slopes = call(
-        functools.partial(second_kernel, width=width),
-        "score",
-        [
-            latent_shape,
-            latent_shape,
-            shape((1, tokens), f32),
-            *slope_shapes,
-        ],
-        (own_first, by2, by3, by1, mix, gram, *proj, turned, readout, columns),
-    )
-    fake, adversarial, real = (swap(piece, "role", roles, bit) for bit in (2, 3, 1))
     flat, drawn = lax.optimization_barrier((flat, drawn))
 
-    tail = (*first_slopes, *slopes, columns)
+    tail = (slope, scaled, columns)
     cot, *send = call(
         send_kernel,
         "cotangent_send",
         [shape((2 * channels, tokens), bf16)] + [shape((rows, tile), bf16)] * chains,
-        (fake, adversarial, real, generated, piece, flat, *tail),
+        (real, adversarial, fake, generated, piece, flat, *tail),
         cost=cost,
     )
     kept = call(

time: 61.7 us -> 61.1 us (level)
  transfers between devices with their start and end apart: 22 -> 22, of which waited for: 14 -> 13; matrix products, arithmetic and copies ran while one was open for 6% -> 6% of each run, Pallas kernels for 9% -> 9%
where the time goes in v5:
time: 61.1 us; the launch traced here: 60.9 us
  starting transfers between devices  29.5 us (48%)
  waiting for transfers between devices  16 us (26%)
  Pallas kernels  10.2 us (17%)
  other arithmetic  3 us (5%)
  matrix products  0.98 us (2%)
  between operations  0.88 us (1%)
    ppermute x22, starting transfers between devices, swap(): return lax.ppermute(value, axis, [(i, i ^ bit) for i in range(n)])  29.5 us
    ppermute x22, waiting for transfers between devices, swap(): return lax.ppermute(value, axis, [(i, i ^ bit) for i in range(n)])  16 us
    pallas_call x6, Pallas kernels, call(): pl.pallas_call(kernel, out_shape=out_shape, in_specs=[vmem] * len(inputs)...  4.78 us
    pallas_call x3, Pallas kernels, gradient(): pl.pallas_call(functools.partial(grad_kernel, factor=factor, first_piece=...  3.42 us
    pallas_call x1, Pallas kernels, part_of(): pl.pallas_call(part_kernel, out_shape=shapes, in_specs=[hbm, vmem, hbm],...  1.99 us
  transfers between devices with their start and end apart: 22, of which 13 were waited for; matrix products, arithmetic and copies ran while one was open for 6% of the time, Pallas kernels for 9%

profile of v5, /device:TPU:0, one launch (start us, length us, event | category | flops | bytes accessed | tf_op | source)
XLA Modules:
  0.0 60.9 jit_solution(17660516100675685203)
XLA Ops:
  1.4 2.0 %part.1 = (f32[72,384]{1,0:T(8,128)S(1)}, f32[72,384]{1,0:T(8,128)S(1)}, bf16[72,384]{1,0:T(8,128)(2,1)S(1)}, bf16[72,384]{1,0:T(8,128)(2,1)S(1)}, bf16[144,384]{1,0:T(8,128)(2,1)S(1)}) custom-call(bf16[64,3072]{1,0:T(8,128)(2,1)} %bitcast.22, f32[2,3072]{1,0:T(2,128)S(1)} %pad_maximum_fusion.vectors_ref, bf16[1,384,1536]{2,1,0:T(8,128)(2,1)} %block_ref.1), custom_call_target="tpu_custom_call" | custom-call | flops 169869312 | bytes 1179648 | tf_op jit(solution)/shard_map/part/pallas_call | solution.py:309
  3.5 3.0 %collective-permute-start = (bf16[72,384]{1,0:T(8,128)(2,1)S(1)}, bf16[72,384]{1,0:T(8,128)(2,1)S(1)}, u32[]{:S(2)}, u32[]{:S(2)}) collective-permute-start(bf16[72,384]{1,0:T(8,128)(2,1)S(1)} %get-tuple-element.25), channel_id=1, source_target_pairs={{0,1},{1,0},{2,3},{3,2},{4,5},{5,4},{6,7},{7,6},{8,9},{9,8},{10,11... | collective-permute-start | bytes 165896 | tf_op jit(solution)/shard_map/ppermute | solution.py:354
  6.6 1.0 %bitcast_convert_fusion = f32[64,3072]{1,0:T(8,128)S(1)} fusion(bf16[1,64,3072]{2,1,0:T(8,128)(2,1)} %param.11), kind=kLoop, calls=%fused_computation.30 | loop fusion | flops 196608 | bytes 1179648 | tf_op jit(solution)/shard_map/convert_element_type | solution.py:396
  7.7 0.9 %collective-permute-done = bf16[72,384]{1,0:T(8,128)(2,1)S(1)} collective-permute-done((bf16[72,384]{1,0:T(8,128)(2,1)S(1)}, bf16[72,384]{1,0:T(8,128)(2,1)S(1)}, u32[]{:S(2)}, u32[]{:S(2)}) %collective-permute-start) | collective-permute-done | bytes 55328 | tf_op jit(solution)/shard_map/ppermute | solution.py:354
  8.7 2.6 %collective-permute-start.1 = (bf16[72,384]{1,0:T(8,128)(2,1)S(1)}, bf16[72,384]{1,0:T(8,128)(2,1)S(1)}, u32[]{:S(2)}, u32[]{:S(2)}) collective-permute-start(bf16[72,384]{1,0:T(8,128)(2,1)S(1)} %fusion.6), channel_id=1, source_target_pairs={{0,2},{1,3},{2,0},{3,1},{4,6},{5,7},{6,4},{7,5},{8,10},{9,11},{10,... | collective-permute-start | bytes 165896 | tf_op jit(solution)/shard_map/ppermute | solution.py:354
  11.3 1.0 %collective-permute-start.4 = (bf16[72,384]{1,0:T(8,128)(2,1)S(1)}, bf16[72,384]{1,0:T(8,128)(2,1)S(1)}, u32[]{:S(2)}, u32[]{:S(2)}) collective-permute-start(bf16[72,384]{1,0:T(8,128)(2,1)S(1)} %fusion.7), channel_id=1, source_target_pairs={{0,2},{1,3},{2,0},{3,1},{4,6},{5,7},{6,4},{7,5},{8,10},{9,11},{10,... | collective-permute-start | bytes 165896 | tf_op jit(solution)/shard_map/ppermute | solution.py:354
  12.3 1.1 %collective-permute-done.1 = bf16[72,384]{1,0:T(8,128)(2,1)S(1)} collective-permute-done((bf16[72,384]{1,0:T(8,128)(2,1)S(1)}, bf16[72,384]{1,0:T(8,128)(2,1)S(1)}, u32[]{:S(2)}, u32[]{:S(2)}) %collective-permute-start.1) | collective-permute-done | bytes 55328 | tf_op jit(solution)/shard_map/ppermute | solution.py:354
  13.5 3.4 %collective-permute-start.2 = (bf16[72,384]{1,0:T(8,128)(2,1)S(1)}, bf16[72,384]{1,0:T(8,128)(2,1)S(1)}, u32[]{:S(2)}, u32[]{:S(2)}) collective-permute-start(bf16[72,384]{1,0:T(8,128)(2,1)S(1)} %fusion.10), channel_id=1, source_target_pairs={{0,4},{1,5},{2,6},{3,7},{4,0},{5,1},{6,2},{7,3},{8,12},{9,13},{10,... | collective-permute-start | bytes 165896 | tf_op jit(solution)/shard_map/ppermute | solution.py:354
  16.9 1.3 %collective-permute-start.5 = (bf16[72,384]{1,0:T(8,128)(2,1)S(1)}, bf16[72,384]{1,0:T(8,128)(2,1)S(1)}, u32[]{:S(2)}, u32[]{:S(2)}) collective-permute-start(bf16[72,384]{1,0:T(8,128)(2,1)S(1)} %fusion.11), channel_id=1, source_target_pairs={{0,4},{1,5},{2,6},{3,7},{4,0},{5,1},{6,2},{7,3},{8,12},{9,13},{10,... | collective-permute-start | bytes 165896 | tf_op jit(solution)/shard_map/ppermute | solution.py:354
  18.2 0.9 %collective-permute-done.2 = bf16[72,384]{1,0:T(8,128)(2,1)S(1)} collective-permute-done((bf16[72,384]{1,0:T(8,128)(2,1)S(1)}, bf16[72,384]{1,0:T(8,128)(2,1)S(1)}, u32[]{:S(2)}, u32[]{:S(2)}) %collective-permute-start.2) | collective-permute-done | bytes 55328 | tf_op jit(solution)/shard_map/ppermute | solution.py:354
  19.1 2.2 %collective-permute-start.6 = (bf16[72,384]{1,0:T(8,128)(2,1)S(1)}, bf16[72,384]{1,0:T(8,128)(2,1)S(1)}, u32[]{:S(2)}, u32[]{:S(2)}) collective-permute-start(bf16[72,384]{1,0:T(8,128)(2,1)S(1)} %add_convert_fusion.3.rest_0_), channel_id=1, source_target_pairs={{0,1},{1,0},{2,3},{3,2},{4,5},{5,4},{6,7},{7,6},{8,9},{9,8},{10,11... | collective-permute-start | bytes 165896 | tf_op jit(solution)/shard_map/ppermute | solution.py:354
  22.9 1.0 %fusion.gram_ref = f32[72,72]{1,0:T(8,128)S(1)} fusion(f32[3,3072]{1,0:T(4,128)S(1)} %broadcast_in_dim.15, f32[64,3072]{1,0:T(8,128)S(1)} %bitcast_convert_fusion, f32[72]{0:T(128)S(1)} %pad.6.clone), kind=kOutput, calls=%fused_computation | convolution fusion | flops 191545344 | bytes 844320 | tf_op jit(solution)/shard_map/dot_general | solution.py:398
  24.2 0.9 %generator_early.1.total_ref = f32[72,384]{1,0:T(8,128)S(1)} custom-call(bf16[64,384]{1,0:T(8,128)(2,1)S(1)} %bitcast.17, f32[72,72]{1,0:T(8,128)S(1)} %fusion.gram_ref, bf16[72,384]{1,0:T(8,128)(2,1)S(1)} %add_convert_fusion.3.rest_0_, bf16[72,384]{1,0:T(8,128)(2,1)S(1)} %add_convert_fusion.2.rest_1_, bf16[64,1536]{1,0:T(8,128)(2,1)S(1)} %bitcast.14), custom_call_target="tpu_custom_call" | custom-call | flops 84934656 | bytes 84934 | tf_op jit(solution)/shard_map/generator_early/pallas_call | solution.py:284
  25.0 1.3 %collective-permute-done.7.rest_1_.rest_3_ = bf16[72,384]{1,0:T(8,128)(2,1)S(1)} collective-permute-done((bf16[72,384]{1,0:T(8,128)(2,1)S(1)}, bf16[72,384]{1,0:T(8,128)(2,1)S(1)}, u32[]{:S(2)}, u32[]{:S(2)}) %collective-permute-start.7) | collective-permute-done | bytes 55328 | tf_op jit(solution)/shard_map/ppermute | solution.py:354
  27.1 0.8 %collective-permute-start.10 = (bf16[64,384]{1,0:T(8,128)(2,1)S(1)}, bf16[64,384]{1,0:T(8,128)(2,1)S(1)}, u32[]{:S(2)}, u32[]{:S(2)}) collective-permute-start(bf16[64,384]{1,0:T(8,128)(2,1)S(1)} %get-tuple-element.28.own_ref), channel_id=1, source_target_pairs={{0,16},{8,24},{16,0},{24,8},{1,17},{9,25},{17,1},{25,9},{2,18},{10... | collective-permute-start | bytes 147464 | tf_op jit(solution)/shard_map/ppermute | solution.py:354
  27.9 1.4 %collective-permute-start.8 = (bf16[64,384]{1,0:T(8,128)(2,1)S(1)}, bf16[64,384]{1,0:T(8,128)(2,1)S(1)}, u32[]{:S(2)}, u32[]{:S(2)}) collective-permute-start(bf16[64,384]{1,0:T(8,128)(2,1)S(1)} %get-tuple-element.28.own_ref), channel_id=1, source_target_pairs={{0,8},{8,0},{16,24},{24,16},{1,9},{9,1},{17,25},{25,17},{2,10},{10... | collective-permute-start | bytes 147464 | tf_op jit(solution)/shard_map/ppermute | solution.py:354
  29.5 2.1 %collective-permute-done.10.by2_ref = bf16[64,384]{1,0:T(8,128)(2,1)S(1)} collective-permute-done((bf16[64,384]{1,0:T(8,128)(2,1)S(1)}, bf16[64,384]{1,0:T(8,128)(2,1)S(1)}, u32[]{:S(2)}, u32[]{:S(2)}) %collective-permute-start.10) | collective-permute-done | bytes 49184 | tf_op jit(solution)/shard_map/ppermute | solution.py:354
  32.0 2.6 %collective-permute-start.13 = (bf16[64,384]{1,0:T(8,128)(2,1)S(1)}, bf16[64,384]{1,0:T(8,128)(2,1)S(1)}, u32[]{:S(2)}, u32[]{:S(2)}) collective-permute-start(bf16[64,384]{1,0:T(8,128)(2,1)S(1)} %get-tuple-element.34.piece_ref), channel_id=1, source_target_pairs={{0,16},{8,24},{16,0},{24,8},{1,17},{9,25},{17,1},{25,9},{2,18},{10... | collective-permute-start | bytes 147464 | tf_op jit(solution)/shard_map/ppermute | solution.py:354
  36.0 1.7 %slopes.1 = (bf16[384,256]{1,0:T(8,128)(2,1)S(1)}, f32[1536,384]{1,0:T(8,128)S(1)}, bf16[144,384]{1,0:T(8,128)(2,1)S(1)}) custom-call(bf16[64,384]{1,0:T(8,128)(2,1)S(1)} %bitcast.19, f32[72,384]{1,0:T(8,128)S(1)} %get-tuple-element.31.scaled_in_ref, f32[72,72]{1,0:T(8,128)S(1)} %get-tuple-element.30.gram_ref, ...), custom_call_target="tpu_custom_call" | custom-call | flops 84934656 | bytes 84934 | tf_op jit(solution)/shard_map/slopes/pallas_call | solution.py:284
  39.7 1.3 %collective-permute-start.14 = (bf16[72,384]{1,0:T(8,128)(2,1)S(1)}, bf16[72,384]{1,0:T(8,128)(2,1)S(1)}, u32[]{:S(2)}, u32[]{:S(2)}) collective-permute-start(bf16[72,384]{1,0:T(8,128)(2,1)S(1)} %get-tuple-element.42), channel_id=1, source_target_pairs={{0,1},{1,0},{2,3},{3,2},{4,5},{5,4},{6,7},{7,6},{8,9},{9,8},{10,11... | collective-permute-start | bytes 165896 | tf_op jit(solution)/shard_map/ppermute | solution.py:354
  41.7 2.0 %collective-permute-done.18 = bf16[72,384]{1,0:T(8,128)(2,1)S(1)} collective-permute-done((bf16[72,384]{1,0:T(8,128)(2,1)S(1)}, bf16[72,384]{1,0:T(8,128)(2,1)S(1)}, u32[]{:S(2)}, u32[]{:S(2)}) %collective-permute-start.18) | collective-permute-done | bytes 55328 | tf_op jit(solution)/shard_map/ppermute | solution.py:354
  43.7 1.3 %collective-permute-start.19 = (bf16[72,384]{1,0:T(8,128)(2,1)S(1)}, bf16[72,384]{1,0:T(8,128)(2,1)S(1)}, u32[]{:S(2)}, u32[]{:S(2)}) collective-permute-start(bf16[72,384]{1,0:T(8,128)(2,1)S(1)} %fusion.9), channel_id=1, source_target_pairs={{0,2},{1,3},{2,0},{3,1},{4,6},{5,7},{6,4},{7,5},{8,10},{9,11},{10,... | collective-permute-start | bytes 165896 | tf_op jit(solution)/shard_map/ppermute | solution.py:354
  45.0 0.9 %collective-permute-start.15 = (bf16[72,384]{1,0:T(8,128)(2,1)S(1)}, bf16[72,384]{1,0:T(8,128)(2,1)S(1)}, u32[]{:S(2)}, u32[]{:S(2)}) collective-permute-start(bf16[72,384]{1,0:T(8,128)(2,1)S(1)} %fusion.8), channel_id=1, source_target_pairs={{0,2},{1,3},{2,0},{3,1},{4,6},{5,7},{6,4},{7,5},{8,10},{9,11},{10,... | collective-permute-start | bytes 165896 | tf_op jit(solution)/shard_map/ppermute | solution.py:354
  46.0 2.4 %collective-permute-done.19 = bf16[72,384]{1,0:T(8,128)(2,1)S(1)} collective-permute-done((bf16[72,384]{1,0:T(8,128)(2,1)S(1)}, bf16[72,384]{1,0:T(8,128)(2,1)S(1)}, u32[]{:S(2)}, u32[]{:S(2)}) %collective-permute-start.19) | collective-permute-done | bytes 55328 | tf_op jit(solution)/shard_map/ppermute | solution.py:354
  48.4 1.4 %collective-permute-start.20 = (bf16[72,384]{1,0:T(8,128)(2,1)S(1)}, bf16[72,384]{1,0:T(8,128)(2,1)S(1)}, u32[]{:S(2)}, u32[]{:S(2)}) collective-permute-start(bf16[72,384]{1,0:T(8,128)(2,1)S(1)} %fusion.13), channel_id=1, source_target_pairs={{0,4},{1,5},{2,6},{3,7},{4,0},{5,1},{6,2},{7,3},{8,12},{9,13},{10,... | collective-permute-start | bytes 165896 | tf_op jit(solution)/shard_map/ppermute | solution.py:354
  49.9 1.7 %collective-permute-start.16 = (bf16[72,384]{1,0:T(8,128)(2,1)S(1)}, bf16[72,384]{1,0:T(8,128)(2,1)S(1)}, u32[]{:S(2)}, u32[]{:S(2)}) collective-permute-start(bf16[72,384]{1,0:T(8,128)(2,1)S(1)} %fusion.12), channel_id=1, source_target_pairs={{0,4},{1,5},{2,6},{3,7},{4,0},{5,1},{6,2},{7,3},{8,12},{9,13},{10,... | collective-permute-start | bytes 165896 | tf_op jit(solution)/shard_map/ppermute | solution.py:354
  51.5 2.9 %collective-permute-done.20 = bf16[72,384]{1,0:T(8,128)(2,1)S(1)} collective-permute-done((bf16[72,384]{1,0:T(8,128)(2,1)S(1)}, bf16[72,384]{1,0:T(8,128)(2,1)S(1)}, u32[]{:S(2)}, u32[]{:S(2)}) %collective-permute-start.20) | collective-permute-done | bytes 55328 | tf_op jit(solution)/shard_map/ppermute | solution.py:354
  54.4 1.1 %collective-permute-start.21 = (bf16[72,384]{1,0:T(8,128)(2,1)S(1)}, bf16[72,384]{1,0:T(8,128)(2,1)S(1)}, u32[]{:S(2)}, u32[]{:S(2)}) collective-permute-start(bf16[72,384]{1,0:T(8,128)(2,1)S(1)} %add_convert_fusion.rest_0_), channel_id=1, source_target_pairs={{0,1},{1,0},{2,3},{3,2},{4,5},{5,4},{6,7},{7,6},{8,9},{9,8},{10,11... | collective-permute-start | bytes 165896 | tf_op jit(solution)/shard_map/ppermute | solution.py:354
  55.6 1.0 %collective-permute-start.17 = (bf16[72,384]{1,0:T(8,128)(2,1)S(1)}, bf16[72,384]{1,0:T(8,128)(2,1)S(1)}, u32[]{:S(2)}, u32[]{:S(2)}) collective-permute-start(bf16[72,384]{1,0:T(8,128)(2,1)S(1)} %add_convert_fusion.1.rest_1_), channel_id=1, source_target_pairs={{0,1},{1,0},{2,3},{3,2},{4,5},{5,4},{6,7},{7,6},{8,9},{9,8},{10,11... | collective-permute-start | bytes 165896 | tf_op jit(solution)/shard_map/ppermute | solution.py:354
  56.6 1.3 %gradient.3.rest_1_ = f32[1,384,1536]{2,1,0:T(8,128)} custom-call(bf16[384,256]{1,0:T(8,128)(2,1)S(1)} %get-tuple-element.33.own_ref, bf16[72,384]{1,0:T(8,128)(2,1)S(1)} %add_convert_fusion.rest_0_, bf16[72,384]{1,0:T(8,128)(2,1)S(1)} %add_convert_fusion.1.rest_1_), custom_call_target="tpu_custom_call" | custom-call | flops 150994944 | bytes 1179648 | tf_op jit(solution)/shard_map/gradient/pallas_call | solution.py:336
  58.7 1.1 %gradient.4.rest_1_ = f32[1,384,1536]{2,1,0:T(8,128)} custom-call(bf16[384,256]{1,0:T(8,128)(2,1)S(1)} %get-tuple-element.33.own_ref, bf16[72,384]{1,0:T(8,128)(2,1)S(1)} %collective-permute-done.21.rest_0_, f32[1,384,1536]{2,1,0:T(8,128)} %gradient.3.rest_1_), custom_call_target="tpu_custom_call", output_to_operand_aliasing={{}: (2, {})} | custom-call | flops 75497472 | bytes 589824 | tf_op jit(solution)/shard_map/gradient/pallas_call | solution.py:336
  59.8 1.1 %gradient.5 = f32[1,384,1536]{2,1,0:T(8,128)} custom-call(bf16[384,256]{1,0:T(8,128)(2,1)S(1)} %get-tuple-element.33.own_ref, bf16[72,384]{1,0:T(8,128)(2,1)S(1)} %collective-permute-done.17.rest_0_, f32[1,384,1536]{2,1,0:T(8,128)} %gradient.4.rest_1_), custom_call_target="tpu_custom_call", output_to_operand_aliasing={{}: (2, {})} | custom-call | flops 75497472 | bytes 589824 | tf_op jit(solution)/shard_map/gradient/pallas_call | solution.py:336
  (54 shorter events, 9.3 us)
Async XLA Ops:
  0.6 22.3 %copy-start.3 = (f32[1,3072]{1,0:T(1,128)S(1)}, f32[1,3072]{1,0:T(1,128)}, u32[]{:S(2)}) copy-start(f32[1,3072]{1,0:T(1,128)} %param.12) | copy-start | bytes 36868
  3.4 20.5 %copy-start.4 = (f32[384]{0:T(512)S(1)}, f32[384]{0:T(512)}, u32[]{:S(2)}) copy-start(f32[384]{0:T(512)} %param.10) | copy-start | bytes 4612
  3.5 20.5 %copy-start = (bf16[1,1536,64]{1,2,0:T(8,128)(2,1)S(1)}, bf16[1,1536,64]{1,2,0:T(8,128)(2,1)}, u32[]{:S(2)}) copy-start(bf16[1,1536,64]{1,2,0:T(8,128)(2,1)} %param.15) | copy-start | bytes 589828
  3.5 20.7 %copy-start.1 = (bf16[384,64]{0,1:T(8,128)(2,1)S(1)}, bf16[384,64]{0,1:T(8,128)(2,1)}, u32[]{:S(2)}) copy-start(bf16[384,64]{0,1:T(8,128)(2,1)} %param.8) | copy-start | bytes 147460
  3.5 5.2 %collective-permute-start = (bf16[72,384]{1,0:T(8,128)(2,1)S(1)}, bf16[72,384]{1,0:T(8,128)(2,1)S(1)}, u32[]{:S(2)}, u32[]{:S(2)}) collective-permute-start(bf16[72,384]{1,0:T(8,128)(2,1)S(1)} %get-tuple-element.25), channel_id=1, source_target_pairs={{0,1},{1,0},{2,3},{3,2},{4,5},{5,4},{6,7},{7,6},{8,9},{9,8},{10,11... | collective-permute-start | bytes 165896 | tf_op jit(solution)/shard_map/ppermute | solution.py:354
  6.5 19.8 %copy-start.2 = (bf16[384,64]{0,1:T(8,128)(2,1)S(1)}, bf16[384,64]{0,1:T(8,128)(2,1)}, u32[]{:S(2)}) copy-start(bf16[384,64]{0,1:T(8,128)(2,1)} %param.9) | copy-start | bytes 147460
  6.5 4.8 %collective-permute-start.3 = (bf16[72,384]{1,0:T(8,128)(2,1)S(1)}, bf16[72,384]{1,0:T(8,128)(2,1)S(1)}, u32[]{:S(2)}, u32[]{:S(2)}) collective-permute-start(bf16[72,384]{1,0:T(8,128)(2,1)S(1)} %get-tuple-element.27), channel_id=1, source_target_pairs={{0,1},{1,0},{2,3},{3,2},{4,5},{5,4},{6,7},{7,6},{8,9},{9,8},{10,11... | collective-permute-start | bytes 165896 | tf_op jit(solution)/shard_map/ppermute | solution.py:354
  8.7 4.8 %collective-permute-start.1 = (bf16[72,384]{1,0:T(8,128)(2,1)S(1)}, bf16[72,384]{1,0:T(8,128)(2,1)S(1)}, u32[]{:S(2)}, u32[]{:S(2)}) collective-permute-start(bf16[72,384]{1,0:T(8,128)(2,1)S(1)} %fusion.6), channel_id=1, source_target_pairs={{0,2},{1,3},{2,0},{3,1},{4,6},{5,7},{6,4},{7,5},{8,10},{9,11},{10,... | collective-permute-start | bytes 165896 | tf_op jit(solution)/shard_map/ppermute | solution.py:354
  11.3 5.6 %collective-permute-start.4 = (bf16[72,384]{1,0:T(8,128)(2,1)S(1)}, bf16[72,384]{1,0:T(8,128)(2,1)S(1)}, u32[]{:S(2)}, u32[]{:S(2)}) collective-permute-start(bf16[72,384]{1,0:T(8,128)(2,1)S(1)} %fusion.7), channel_id=1, source_target_pairs={{0,2},{1,3},{2,0},{3,1},{4,6},{5,7},{6,4},{7,5},{8,10},{9,11},{10,... | collective-permute-start | bytes 165896 | tf_op jit(solution)/shard_map/ppermute | solution.py:354
  13.5 5.6 %collective-permute-start.2 = (bf16[72,384]{1,0:T(8,128)(2,1)S(1)}, bf16[72,384]{1,0:T(8,128)(2,1)S(1)}, u32[]{:S(2)}, u32[]{:S(2)}) collective-permute-start(bf16[72,384]{1,0:T(8,128)(2,1)S(1)} %fusion.10), channel_id=1, source_target_pairs={{0,4},{1,5},{2,6},{3,7},{4,0},{5,1},{6,2},{7,3},{8,12},{9,13},{10,... | collective-permute-start | bytes 165896 | tf_op jit(solution)/shard_map/ppermute | solution.py:354
  16.9 5.1 %collective-permute-start.5 = (bf16[72,384]{1,0:T(8,128)(2,1)S(1)}, bf16[72,384]{1,0:T(8,128)(2,1)S(1)}, u32[]{:S(2)}, u32[]{:S(2)}) collective-permute-start(bf16[72,384]{1,0:T(8,128)(2,1)S(1)} %fusion.11), channel_id=1, source_target_pairs={{0,4},{1,5},{2,6},{3,7},{4,0},{5,1},{6,2},{7,3},{8,12},{9,13},{10,... | collective-permute-start | bytes 165896 | tf_op jit(solution)/shard_map/ppermute | solution.py:354
  19.1 5.9 %collective-permute-start.6 = (bf16[72,384]{1,0:T(8,128)(2,1)S(1)}, bf16[72,384]{1,0:T(8,128)(2,1)S(1)}, u32[]{:S(2)}, u32[]{:S(2)}) collective-permute-start(bf16[72,384]{1,0:T(8,128)(2,1)S(1)} %add_convert_fusion.3.rest_0_), channel_id=1, source_target_pairs={{0,1},{1,0},{2,3},{3,2},{4,5},{5,4},{6,7},{7,6},{8,9},{9,8},{10,11... | collective-permute-start | bytes 165896 | tf_op jit(solution)/shard_map/ppermute | solution.py:354
  22.1 4.2 %collective-permute-start.7 = (bf16[72,384]{1,0:T(8,128)(2,1)S(1)}, bf16[72,384]{1,0:T(8,128)(2,1)S(1)}, u32[]{:S(2)}, u32[]{:S(2)}) collective-permute-start(bf16[72,384]{1,0:T(8,128)(2,1)S(1)} %add_convert_fusion.2.rest_1_), channel_id=1, source_target_pairs={{0,1},{1,0},{2,3},{3,2},{4,5},{5,4},{6,7},{7,6},{8,9},{9,8},{10,11... | collective-permute-start | bytes 165896 | tf_op jit(solution)/shard_map/ppermute | solution.py:354
  27.1 4.5 %collective-permute-start.10 = (bf16[64,384]{1,0:T(8,128)(2,1)S(1)}, bf16[64,384]{1,0:T(8,128)(2,1)S(1)}, u32[]{:S(2)}, u32[]{:S(2)}) collective-permute-start(bf16[64,384]{1,0:T(8,128)(2,1)S(1)} %get-tuple-element.28.own_ref), channel_id=1, source_target_pairs={{0,16},{8,24},{16,0},{24,8},{1,17},{9,25},{17,1},{25,9},{2,18},{10... | collective-permute-start | bytes 147464 | tf_op jit(solution)/shard_map/ppermute | solution.py:354
  27.9 4.0 %collective-permute-start.9 = (bf16[64,384]{1,0:T(8,128)(2,1)S(1)}, bf16[64,384]{1,0:T(8,128)(2,1)S(1)}, u32[]{:S(2)}, u32[]{:S(2)}) collective-permute-start(bf16[64,384]{1,0:T(8,128)(2,1)S(1)} %get-tuple-element.28.own_ref), channel_id=1, source_target_pairs={{0,24},{8,16},{16,8},{24,0},{1,25},{9,17},{17,9},{25,1},{2,26},{10... | collective-permute-start | bytes 147464 | tf_op jit(solution)/shard_map/ppermute | solution.py:354
  27.9 4.0 %collective-permute-start.8 = (bf16[64,384]{1,0:T(8,128)(2,1)S(1)}, bf16[64,384]{1,0:T(8,128)(2,1)S(1)}, u32[]{:S(2)}, u32[]{:S(2)}) collective-permute-start(bf16[64,384]{1,0:T(8,128)(2,1)S(1)} %get-tuple-element.28.own_ref), channel_id=1, source_target_pairs={{0,8},{8,0},{16,24},{24,16},{1,9},{9,1},{17,25},{25,17},{2,10},{10... | collective-permute-start | bytes 147464 | tf_op jit(solution)/shard_map/ppermute | solution.py:354
  32.0 5.7 %collective-permute-start.13 = (bf16[64,384]{1,0:T(8,128)(2,1)S(1)}, bf16[64,384]{1,0:T(8,128)(2,1)S(1)}, u32[]{:S(2)}, u32[]{:S(2)}) collective-permute-start(bf16[64,384]{1,0:T(8,128)(2,1)S(1)} %get-tuple-element.34.piece_ref), channel_id=1, source_target_pairs={{0,16},{8,24},{16,0},{24,8},{1,17},{9,25},{17,1},{25,9},{2,18},{10... | collective-permute-start | bytes 147464 | tf_op jit(solution)/shard_map/ppermute | solution.py:354
  34.6 3.5 %collective-permute-start.12 = (bf16[64,384]{1,0:T(8,128)(2,1)S(1)}, bf16[64,384]{1,0:T(8,128)(2,1)S(1)}, u32[]{:S(2)}, u32[]{:S(2)}) collective-permute-start(bf16[64,384]{1,0:T(8,128)(2,1)S(1)} %get-tuple-element.34.piece_ref), channel_id=1, source_target_pairs={{0,24},{8,16},{16,8},{24,0},{1,25},{9,17},{17,9},{25,1},{2,26},{10... | collective-permute-start | bytes 147464 | tf_op jit(solution)/shard_map/ppermute | solution.py:354
  35.3 2.8 %collective-permute-start.11 = (bf16[64,384]{1,0:T(8,128)(2,1)S(1)}, bf16[64,384]{1,0:T(8,128)(2,1)S(1)}, u32[]{:S(2)}, u32[]{:S(2)}) collective-permute-start(bf16[64,384]{1,0:T(8,128)(2,1)S(1)} %get-tuple-element.34.piece_ref), channel_id=1, source_target_pairs={{0,8},{8,0},{16,24},{24,16},{1,9},{9,1},{17,25},{25,17},{2,10},{10... | collective-permute-start | bytes 147464 | tf_op jit(solution)/shard_map/ppermute | solution.py:354
  38.9 4.8 %collective-permute-start.18 = (bf16[72,384]{1,0:T(8,128)(2,1)S(1)}, bf16[72,384]{1,0:T(8,128)(2,1)S(1)}, u32[]{:S(2)}, u32[]{:S(2)}) collective-permute-start(bf16[72,384]{1,0:T(8,128)(2,1)S(1)} %get-tuple-element.44), channel_id=1, source_target_pairs={{0,1},{1,0},{2,3},{3,2},{4,5},{5,4},{6,7},{7,6},{8,9},{9,8},{10,11... | collective-permute-start | bytes 165896 | tf_op jit(solution)/shard_map/ppermute | solution.py:354
  39.7 5.3 %collective-permute-start.14 = (bf16[72,384]{1,0:T(8,128)(2,1)S(1)}, bf16[72,384]{1,0:T(8,128)(2,1)S(1)}, u32[]{:S(2)}, u32[]{:S(2)}) collective-permute-start(bf16[72,384]{1,0:T(8,128)(2,1)S(1)} %get-tuple-element.42), channel_id=1, source_target_pairs={{0,1},{1,0},{2,3},{3,2},{4,5},{5,4},{6,7},{7,6},{8,9},{9,8},{10,11... | collective-permute-start | bytes 165896 | tf_op jit(solution)/shard_map/ppermute | solution.py:354
  43.7 4.7 %collective-permute-start.19 = (bf16[72,384]{1,0:T(8,128)(2,1)S(1)}, bf16[72,384]{1,0:T(8,128)(2,1)S(1)}, u32[]{:S(2)}, u32[]{:S(2)}) collective-permute-start(bf16[72,384]{1,0:T(8,128)(2,1)S(1)} %fusion.9), channel_id=1, source_target_pairs={{0,2},{1,3},{2,0},{3,1},{4,6},{5,7},{6,4},{7,5},{8,10},{9,11},{10,... | collective-permute-start | bytes 165896 | tf_op jit(solution)/shard_map/ppermute | solution.py:354
  45.0 4.8 %collective-permute-start.15 = (bf16[72,384]{1,0:T(8,128)(2,1)S(1)}, bf16[72,384]{1,0:T(8,128)(2,1)S(1)}, u32[]{:S(2)}, u32[]{:S(2)}) collective-permute-start(bf16[72,384]{1,0:T(8,128)(2,1)S(1)} %fusion.8), channel_id=1, source_target_pairs={{0,2},{1,3},{2,0},{3,1},{4,6},{5,7},{6,4},{7,5},{8,10},{9,11},{10,... | collective-permute-start | bytes 165896 | tf_op jit(solution)/shard_map/ppermute | solution.py:354
  48.4 6.0 %collective-permute-start.20 = (bf16[72,384]{1,0:T(8,128)(2,1)S(1)}, bf16[72,384]{1,0:T(8,128)(2,1)S(1)}, u32[]{:S(2)}, u32[]{:S(2)}) collective-permute-start(bf16[72,384]{1,0:T(8,128)(2,1)S(1)} %fusion.13), channel_id=1, source_target_pairs={{0,4},{1,5},{2,6},{3,7},{4,0},{5,1},{6,2},{7,3},{8,12},{9,13},{10,... | collective-permute-start | bytes 165896 | tf_op jit(solution)/shard_map/ppermute | solution.py:354
  49.9 5.7 %collective-permute-start.16 = (bf16[72,384]{1,0:T(8,128)(2,1)S(1)}, bf16[72,384]{1,0:T(8,128)(2,1)S(1)}, u32[]{:S(2)}, u32[]{:S(2)}) collective-permute-start(bf16[72,384]{1,0:T(8,128)(2,1)S(1)} %fusion.12), channel_id=1, source_target_pairs={{0,4},{1,5},{2,6},{3,7},{4,0},{5,1},{6,2},{7,3},{8,12},{9,13},{10,... | collective-permute-start | bytes 165896 | tf_op jit(solution)/shard_map/ppermute | solution.py:354
  54.4 4.2 %collective-permute-start.21 = (bf16[72,384]{1,0:T(8,128)(2,1)S(1)}, bf16[72,384]{1,0:T(8,128)(2,1)S(1)}, u32[]{:S(2)}, u32[]{:S(2)}) collective-permute-start(bf16[72,384]{1,0:T(8,128)(2,1)S(1)} %add_convert_fusion.rest_0_), channel_id=1, source_target_pairs={{0,1},{1,0},{2,3},{3,2},{4,5},{5,4},{6,7},{7,6},{8,9},{9,8},{10,11... | collective-permute-start | bytes 165896 | tf_op jit(solution)/shard_map/ppermute | solution.py:354
  55.6 4.2 %collective-permute-start.17 = (bf16[72,384]{1,0:T(8,128)(2,1)S(1)}, bf16[72,384]{1,0:T(8,128)(2,1)S(1)}, u32[]{:S(2)}, u32[]{:S(2)}) collective-permute-start(bf16[72,384]{1,0:T(8,128)(2,1)S(1)} %add_convert_fusion.1.rest_1_), channel_id=1, source_target_pairs={{0,1},{1,0},{2,3},{3,2},{4,5},{5,4},{6,7},{7,6},{8,9},{9,8},{10,11... | collective-permute-start | bytes 165896 | tf_op jit(solution)/shard_map/ppermute | solution.py:354

commit v6 on v5

--- a/solution.py
+++ b/solution.py
@@ -58,7 +58,7 @@
         precision=lax.Precision.HIGHEST,
         preferred_element_type=f32,
     )
-    square = jnp.sum(seen * wide, axis=0, keepdims=True)
+    square = jnp.maximum(jnp.sum(seen * wide, axis=0, keepdims=True), 0.0)
     return lax.rsqrt(square * (1.0 / width) + 1e-06), seen
 
 

time: 61.1 us -> 61.1 us (level)
  transfers between devices with their start and end apart: 22 -> 22, of which waited for: 13 -> 12; matrix products, arithmetic and copies ran while one was open for 6% -> 6% of each run, Pallas kernels for 9% -> 9%
where the time goes in v6:
time: 61.1 us; the launch traced here: 60.9 us
  starting transfers between devices  29.5 us (48%)
  waiting for transfers between devices  16 us (26%)
  Pallas kernels  10.2 us (17%)
  other arithmetic  3 us (5%)
  matrix products  0.98 us (2%)
  between operations  0.88 us (1%)
    ppermute x22, starting transfers between devices, swap(): return lax.ppermute(value, axis, [(i, i ^ bit) for i in range(n)])  29.5 us
    ppermute x22, waiting for transfers between devices, swap(): return lax.ppermute(value, axis, [(i, i ^ bit) for i in range(n)])  16 us
    pallas_call x6, Pallas kernels, call(): pl.pallas_call(kernel, out_shape=out_shape, in_specs=[vmem] * len(inputs)...  4.77 us
    pallas_call x3, Pallas kernels, gradient(): pl.pallas_call(functools.partial(grad_kernel, factor=factor, first_piece=...  3.42 us
    pallas_call x1, Pallas kernels, part_of(): pl.pallas_call(part_kernel, out_shape=shapes, in_specs=[hbm, vmem, hbm],...  1.99 us
  transfers between devices with their start and end apart: 22, of which 12 were waited for; matrix products, arithmetic and copies ran while one was open for 6% of the time, Pallas kernels for 9%

profile of v6, /device:TPU:0, one launch (start us, length us, event | category | flops | bytes accessed | tf_op | source)
XLA Modules:
  0.0 60.9 jit_solution(16196414686725091670)
XLA Ops:
  1.4 2.0 %part.1 = (f32[72,384]{1,0:T(8,128)S(1)}, f32[72,384]{1,0:T(8,128)S(1)}, bf16[72,384]{1,0:T(8,128)(2,1)S(1)}, bf16[72,384]{1,0:T(8,128)(2,1)S(1)}, bf16[144,384]{1,0:T(8,128)(2,1)S(1)}) custom-call(bf16[64,3072]{1,0:T(8,128)(2,1)} %bitcast.22, f32[2,3072]{1,0:T(2,128)S(1)} %pad_maximum_fusion.vectors_ref, bf16[1,384,1536]{2,1,0:T(8,128)(2,1)} %block_ref.1), custom_call_target="tpu_custom_call" | custom-call | flops 169869312 | bytes 1179648 | tf_op jit(solution)/shard_map/part/pallas_call | solution.py:309
  3.5 3.0 %collective-permute-start = (bf16[72,384]{1,0:T(8,128)(2,1)S(1)}, bf16[72,384]{1,0:T(8,128)(2,1)S(1)}, u32[]{:S(2)}, u32[]{:S(2)}) collective-permute-start(bf16[72,384]{1,0:T(8,128)(2,1)S(1)} %get-tuple-element.25), channel_id=1, source_target_pairs={{0,1},{1,0},{2,3},{3,2},{4,5},{5,4},{6,7},{7,6},{8,9},{9,8},{10,11... | collective-permute-start | bytes 165896 | tf_op jit(solution)/shard_map/ppermute | solution.py:354
  6.6 1.0 %bitcast_convert_fusion = f32[64,3072]{1,0:T(8,128)S(1)} fusion(bf16[1,64,3072]{2,1,0:T(8,128)(2,1)} %param.11), kind=kLoop, calls=%fused_computation.30 | loop fusion | flops 196608 | bytes 1179648 | tf_op jit(solution)/shard_map/convert_element_type | solution.py:396
  7.7 0.9 %collective-permute-done = bf16[72,384]{1,0:T(8,128)(2,1)S(1)} collective-permute-done((bf16[72,384]{1,0:T(8,128)(2,1)S(1)}, bf16[72,384]{1,0:T(8,128)(2,1)S(1)}, u32[]{:S(2)}, u32[]{:S(2)}) %collective-permute-start) | collective-permute-done | bytes 55328 | tf_op jit(solution)/shard_map/ppermute | solution.py:354
  8.7 2.6 %collective-permute-start.1 = (bf16[72,384]{1,0:T(8,128)(2,1)S(1)}, bf16[72,384]{1,0:T(8,128)(2,1)S(1)}, u32[]{:S(2)}, u32[]{:S(2)}) collective-permute-start(bf16[72,384]{1,0:T(8,128)(2,1)S(1)} %fusion.6), channel_id=1, source_target_pairs={{0,2},{1,3},{2,0},{3,1},{4,6},{5,7},{6,4},{7,5},{8,10},{9,11},{10,... | collective-permute-start | bytes 165896 | tf_op jit(solution)/shard_map/ppermute | solution.py:354
  11.3 1.0 %collective-permute-start.4 = (bf16[72,384]{1,0:T(8,128)(2,1)S(1)}, bf16[72,384]{1,0:T(8,128)(2,1)S(1)}, u32[]{:S(2)}, u32[]{:S(2)}) collective-permute-start(bf16[72,384]{1,0:T(8,128)(2,1)S(1)} %fusion.7), channel_id=1, source_target_pairs={{0,2},{1,3},{2,0},{3,1},{4,6},{5,7},{6,4},{7,5},{8,10},{9,11},{10,... | collective-permute-start | bytes 165896 | tf_op jit(solution)/shard_map/ppermute | solution.py:354
  12.3 1.1 %collective-permute-done.1 = bf16[72,384]{1,0:T(8,128)(2,1)S(1)} collective-permute-done((bf16[72,384]{1,0:T(8,128)(2,1)S(1)}, bf16[72,384]{1,0:T(8,128)(2,1)S(1)}, u32[]{:S(2)}, u32[]{:S(2)}) %collective-permute-start.1) | collective-permute-done | bytes 55328 | tf_op jit(solution)/shard_map/ppermute | solution.py:354
  13.5 3.4 %collective-permute-start.2 = (bf16[72,384]{1,0:T(8,128)(2,1)S(1)}, bf16[72,384]{1,0:T(8,128)(2,1)S(1)}, u32[]{:S(2)}, u32[]{:S(2)}) collective-permute-start(bf16[72,384]{1,0:T(8,128)(2,1)S(1)} %fusion.10), channel_id=1, source_target_pairs={{0,4},{1,5},{2,6},{3,7},{4,0},{5,1},{6,2},{7,3},{8,12},{9,13},{10,... | collective-permute-start | bytes 165896 | tf_op jit(solution)/shard_map/ppermute | solution.py:354
  16.9 1.3 %collective-permute-start.5 = (bf16[72,384]{1,0:T(8,128)(2,1)S(1)}, bf16[72,384]{1,0:T(8,128)(2,1)S(1)}, u32[]{:S(2)}, u32[]{:S(2)}) collective-permute-start(bf16[72,384]{1,0:T(8,128)(2,1)S(1)} %fusion.11), channel_id=1, source_target_pairs={{0,4},{1,5},{2,6},{3,7},{4,0},{5,1},{6,2},{7,3},{8,12},{9,13},{10,... | collective-permute-start | bytes 165896 | tf_op jit(solution)/shard_map/ppermute | solution.py:354
  18.2 0.9 %collective-permute-done.2 = bf16[72,384]{1,0:T(8,128)(2,1)S(1)} collective-permute-done((bf16[72,384]{1,0:T(8,128)(2,1)S(1)}, bf16[72,384]{1,0:T(8,128)(2,1)S(1)}, u32[]{:S(2)}, u32[]{:S(2)}) %collective-permute-start.2) | collective-permute-done | bytes 55328 | tf_op jit(solution)/shard_map/ppermute | solution.py:354
  19.1 2.2 %collective-permute-start.6 = (bf16[72,384]{1,0:T(8,128)(2,1)S(1)}, bf16[72,384]{1,0:T(8,128)(2,1)S(1)}, u32[]{:S(2)}, u32[]{:S(2)}) collective-permute-start(bf16[72,384]{1,0:T(8,128)(2,1)S(1)} %add_convert_fusion.3.rest_0_), channel_id=1, source_target_pairs={{0,1},{1,0},{2,3},{3,2},{4,5},{5,4},{6,7},{7,6},{8,9},{9,8},{10,11... | collective-permute-start | bytes 165896 | tf_op jit(solution)/shard_map/ppermute | solution.py:354
  22.9 1.0 %fusion.gram_ref = f32[72,72]{1,0:T(8,128)S(1)} fusion(f32[3,3072]{1,0:T(4,128)S(1)} %broadcast_in_dim.15, f32[64,3072]{1,0:T(8,128)S(1)} %bitcast_convert_fusion, f32[72]{0:T(128)S(1)} %pad.6.clone), kind=kOutput, calls=%fused_computation | convolution fusion | flops 191545344 | bytes 844320 | tf_op jit(solution)/shard_map/dot_general | solution.py:398
  24.2 0.9 %generator_early.1.total_ref = f32[72,384]{1,0:T(8,128)S(1)} custom-call(bf16[64,384]{1,0:T(8,128)(2,1)S(1)} %bitcast.17, f32[72,72]{1,0:T(8,128)S(1)} %fusion.gram_ref, bf16[72,384]{1,0:T(8,128)(2,1)S(1)} %add_convert_fusion.3.rest_0_, bf16[72,384]{1,0:T(8,128)(2,1)S(1)} %add_convert_fusion.2.rest_1_, bf16[64,1536]{1,0:T(8,128)(2,1)S(1)} %bitcast.14), custom_call_target="tpu_custom_call" | custom-call | flops 84934656 | bytes 84934 | tf_op jit(solution)/shard_map/generator_early/pallas_call | solution.py:284
  25.0 1.3 %collective-permute-done.7.rest_1_.rest_3_ = bf16[72,384]{1,0:T(8,128)(2,1)S(1)} collective-permute-done((bf16[72,384]{1,0:T(8,128)(2,1)S(1)}, bf16[72,384]{1,0:T(8,128)(2,1)S(1)}, u32[]{:S(2)}, u32[]{:S(2)}) %collective-permute-start.7) | collective-permute-done | bytes 55328 | tf_op jit(solution)/shard_map/ppermute | solution.py:354
  27.1 0.8 %collective-permute-start.10 = (bf16[64,384]{1,0:T(8,128)(2,1)S(1)}, bf16[64,384]{1,0:T(8,128)(2,1)S(1)}, u32[]{:S(2)}, u32[]{:S(2)}) collective-permute-start(bf16[64,384]{1,0:T(8,128)(2,1)S(1)} %get-tuple-element.28.own_ref), channel_id=1, source_target_pairs={{0,16},{8,24},{16,0},{24,8},{1,17},{9,25},{17,1},{25,9},{2,18},{10... | collective-permute-start | bytes 147464 | tf_op jit(solution)/shard_map/ppermute | solution.py:354
  27.9 1.4 %collective-permute-start.8 = (bf16[64,384]{1,0:T(8,128)(2,1)S(1)}, bf16[64,384]{1,0:T(8,128)(2,1)S(1)}, u32[]{:S(2)}, u32[]{:S(2)}) collective-permute-start(bf16[64,384]{1,0:T(8,128)(2,1)S(1)} %get-tuple-element.28.own_ref), channel_id=1, source_target_pairs={{0,8},{8,0},{16,24},{24,16},{1,9},{9,1},{17,25},{25,17},{2,10},{10... | collective-permute-start | bytes 147464 | tf_op jit(solution)/shard_map/ppermute | solution.py:354
  29.5 2.1 %collective-permute-done.10.by2_ref = bf16[64,384]{1,0:T(8,128)(2,1)S(1)} collective-permute-done((bf16[64,384]{1,0:T(8,128)(2,1)S(1)}, bf16[64,384]{1,0:T(8,128)(2,1)S(1)}, u32[]{:S(2)}, u32[]{:S(2)}) %collective-permute-start.10) | collective-permute-done | bytes 49184 | tf_op jit(solution)/shard_map/ppermute | solution.py:354
  32.0 2.6 %collective-permute-start.13 = (bf16[64,384]{1,0:T(8,128)(2,1)S(1)}, bf16[64,384]{1,0:T(8,128)(2,1)S(1)}, u32[]{:S(2)}, u32[]{:S(2)}) collective-permute-start(bf16[64,384]{1,0:T(8,128)(2,1)S(1)} %get-tuple-element.34.piece_ref), channel_id=1, source_target_pairs={{0,16},{8,24},{16,0},{24,8},{1,17},{9,25},{17,1},{25,9},{2,18},{10... | collective-permute-start | bytes 147464 | tf_op jit(solution)/shard_map/ppermute | solution.py:354
  36.0 1.6 %slopes.1 = (bf16[384,256]{1,0:T(8,128)(2,1)S(1)}, f32[1536,384]{1,0:T(8,128)S(1)}, bf16[144,384]{1,0:T(8,128)(2,1)S(1)}) custom-call(bf16[64,384]{1,0:T(8,128)(2,1)S(1)} %bitcast.19, f32[72,384]{1,0:T(8,128)S(1)} %get-tuple-element.31.scaled_in_ref, f32[72,72]{1,0:T(8,128)S(1)} %get-tuple-element.30.gram_ref, ...), custom_call_target="tpu_custom_call" | custom-call | flops 84934656 | bytes 84934 | tf_op jit(solution)/shard_map/slopes/pallas_call | solution.py:284
  39.7 1.3 %collective-permute-start.14 = (bf16[72,384]{1,0:T(8,128)(2,1)S(1)}, bf16[72,384]{1,0:T(8,128)(2,1)S(1)}, u32[]{:S(2)}, u32[]{:S(2)}) collective-permute-start(bf16[72,384]{1,0:T(8,128)(2,1)S(1)} %get-tuple-element.42), channel_id=1, source_target_pairs={{0,1},{1,0},{2,3},{3,2},{4,5},{5,4},{6,7},{7,6},{8,9},{9,8},{10,11... | collective-permute-start | bytes 165896 | tf_op jit(solution)/shard_map/ppermute | solution.py:354
  41.7 2.0 %collective-permute-done.18 = bf16[72,384]{1,0:T(8,128)(2,1)S(1)} collective-permute-done((bf16[72,384]{1,0:T(8,128)(2,1)S(1)}, bf16[72,384]{1,0:T(8,128)(2,1)S(1)}, u32[]{:S(2)}, u32[]{:S(2)}) %collective-permute-start.18) | collective-permute-done | bytes 55328 | tf_op jit(solution)/shard_map/ppermute | solution.py:354
  43.7 1.3 %collective-permute-start.19 = (bf16[72,384]{1,0:T(8,128)(2,1)S(1)}, bf16[72,384]{1,0:T(8,128)(2,1)S(1)}, u32[]{:S(2)}, u32[]{:S(2)}) collective-permute-start(bf16[72,384]{1,0:T(8,128)(2,1)S(1)} %fusion.9), channel_id=1, source_target_pairs={{0,2},{1,3},{2,0},{3,1},{4,6},{5,7},{6,4},{7,5},{8,10},{9,11},{10,... | collective-permute-start | bytes 165896 | tf_op jit(solution)/shard_map/ppermute | solution.py:354
  45.0 0.9 %collective-permute-start.15 = (bf16[72,384]{1,0:T(8,128)(2,1)S(1)}, bf16[72,384]{1,0:T(8,128)(2,1)S(1)}, u32[]{:S(2)}, u32[]{:S(2)}) collective-permute-start(bf16[72,384]{1,0:T(8,128)(2,1)S(1)} %fusion.8), channel_id=1, source_target_pairs={{0,2},{1,3},{2,0},{3,1},{4,6},{5,7},{6,4},{7,5},{8,10},{9,11},{10,... | collective-permute-start | bytes 165896 | tf_op jit(solution)/shard_map/ppermute | solution.py:354
  46.0 2.4 %collective-permute-done.19 = bf16[72,384]{1,0:T(8,128)(2,1)S(1)} collective-permute-done((bf16[72,384]{1,0:T(8,128)(2,1)S(1)}, bf16[72,384]{1,0:T(8,128)(2,1)S(1)}, u32[]{:S(2)}, u32[]{:S(2)}) %collective-permute-start.19) | collective-permute-done | bytes 55328 | tf_op jit(solution)/shard_map/ppermute | solution.py:354
  48.4 1.4 %collective-permute-start.20 = (bf16[72,384]{1,0:T(8,128)(2,1)S(1)}, bf16[72,384]{1,0:T(8,128)(2,1)S(1)}, u32[]{:S(2)}, u32[]{:S(2)}) collective-permute-start(bf16[72,384]{1,0:T(8,128)(2,1)S(1)} %fusion.13), channel_id=1, source_target_pairs={{0,4},{1,5},{2,6},{3,7},{4,0},{5,1},{6,2},{7,3},{8,12},{9,13},{10,... | collective-permute-start | bytes 165896 | tf_op jit(solution)/shard_map/ppermute | solution.py:354
  49.9 1.7 %collective-permute-start.16 = (bf16[72,384]{1,0:T(8,128)(2,1)S(1)}, bf16[72,384]{1,0:T(8,128)(2,1)S(1)}, u32[]{:S(2)}, u32[]{:S(2)}) collective-permute-start(bf16[72,384]{1,0:T(8,128)(2,1)S(1)} %fusion.12), channel_id=1, source_target_pairs={{0,4},{1,5},{2,6},{3,7},{4,0},{5,1},{6,2},{7,3},{8,12},{9,13},{10,... | collective-permute-start | bytes 165896 | tf_op jit(solution)/shard_map/ppermute | solution.py:354
  51.5 2.9 %collective-permute-done.20 = bf16[72,384]{1,0:T(8,128)(2,1)S(1)} collective-permute-done((bf16[72,384]{1,0:T(8,128)(2,1)S(1)}, bf16[72,384]{1,0:T(8,128)(2,1)S(1)}, u32[]{:S(2)}, u32[]{:S(2)}) %collective-permute-start.20) | collective-permute-done | bytes 55328 | tf_op jit(solution)/shard_map/ppermute | solution.py:354
  54.5 1.1 %collective-permute-start.21 = (bf16[72,384]{1,0:T(8,128)(2,1)S(1)}, bf16[72,384]{1,0:T(8,128)(2,1)S(1)}, u32[]{:S(2)}, u32[]{:S(2)}) collective-permute-start(bf16[72,384]{1,0:T(8,128)(2,1)S(1)} %add_convert_fusion.rest_0_), channel_id=1, source_target_pairs={{0,1},{1,0},{2,3},{3,2},{4,5},{5,4},{6,7},{7,6},{8,9},{9,8},{10,11... | collective-permute-start | bytes 165896 | tf_op jit(solution)/shard_map/ppermute | solution.py:354
  55.6 1.1 %collective-permute-start.17 = (bf16[72,384]{1,0:T(8,128)(2,1)S(1)}, bf16[72,384]{1,0:T(8,128)(2,1)S(1)}, u32[]{:S(2)}, u32[]{:S(2)}) collective-permute-start(bf16[72,384]{1,0:T(8,128)(2,1)S(1)} %add_convert_fusion.1.rest_1_), channel_id=1, source_target_pairs={{0,1},{1,0},{2,3},{3,2},{4,5},{5,4},{6,7},{7,6},{8,9},{9,8},{10,11... | collective-permute-start | bytes 165896 | tf_op jit(solution)/shard_map/ppermute | solution.py:354
  56.7 1.3 %gradient.3.rest_1_ = f32[1,384,1536]{2,1,0:T(8,128)} custom-call(bf16[384,256]{1,0:T(8,128)(2,1)S(1)} %get-tuple-element.33.own_ref, bf16[72,384]{1,0:T(8,128)(2,1)S(1)} %add_convert_fusion.rest_0_, bf16[72,384]{1,0:T(8,128)(2,1)S(1)} %add_convert_fusion.1.rest_1_), custom_call_target="tpu_custom_call" | custom-call | flops 150994944 | bytes 1179648 | tf_op jit(solution)/shard_map/gradient/pallas_call | solution.py:336
  58.7 1.1 %gradient.4.rest_1_ = f32[1,384,1536]{2,1,0:T(8,128)} custom-call(bf16[384,256]{1,0:T(8,128)(2,1)S(1)} %get-tuple-element.33.own_ref, bf16[72,384]{1,0:T(8,128)(2,1)S(1)} %collective-permute-done.21.rest_0_, f32[1,384,1536]{2,1,0:T(8,128)} %gradient.3.rest_1_), custom_call_target="tpu_custom_call", output_to_operand_aliasing={{}: (2, {})} | custom-call | flops 75497472 | bytes 589824 | tf_op jit(solution)/shard_map/gradient/pallas_call | solution.py:336
  59.8 1.1 %gradient.5 = f32[1,384,1536]{2,1,0:T(8,128)} custom-call(bf16[384,256]{1,0:T(8,128)(2,1)S(1)} %get-tuple-element.33.own_ref, bf16[72,384]{1,0:T(8,128)(2,1)S(1)} %collective-permute-done.17.rest_0_, f32[1,384,1536]{2,1,0:T(8,128)} %gradient.4.rest_1_), custom_call_target="tpu_custom_call", output_to_operand_aliasing={{}: (2, {})} | custom-call | flops 75497472 | bytes 589824 | tf_op jit(solution)/shard_map/gradient/pallas_call | solution.py:336
  (54 shorter events, 9.3 us)
Async XLA Ops:
  0.6 22.3 %copy-start.3 = (f32[1,3072]{1,0:T(1,128)S(1)}, f32[1,3072]{1,0:T(1,128)}, u32[]{:S(2)}) copy-start(f32[1,3072]{1,0:T(1,128)} %param.12) | copy-start | bytes 36868
  3.4 20.5 %copy-start.4 = (f32[384]{0:T(512)S(1)}, f32[384]{0:T(512)}, u32[]{:S(2)}) copy-start(f32[384]{0:T(512)} %param.10) | copy-start | bytes 4612
  3.5 20.5 %copy-start = (bf16[1,1536,64]{1,2,0:T(8,128)(2,1)S(1)}, bf16[1,1536,64]{1,2,0:T(8,128)(2,1)}, u32[]{:S(2)}) copy-start(bf16[1,1536,64]{1,2,0:T(8,128)(2,1)} %param.15) | copy-start | bytes 589828
  3.5 20.7 %copy-start.1 = (bf16[384,64]{0,1:T(8,128)(2,1)S(1)}, bf16[384,64]{0,1:T(8,128)(2,1)}, u32[]{:S(2)}) copy-start(bf16[384,64]{0,1:T(8,128)(2,1)} %param.8) | copy-start | bytes 147460
  3.5 5.2 %collective-permute-start = (bf16[72,384]{1,0:T(8,128)(2,1)S(1)}, bf16[72,384]{1,0:T(8,128)(2,1)S(1)}, u32[]{:S(2)}, u32[]{:S(2)}) collective-permute-start(bf16[72,384]{1,0:T(8,128)(2,1)S(1)} %get-tuple-element.25), channel_id=1, source_target_pairs={{0,1},{1,0},{2,3},{3,2},{4,5},{5,4},{6,7},{7,6},{8,9},{9,8},{10,11... | collective-permute-start | bytes 165896 | tf_op jit(solution)/shard_map/ppermute | solution.py:354
  6.5 19.8 %copy-start.2 = (bf16[384,64]{0,1:T(8,128)(2,1)S(1)}, bf16[384,64]{0,1:T(8,128)(2,1)}, u32[]{:S(2)}) copy-start(bf16[384,64]{0,1:T(8,128)(2,1)} %param.9) | copy-start | bytes 147460
  6.5 4.8 %collective-permute-start.3 = (bf16[72,384]{1,0:T(8,128)(2,1)S(1)}, bf16[72,384]{1,0:T(8,128)(2,1)S(1)}, u32[]{:S(2)}, u32[]{:S(2)}) collective-permute-start(bf16[72,384]{1,0:T(8,128)(2,1)S(1)} %get-tuple-element.27), channel_id=1, source_target_pairs={{0,1},{1,0},{2,3},{3,2},{4,5},{5,4},{6,7},{7,6},{8,9},{9,8},{10,11... | collective-permute-start | bytes 165896 | tf_op jit(solution)/shard_map/ppermute | solution.py:354
  8.7 4.8 %collective-permute-start.1 = (bf16[72,384]{1,0:T(8,128)(2,1)S(1)}, bf16[72,384]{1,0:T(8,128)(2,1)S(1)}, u32[]{:S(2)}, u32[]{:S(2)}) collective-permute-start(bf16[72,384]{1,0:T(8,128)(2,1)S(1)} %fusion.6), channel_id=1, source_target_pairs={{0,2},{1,3},{2,0},{3,1},{4,6},{5,7},{6,4},{7,5},{8,10},{9,11},{10,... | collective-permute-start | bytes 165896 | tf_op jit(solution)/shard_map/ppermute | solution.py:354
  11.3 5.6 %collective-permute-start.4 = (bf16[72,384]{1,0:T(8,128)(2,1)S(1)}, bf16[72,384]{1,0:T(8,128)(2,1)S(1)}, u32[]{:S(2)}, u32[]{:S(2)}) collective-permute-start(bf16[72,384]{1,0:T(8,128)(2,1)S(1)} %fusion.7), channel_id=1, source_target_pairs={{0,2},{1,3},{2,0},{3,1},{4,6},{5,7},{6,4},{7,5},{8,10},{9,11},{10,... | collective-permute-start | bytes 165896 | tf_op jit(solution)/shard_map/ppermute | solution.py:354
  13.5 5.6 %collective-permute-start.2 = (bf16[72,384]{1,0:T(8,128)(2,1)S(1)}, bf16[72,384]{1,0:T(8,128)(2,1)S(1)}, u32[]{:S(2)}, u32[]{:S(2)}) collective-permute-start(bf16[72,384]{1,0:T(8,128)(2,1)S(1)} %fusion.10), channel_id=1, source_target_pairs={{0,4},{1,5},{2,6},{3,7},{4,0},{5,1},{6,2},{7,3},{8,12},{9,13},{10,... | collective-permute-start | bytes 165896 | tf_op jit(solution)/shard_map/ppermute | solution.py:354
  16.9 5.1 %collective-permute-start.5 = (bf16[72,384]{1,0:T(8,128)(2,1)S(1)}, bf16[72,384]{1,0:T(8,128)(2,1)S(1)}, u32[]{:S(2)}, u32[]{:S(2)}) collective-permute-start(bf16[72,384]{1,0:T(8,128)(2,1)S(1)} %fusion.11), channel_id=1, source_target_pairs={{0,4},{1,5},{2,6},{3,7},{4,0},{5,1},{6,2},{7,3},{8,12},{9,13},{10,... | collective-permute-start | bytes 165896 | tf_op jit(solution)/shard_map/ppermute | solution.py:354
  19.1 5.9 %collective-permute-start.6 = (bf16[72,384]{1,0:T(8,128)(2,1)S(1)}, bf16[72,384]{1,0:T(8,128)(2,1)S(1)}, u32[]{:S(2)}, u32[]{:S(2)}) collective-permute-start(bf16[72,384]{1,0:T(8,128)(2,1)S(1)} %add_convert_fusion.3.rest_0_), channel_id=1, source_target_pairs={{0,1},{1,0},{2,3},{3,2},{4,5},{5,4},{6,7},{7,6},{8,9},{9,8},{10,11... | collective-permute-start | bytes 165896 | tf_op jit(solution)/shard_map/ppermute | solution.py:354
  22.1 4.2 %collective-permute-start.7 = (bf16[72,384]{1,0:T(8,128)(2,1)S(1)}, bf16[72,384]{1,0:T(8,128)(2,1)S(1)}, u32[]{:S(2)}, u32[]{:S(2)}) collective-permute-start(bf16[72,384]{1,0:T(8,128)(2,1)S(1)} %add_convert_fusion.2.rest_1_), channel_id=1, source_target_pairs={{0,1},{1,0},{2,3},{3,2},{4,5},{5,4},{6,7},{7,6},{8,9},{9,8},{10,11... | collective-permute-start | bytes 165896 | tf_op jit(solution)/shard_map/ppermute | solution.py:354
  27.1 4.5 %collective-permute-start.10 = (bf16[64,384]{1,0:T(8,128)(2,1)S(1)}, bf16[64,384]{1,0:T(8,128)(2,1)S(1)}, u32[]{:S(2)}, u32[]{:S(2)}) collective-permute-start(bf16[64,384]{1,0:T(8,128)(2,1)S(1)} %get-tuple-element.28.own_ref), channel_id=1, source_target_pairs={{0,16},{8,24},{16,0},{24,8},{1,17},{9,25},{17,1},{25,9},{2,18},{10... | collective-permute-start | bytes 147464 | tf_op jit(solution)/shard_map/ppermute | solution.py:354
  27.9 4.0 %collective-permute-start.9 = (bf16[64,384]{1,0:T(8,128)(2,1)S(1)}, bf16[64,384]{1,0:T(8,128)(2,1)S(1)}, u32[]{:S(2)}, u32[]{:S(2)}) collective-permute-start(bf16[64,384]{1,0:T(8,128)(2,1)S(1)} %get-tuple-element.28.own_ref), channel_id=1, source_target_pairs={{0,24},{8,16},{16,8},{24,0},{1,25},{9,17},{17,9},{25,1},{2,26},{10... | collective-permute-start | bytes 147464 | tf_op jit(solution)/shard_map/ppermute | solution.py:354
  27.9 4.0 %collective-permute-start.8 = (bf16[64,384]{1,0:T(8,128)(2,1)S(1)}, bf16[64,384]{1,0:T(8,128)(2,1)S(1)}, u32[]{:S(2)}, u32[]{:S(2)}) collective-permute-start(bf16[64,384]{1,0:T(8,128)(2,1)S(1)} %get-tuple-element.28.own_ref), channel_id=1, source_target_pairs={{0,8},{8,0},{16,24},{24,16},{1,9},{9,1},{17,25},{25,17},{2,10},{10... | collective-permute-start | bytes 147464 | tf_op jit(solution)/shard_map/ppermute | solution.py:354
  32.0 5.7 %collective-permute-start.13 = (bf16[64,384]{1,0:T(8,128)(2,1)S(1)}, bf16[64,384]{1,0:T(8,128)(2,1)S(1)}, u32[]{:S(2)}, u32[]{:S(2)}) collective-permute-start(bf16[64,384]{1,0:T(8,128)(2,1)S(1)} %get-tuple-element.34.piece_ref), channel_id=1, source_target_pairs={{0,16},{8,24},{16,0},{24,8},{1,17},{9,25},{17,1},{25,9},{2,18},{10... | collective-permute-start | bytes 147464 | tf_op jit(solution)/shard_map/ppermute | solution.py:354
  34.6 3.5 %collective-permute-start.12 = (bf16[64,384]{1,0:T(8,128)(2,1)S(1)}, bf16[64,384]{1,0:T(8,128)(2,1)S(1)}, u32[]{:S(2)}, u32[]{:S(2)}) collective-permute-start(bf16[64,384]{1,0:T(8,128)(2,1)S(1)} %get-tuple-element.34.piece_ref), channel_id=1, source_target_pairs={{0,24},{8,16},{16,8},{24,0},{1,25},{9,17},{17,9},{25,1},{2,26},{10... | collective-permute-start | bytes 147464 | tf_op jit(solution)/shard_map/ppermute | solution.py:354
  35.3 2.8 %collective-permute-start.11 = (bf16[64,384]{1,0:T(8,128)(2,1)S(1)}, bf16[64,384]{1,0:T(8,128)(2,1)S(1)}, u32[]{:S(2)}, u32[]{:S(2)}) collective-permute-start(bf16[64,384]{1,0:T(8,128)(2,1)S(1)} %get-tuple-element.34.piece_ref), channel_id=1, source_target_pairs={{0,8},{8,0},{16,24},{24,16},{1,9},{9,1},{17,25},{25,17},{2,10},{10... | collective-permute-start | bytes 147464 | tf_op jit(solution)/shard_map/ppermute | solution.py:354
  38.9 4.8 %collective-permute-start.18 = (bf16[72,384]{1,0:T(8,128)(2,1)S(1)}, bf16[72,384]{1,0:T(8,128)(2,1)S(1)}, u32[]{:S(2)}, u32[]{:S(2)}) collective-permute-start(bf16[72,384]{1,0:T(8,128)(2,1)S(1)} %get-tuple-element.44), channel_id=1, source_target_pairs={{0,1},{1,0},{2,3},{3,2},{4,5},{5,4},{6,7},{7,6},{8,9},{9,8},{10,11... | collective-permute-start | bytes 165896 | tf_op jit(solution)/shard_map/ppermute | solution.py:354
  39.7 5.3 %collective-permute-start.14 = (bf16[72,384]{1,0:T(8,128)(2,1)S(1)}, bf16[72,384]{1,0:T(8,128)(2,1)S(1)}, u32[]{:S(2)}, u32[]{:S(2)}) collective-permute-start(bf16[72,384]{1,0:T(8,128)(2,1)S(1)} %get-tuple-element.42), channel_id=1, source_target_pairs={{0,1},{1,0},{2,3},{3,2},{4,5},{5,4},{6,7},{7,6},{8,9},{9,8},{10,11... | collective-permute-start | bytes 165896 | tf_op jit(solution)/shard_map/ppermute | solution.py:354
  43.7 4.7 %collective-permute-start.19 = (bf16[72,384]{1,0:T(8,128)(2,1)S(1)}, bf16[72,384]{1,0:T(8,128)(2,1)S(1)}, u32[]{:S(2)}, u32[]{:S(2)}) collective-permute-start(bf16[72,384]{1,0:T(8,128)(2,1)S(1)} %fusion.9), channel_id=1, source_target_pairs={{0,2},{1,3},{2,0},{3,1},{4,6},{5,7},{6,4},{7,5},{8,10},{9,11},{10,... | collective-permute-start | bytes 165896 | tf_op jit(solution)/shard_map/ppermute | solution.py:354
  45.0 4.8 %collective-permute-start.15 = (bf16[72,384]{1,0:T(8,128)(2,1)S(1)}, bf16[72,384]{1,0:T(8,128)(2,1)S(1)}, u32[]{:S(2)}, u32[]{:S(2)}) collective-permute-start(bf16[72,384]{1,0:T(8,128)(2,1)S(1)} %fusion.8), channel_id=1, source_target_pairs={{0,2},{1,3},{2,0},{3,1},{4,6},{5,7},{6,4},{7,5},{8,10},{9,11},{10,... | collective-permute-start | bytes 165896 | tf_op jit(solution)/shard_map/ppermute | solution.py:354
  48.4 6.0 %collective-permute-start.20 = (bf16[72,384]{1,0:T(8,128)(2,1)S(1)}, bf16[72,384]{1,0:T(8,128)(2,1)S(1)}, u32[]{:S(2)}, u32[]{:S(2)}) collective-permute-start(bf16[72,384]{1,0:T(8,128)(2,1)S(1)} %fusion.13), channel_id=1, source_target_pairs={{0,4},{1,5},{2,6},{3,7},{4,0},{5,1},{6,2},{7,3},{8,12},{9,13},{10,... | collective-permute-start | bytes 165896 | tf_op jit(solution)/shard_map/ppermute | solution.py:354
  49.9 5.7 %collective-permute-start.16 = (bf16[72,384]{1,0:T(8,128)(2,1)S(1)}, bf16[72,384]{1,0:T(8,128)(2,1)S(1)}, u32[]{:S(2)}, u32[]{:S(2)}) collective-permute-start(bf16[72,384]{1,0:T(8,128)(2,1)S(1)} %fusion.12), channel_id=1, source_target_pairs={{0,4},{1,5},{2,6},{3,7},{4,0},{5,1},{6,2},{7,3},{8,12},{9,13},{10,... | collective-permute-start | bytes 165896 | tf_op jit(solution)/shard_map/ppermute | solution.py:354
  54.5 4.2 %collective-permute-start.21 = (bf16[72,384]{1,0:T(8,128)(2,1)S(1)}, bf16[72,384]{1,0:T(8,128)(2,1)S(1)}, u32[]{:S(2)}, u32[]{:S(2)}) collective-permute-start(bf16[72,384]{1,0:T(8,128)(2,1)S(1)} %add_convert_fusion.rest_0_), channel_id=1, source_target_pairs={{0,1},{1,0},{2,3},{3,2},{4,5},{5,4},{6,7},{7,6},{8,9},{9,8},{10,11... | collective-permute-start | bytes 165896 | tf_op jit(solution)/shard_map/ppermute | solution.py:354
  55.6 4.2 %collective-permute-start.17 = (bf16[72,384]{1,0:T(8,128)(2,1)S(1)}, bf16[72,384]{1,0:T(8,128)(2,1)S(1)}, u32[]{:S(2)}, u32[]{:S(2)}) collective-permute-start(bf16[72,384]{1,0:T(8,128)(2,1)S(1)} %add_convert_fusion.1.rest_1_), channel_id=1, source_target_pairs={{0,1},{1,0},{2,3},{3,2},{4,5},{5,4},{6,7},{7,6},{8,9},{9,8},{10,11... | collective-permute-start | bytes 165896 | tf_op jit(solution)/shard_map/ppermute | solution.py:354

commit v7 on v6

--- a/solution.py
+++ b/solution.py
@@ -424,7 +424,8 @@
         (own_first, by1, by3, by2, mix, gram, *proj, readout, columns),
         scratch=[pltpu.VMEM((cols, tokens), f32)],
     )
-    fake, adversarial, real = (swap(piece, "role", roles, bit) for bit in (2, 3, 1))
+    fake = lax.ppermute(piece, "role", [(2, 0)])
+    adversarial, real = (swap(piece, "role", roles, bit) for bit in (3, 1))
     own_turned, slope, scaled = call(
         functools.partial(slope_kernel, width=width),
         "slopes",

time: 61.1 us -> 60.7 us (level)
  waiting for transfers between devices: 16 us -> 14.7 us
  starting transfers between devices: 29.5 us -> 30.4 us
    ppermute x0 -> x1, starting transfers between devices: none -> 1.29 us  [shards(): fake = lax.ppermute(piece, 'role', [(2, 0)])]
    ppermute x22 -> x21, waiting for transfers between devices: 16 us -> 14.7 us  [swap(): return lax.ppermute(value, axis, [(i, i ^ bit) for i in range(n)])]
    ppermute x22 -> x21, starting transfers between devices: 29.5 us -> 29.1 us  [swap(): return lax.ppermute(value, axis, [(i, i ^ bit) for i in range(n)])]
where the time goes in v7:
time: 60.7 us; the launch traced here: 60.5 us
  starting transfers between devices  30.4 us (50%)
  waiting for transfers between devices  14.7 us (24%)
  Pallas kernels  10.2 us (17%)
  other arithmetic  3 us (5%)
  matrix products  0.98 us (2%)
  between operations  0.91 us (1%)
    ppermute x21, starting transfers between devices, swap(): return lax.ppermute(value, axis, [(i, i ^ bit) for i in range(n)])  29.1 us
    ppermute x21, waiting for transfers between devices, swap(): return lax.ppermute(value, axis, [(i, i ^ bit) for i in range(n)])  14.7 us
    pallas_call x6, Pallas kernels, call(): pl.pallas_call(kernel, out_shape=out_shape, in_specs=[vmem] * len(inputs)...  4.78 us
    pallas_call x3, Pallas kernels, gradient(): pl.pallas_call(functools.partial(grad_kernel, factor=factor, first_piece=...  3.41 us
    pallas_call x1, Pallas kernels, part_of(): pl.pallas_call(part_kernel, out_shape=shapes, in_specs=[hbm, vmem, hbm],...  1.99 us
    ppermute x1, starting transfers between devices, shards(): fake = lax.ppermute(piece, 'role', [(2, 0)])  1.29 us
  transfers between devices with their start and end apart: 22, of which 12 were waited for; matrix products, arithmetic and copies ran while one was open for 6% of the time, Pallas kernels for 9%

profile of v7, /device:TPU:0, one launch (start us, length us, event | category | flops | bytes accessed | tf_op | source)
XLA Modules:
  0.0 60.5 jit_solution(7345902306484643411)
XLA Ops:
  1.4 2.0 %part.1 = (f32[72,384]{1,0:T(8,128)S(1)}, f32[72,384]{1,0:T(8,128)S(1)}, bf16[72,384]{1,0:T(8,128)(2,1)S(1)}, bf16[72,384]{1,0:T(8,128)(2,1)S(1)}, bf16[144,384]{1,0:T(8,128)(2,1)S(1)}) custom-call(bf16[64,3072]{1,0:T(8,128)(2,1)} %bitcast.22, f32[2,3072]{1,0:T(2,128)S(1)} %pad_maximum_fusion.vectors_ref, bf16[1,384,1536]{2,1,0:T(8,128)(2,1)} %block_ref.1), custom_call_target="tpu_custom_call" | custom-call | flops 169869312 | bytes 1179648 | tf_op jit(solution)/shard_map/part/pallas_call | solution.py:309
  3.5 3.0 %collective-permute-start = (bf16[72,384]{1,0:T(8,128)(2,1)S(1)}, bf16[72,384]{1,0:T(8,128)(2,1)S(1)}, u32[]{:S(2)}, u32[]{:S(2)}) collective-permute-start(bf16[72,384]{1,0:T(8,128)(2,1)S(1)} %get-tuple-element.25), channel_id=1, source_target_pairs={{0,1},{1,0},{2,3},{3,2},{4,5},{5,4},{6,7},{7,6},{8,9},{9,8},{10,11... | collective-permute-start | bytes 165896 | tf_op jit(solution)/shard_map/ppermute | solution.py:354
  6.6 1.0 %bitcast_convert_fusion = f32[64,3072]{1,0:T(8,128)S(1)} fusion(bf16[1,64,3072]{2,1,0:T(8,128)(2,1)} %param.11), kind=kLoop, calls=%fused_computation.30 | loop fusion | flops 196608 | bytes 1179648 | tf_op jit(solution)/shard_map/convert_element_type | solution.py:396
  7.7 0.9 %collective-permute-done = bf16[72,384]{1,0:T(8,128)(2,1)S(1)} collective-permute-done((bf16[72,384]{1,0:T(8,128)(2,1)S(1)}, bf16[72,384]{1,0:T(8,128)(2,1)S(1)}, u32[]{:S(2)}, u32[]{:S(2)}) %collective-permute-start) | collective-permute-done | bytes 55328 | tf_op jit(solution)/shard_map/ppermute | solution.py:354
  8.7 2.6 %collective-permute-start.1 = (bf16[72,384]{1,0:T(8,128)(2,1)S(1)}, bf16[72,384]{1,0:T(8,128)(2,1)S(1)}, u32[]{:S(2)}, u32[]{:S(2)}) collective-permute-start(bf16[72,384]{1,0:T(8,128)(2,1)S(1)} %fusion.6), channel_id=1, source_target_pairs={{0,2},{1,3},{2,0},{3,1},{4,6},{5,7},{6,4},{7,5},{8,10},{9,11},{10,... | collective-permute-start | bytes 165896 | tf_op jit(solution)/shard_map/ppermute | solution.py:354
  11.3 1.0 %collective-permute-start.4 = (bf16[72,384]{1,0:T(8,128)(2,1)S(1)}, bf16[72,384]{1,0:T(8,128)(2,1)S(1)}, u32[]{:S(2)}, u32[]{:S(2)}) collective-permute-start(bf16[72,384]{1,0:T(8,128)(2,1)S(1)} %fusion.7), channel_id=1, source_target_pairs={{0,2},{1,3},{2,0},{3,1},{4,6},{5,7},{6,4},{7,5},{8,10},{9,11},{10,... | collective-permute-start | bytes 165896 | tf_op jit(solution)/shard_map/ppermute | solution.py:354
  12.3 1.1 %collective-permute-done.1 = bf16[72,384]{1,0:T(8,128)(2,1)S(1)} collective-permute-done((bf16[72,384]{1,0:T(8,128)(2,1)S(1)}, bf16[72,384]{1,0:T(8,128)(2,1)S(1)}, u32[]{:S(2)}, u32[]{:S(2)}) %collective-permute-start.1) | collective-permute-done | bytes 55328 | tf_op jit(solution)/shard_map/ppermute | solution.py:354
  13.5 3.4 %collective-permute-start.2 = (bf16[72,384]{1,0:T(8,128)(2,1)S(1)}, bf16[72,384]{1,0:T(8,128)(2,1)S(1)}, u32[]{:S(2)}, u32[]{:S(2)}) collective-permute-start(bf16[72,384]{1,0:T(8,128)(2,1)S(1)} %fusion.10), channel_id=1, source_target_pairs={{0,4},{1,5},{2,6},{3,7},{4,0},{5,1},{6,2},{7,3},{8,12},{9,13},{10,... | collective-permute-start | bytes 165896 | tf_op jit(solution)/shard_map/ppermute | solution.py:354
  16.9 1.3 %collective-permute-start.5 = (bf16[72,384]{1,0:T(8,128)(2,1)S(1)}, bf16[72,384]{1,0:T(8,128)(2,1)S(1)}, u32[]{:S(2)}, u32[]{:S(2)}) collective-permute-start(bf16[72,384]{1,0:T(8,128)(2,1)S(1)} %fusion.11), channel_id=1, source_target_pairs={{0,4},{1,5},{2,6},{3,7},{4,0},{5,1},{6,2},{7,3},{8,12},{9,13},{10,... | collective-permute-start | bytes 165896 | tf_op jit(solution)/shard_map/ppermute | solution.py:354
  18.2 0.9 %collective-permute-done.2 = bf16[72,384]{1,0:T(8,128)(2,1)S(1)} collective-permute-done((bf16[72,384]{1,0:T(8,128)(2,1)S(1)}, bf16[72,384]{1,0:T(8,128)(2,1)S(1)}, u32[]{:S(2)}, u32[]{:S(2)}) %collective-permute-start.2) | collective-permute-done | bytes 55328 | tf_op jit(solution)/shard_map/ppermute | solution.py:354
  19.1 2.2 %collective-permute-start.6 = (bf16[72,384]{1,0:T(8,128)(2,1)S(1)}, bf16[72,384]{1,0:T(8,128)(2,1)S(1)}, u32[]{:S(2)}, u32[]{:S(2)}) collective-permute-start(bf16[72,384]{1,0:T(8,128)(2,1)S(1)} %add_convert_fusion.3.rest_0_), channel_id=1, source_target_pairs={{0,1},{1,0},{2,3},{3,2},{4,5},{5,4},{6,7},{7,6},{8,9},{9,8},{10,11... | collective-permute-start | bytes 165896 | tf_op jit(solution)/shard_map/ppermute | solution.py:354
  22.9 1.0 %fusion.gram_ref = f32[72,72]{1,0:T(8,128)S(1)} fusion(f32[3,3072]{1,0:T(4,128)S(1)} %broadcast_in_dim.15, f32[64,3072]{1,0:T(8,128)S(1)} %bitcast_convert_fusion, f32[72]{0:T(128)S(1)} %pad.6.clone), kind=kOutput, calls=%fused_computation | convolution fusion | flops 191545344 | bytes 844320 | tf_op jit(solution)/shard_map/dot_general | solution.py:398
  24.2 0.9 %generator_early.1.total_ref = f32[72,384]{1,0:T(8,128)S(1)} custom-call(bf16[64,384]{1,0:T(8,128)(2,1)S(1)} %bitcast.17, f32[72,72]{1,0:T(8,128)S(1)} %fusion.gram_ref, bf16[72,384]{1,0:T(8,128)(2,1)S(1)} %add_convert_fusion.3.rest_0_, bf16[72,384]{1,0:T(8,128)(2,1)S(1)} %add_convert_fusion.2.rest_1_, bf16[64,1536]{1,0:T(8,128)(2,1)S(1)} %bitcast.14), custom_call_target="tpu_custom_call" | custom-call | flops 84934656 | bytes 84934 | tf_op jit(solution)/shard_map/generator_early/pallas_call | solution.py:284
  25.0 1.3 %collective-permute-done.7.rest_1_.rest_3_ = bf16[72,384]{1,0:T(8,128)(2,1)S(1)} collective-permute-done((bf16[72,384]{1,0:T(8,128)(2,1)S(1)}, bf16[72,384]{1,0:T(8,128)(2,1)S(1)}, u32[]{:S(2)}, u32[]{:S(2)}) %collective-permute-start.7) | collective-permute-done | bytes 55328 | tf_op jit(solution)/shard_map/ppermute | solution.py:354
  27.9 1.4 %collective-permute-start.8 = (bf16[64,384]{1,0:T(8,128)(2,1)S(1)}, bf16[64,384]{1,0:T(8,128)(2,1)S(1)}, u32[]{:S(2)}, u32[]{:S(2)}) collective-permute-start(bf16[64,384]{1,0:T(8,128)(2,1)S(1)} %get-tuple-element.28.own_ref), channel_id=1, source_target_pairs={{0,8},{8,0},{16,24},{24,16},{1,9},{9,1},{17,25},{25,17},{2,10},{10... | collective-permute-start | bytes 147464 | tf_op jit(solution)/shard_map/ppermute | solution.py:354
  29.5 2.1 %collective-permute-done.10.by2_ref = bf16[64,384]{1,0:T(8,128)(2,1)S(1)} collective-permute-done((bf16[64,384]{1,0:T(8,128)(2,1)S(1)}, bf16[64,384]{1,0:T(8,128)(2,1)S(1)}, u32[]{:S(2)}, u32[]{:S(2)}) %collective-permute-start.10) | collective-permute-done | bytes 49184 | tf_op jit(solution)/shard_map/ppermute | solution.py:354
  32.0 1.3 %collective-permute-start.13 = (bf16[64,384]{1,0:T(8,128)(2,1)S(1)}, bf16[64,384]{1,0:T(8,128)(2,1)S(1)}, u32[]{:S(2)}, u32[]{:S(2)}) collective-permute-start(bf16[64,384]{1,0:T(8,128)(2,1)S(1)} %get-tuple-element.34.piece_ref), channel_id=1, source_target_pairs={{16,0},{17,1},{18,2},{19,3},{20,4},{21,5},{22,6},{23,7}} | collective-permute-start | bytes 147464 | tf_op jit(solution)/shard_map/ppermute | solution.py:427
  33.3 2.6 %collective-permute-start.12 = (bf16[64,384]{1,0:T(8,128)(2,1)S(1)}, bf16[64,384]{1,0:T(8,128)(2,1)S(1)}, u32[]{:S(2)}, u32[]{:S(2)}) collective-permute-start(bf16[64,384]{1,0:T(8,128)(2,1)S(1)} %get-tuple-element.34.piece_ref), channel_id=1, source_target_pairs={{0,24},{8,16},{16,8},{24,0},{1,25},{9,17},{17,9},{25,1},{2,26},{10... | collective-permute-start | bytes 147464 | tf_op jit(solution)/shard_map/ppermute | solution.py:354
  36.8 1.7 %slopes.1 = (bf16[384,256]{1,0:T(8,128)(2,1)S(1)}, f32[1536,384]{1,0:T(8,128)S(1)}, bf16[144,384]{1,0:T(8,128)(2,1)S(1)}) custom-call(bf16[64,384]{1,0:T(8,128)(2,1)S(1)} %bitcast.19, f32[72,384]{1,0:T(8,128)S(1)} %get-tuple-element.31.scaled_in_ref, f32[72,72]{1,0:T(8,128)S(1)} %get-tuple-element.30.gram_ref, ...), custom_call_target="tpu_custom_call" | custom-call | flops 84934656 | bytes 84934 | tf_op jit(solution)/shard_map/slopes/pallas_call | solution.py:284
  40.0 1.3 %collective-permute-start.14 = (bf16[72,384]{1,0:T(8,128)(2,1)S(1)}, bf16[72,384]{1,0:T(8,128)(2,1)S(1)}, u32[]{:S(2)}, u32[]{:S(2)}) collective-permute-start(bf16[72,384]{1,0:T(8,128)(2,1)S(1)} %get-tuple-element.42), channel_id=1, source_target_pairs={{0,1},{1,0},{2,3},{3,2},{4,5},{5,4},{6,7},{7,6},{8,9},{9,8},{10,11... | collective-permute-start | bytes 165896 | tf_op jit(solution)/shard_map/ppermute | solution.py:354
  42.0 2.0 %collective-permute-done.18 = bf16[72,384]{1,0:T(8,128)(2,1)S(1)} collective-permute-done((bf16[72,384]{1,0:T(8,128)(2,1)S(1)}, bf16[72,384]{1,0:T(8,128)(2,1)S(1)}, u32[]{:S(2)}, u32[]{:S(2)}) %collective-permute-start.18) | collective-permute-done | bytes 55328 | tf_op jit(solution)/shard_map/ppermute | solution.py:354
  44.0 1.2 %collective-permute-start.19 = (bf16[72,384]{1,0:T(8,128)(2,1)S(1)}, bf16[72,384]{1,0:T(8,128)(2,1)S(1)}, u32[]{:S(2)}, u32[]{:S(2)}) collective-permute-start(bf16[72,384]{1,0:T(8,128)(2,1)S(1)} %fusion.9), channel_id=1, source_target_pairs={{0,2},{1,3},{2,0},{3,1},{4,6},{5,7},{6,4},{7,5},{8,10},{9,11},{10,... | collective-permute-start | bytes 165896 | tf_op jit(solution)/shard_map/ppermute | solution.py:354
  45.2 1.0 %collective-permute-start.15 = (bf16[72,384]{1,0:T(8,128)(2,1)S(1)}, bf16[72,384]{1,0:T(8,128)(2,1)S(1)}, u32[]{:S(2)}, u32[]{:S(2)}) collective-permute-start(bf16[72,384]{1,0:T(8,128)(2,1)S(1)} %fusion.8), channel_id=1, source_target_pairs={{0,2},{1,3},{2,0},{3,1},{4,6},{5,7},{6,4},{7,5},{8,10},{9,11},{10,... | collective-permute-start | bytes 165896 | tf_op jit(solution)/shard_map/ppermute | solution.py:354
  46.2 2.0 %collective-permute-done.19 = bf16[72,384]{1,0:T(8,128)(2,1)S(1)} collective-permute-done((bf16[72,384]{1,0:T(8,128)(2,1)S(1)}, bf16[72,384]{1,0:T(8,128)(2,1)S(1)}, u32[]{:S(2)}, u32[]{:S(2)}) %collective-permute-start.19) | collective-permute-done | bytes 55328 | tf_op jit(solution)/shard_map/ppermute | solution.py:354
  48.2 1.3 %collective-permute-start.20 = (bf16[72,384]{1,0:T(8,128)(2,1)S(1)}, bf16[72,384]{1,0:T(8,128)(2,1)S(1)}, u32[]{:S(2)}, u32[]{:S(2)}) collective-permute-start(bf16[72,384]{1,0:T(8,128)(2,1)S(1)} %fusion.13), channel_id=1, source_target_pairs={{0,4},{1,5},{2,6},{3,7},{4,0},{5,1},{6,2},{7,3},{8,12},{9,13},{10,... | collective-permute-start | bytes 165896 | tf_op jit(solution)/shard_map/ppermute | solution.py:354
  50.0 1.7 %collective-permute-start.16 = (bf16[72,384]{1,0:T(8,128)(2,1)S(1)}, bf16[72,384]{1,0:T(8,128)(2,1)S(1)}, u32[]{:S(2)}, u32[]{:S(2)}) collective-permute-start(bf16[72,384]{1,0:T(8,128)(2,1)S(1)} %fusion.12), channel_id=1, source_target_pairs={{0,4},{1,5},{2,6},{3,7},{4,0},{5,1},{6,2},{7,3},{8,12},{9,13},{10,... | collective-permute-start | bytes 165896 | tf_op jit(solution)/shard_map/ppermute | solution.py:354
  51.8 1.6 %collective-permute-done.20 = bf16[72,384]{1,0:T(8,128)(2,1)S(1)} collective-permute-done((bf16[72,384]{1,0:T(8,128)(2,1)S(1)}, bf16[72,384]{1,0:T(8,128)(2,1)S(1)}, u32[]{:S(2)}, u32[]{:S(2)}) %collective-permute-start.20) | collective-permute-done | bytes 55328 | tf_op jit(solution)/shard_map/ppermute | solution.py:354
  53.9 1.2 %collective-permute-done.16 = bf16[72,384]{1,0:T(8,128)(2,1)S(1)} collective-permute-done((bf16[72,384]{1,0:T(8,128)(2,1)S(1)}, bf16[72,384]{1,0:T(8,128)(2,1)S(1)}, u32[]{:S(2)}, u32[]{:S(2)}) %collective-permute-start.16) | collective-permute-done | bytes 55328 | tf_op jit(solution)/shard_map/ppermute | solution.py:354
  55.2 1.8 %collective-permute-start.17 = (bf16[72,384]{1,0:T(8,128)(2,1)S(1)}, bf16[72,384]{1,0:T(8,128)(2,1)S(1)}, u32[]{:S(2)}, u32[]{:S(2)}) collective-permute-start(bf16[72,384]{1,0:T(8,128)(2,1)S(1)} %add_convert_fusion.1.rest_1_), channel_id=1, source_target_pairs={{0,1},{1,0},{2,3},{3,2},{4,5},{5,4},{6,7},{7,6},{8,9},{9,8},{10,11... | collective-permute-start | bytes 165896 | tf_op jit(solution)/shard_map/ppermute | solution.py:354
  57.0 1.3 %gradient.3.rest_1_ = f32[1,384,1536]{2,1,0:T(8,128)} custom-call(bf16[384,256]{1,0:T(8,128)(2,1)S(1)} %get-tuple-element.33.own_ref, bf16[72,384]{1,0:T(8,128)(2,1)S(1)} %add_convert_fusion.rest_0_, bf16[72,384]{1,0:T(8,128)(2,1)S(1)} %add_convert_fusion.1.rest_1_), custom_call_target="tpu_custom_call" | custom-call | flops 150994944 | bytes 1179648 | tf_op jit(solution)/shard_map/gradient/pallas_call | solution.py:336
  58.3 1.1 %gradient.4.rest_1_ = f32[1,384,1536]{2,1,0:T(8,128)} custom-call(bf16[384,256]{1,0:T(8,128)(2,1)S(1)} %get-tuple-element.33.own_ref, bf16[72,384]{1,0:T(8,128)(2,1)S(1)} %collective-permute-done.21.rest_0_, f32[1,384,1536]{2,1,0:T(8,128)} %gradient.3.rest_1_), custom_call_target="tpu_custom_call", output_to_operand_aliasing={{}: (2, {})} | custom-call | flops 75497472 | bytes 589824 | tf_op jit(solution)/shard_map/gradient/pallas_call | solution.py:336
  59.4 1.1 %gradient.5 = f32[1,384,1536]{2,1,0:T(8,128)} custom-call(bf16[384,256]{1,0:T(8,128)(2,1)S(1)} %get-tuple-element.33.own_ref, bf16[72,384]{1,0:T(8,128)(2,1)S(1)} %collective-permute-done.17.rest_0_, f32[1,384,1536]{2,1,0:T(8,128)} %gradient.4.rest_1_), custom_call_target="tpu_custom_call", output_to_operand_aliasing={{}: (2, {})} | custom-call | flops 75497472 | bytes 589824 | tf_op jit(solution)/shard_map/gradient/pallas_call | solution.py:336
  (54 shorter events, 9.3 us)
Async XLA Ops:
  0.6 22.3 %copy-start.3 = (f32[1,3072]{1,0:T(1,128)S(1)}, f32[1,3072]{1,0:T(1,128)}, u32[]{:S(2)}) copy-start(f32[1,3072]{1,0:T(1,128)} %param.12) | copy-start | bytes 36868
  3.4 20.5 %copy-start.4 = (f32[384]{0:T(512)S(1)}, f32[384]{0:T(512)}, u32[]{:S(2)}) copy-start(f32[384]{0:T(512)} %param.10) | copy-start | bytes 4612
  3.5 20.5 %copy-start = (bf16[1,1536,64]{1,2,0:T(8,128)(2,1)S(1)}, bf16[1,1536,64]{1,2,0:T(8,128)(2,1)}, u32[]{:S(2)}) copy-start(bf16[1,1536,64]{1,2,0:T(8,128)(2,1)} %param.15) | copy-start | bytes 589828
  3.5 20.7 %copy-start.1 = (bf16[384,64]{0,1:T(8,128)(2,1)S(1)}, bf16[384,64]{0,1:T(8,128)(2,1)}, u32[]{:S(2)}) copy-start(bf16[384,64]{0,1:T(8,128)(2,1)} %param.8) | copy-start | bytes 147460
  3.5 5.2 %collective-permute-start = (bf16[72,384]{1,0:T(8,128)(2,1)S(1)}, bf16[72,384]{1,0:T(8,128)(2,1)S(1)}, u32[]{:S(2)}, u32[]{:S(2)}) collective-permute-start(bf16[72,384]{1,0:T(8,128)(2,1)S(1)} %get-tuple-element.25), channel_id=1, source_target_pairs={{0,1},{1,0},{2,3},{3,2},{4,5},{5,4},{6,7},{7,6},{8,9},{9,8},{10,11... | collective-permute-start | bytes 165896 | tf_op jit(solution)/shard_map/ppermute | solution.py:354
  6.5 19.8 %copy-start.2 = (bf16[384,64]{0,1:T(8,128)(2,1)S(1)}, bf16[384,64]{0,1:T(8,128)(2,1)}, u32[]{:S(2)}) copy-start(bf16[384,64]{0,1:T(8,128)(2,1)} %param.9) | copy-start | bytes 147460
  6.5 4.8 %collective-permute-start.3 = (bf16[72,384]{1,0:T(8,128)(2,1)S(1)}, bf16[72,384]{1,0:T(8,128)(2,1)S(1)}, u32[]{:S(2)}, u32[]{:S(2)}) collective-permute-start(bf16[72,384]{1,0:T(8,128)(2,1)S(1)} %get-tuple-element.27), channel_id=1, source_target_pairs={{0,1},{1,0},{2,3},{3,2},{4,5},{5,4},{6,7},{7,6},{8,9},{9,8},{10,11... | collective-permute-start | bytes 165896 | tf_op jit(solution)/shard_map/ppermute | solution.py:354
  8.7 4.8 %collective-permute-start.1 = (bf16[72,384]{1,0:T(8,128)(2,1)S(1)}, bf16[72,384]{1,0:T(8,128)(2,1)S(1)}, u32[]{:S(2)}, u32[]{:S(2)}) collective-permute-start(bf16[72,384]{1,0:T(8,128)(2,1)S(1)} %fusion.6), channel_id=1, source_target_pairs={{0,2},{1,3},{2,0},{3,1},{4,6},{5,7},{6,4},{7,5},{8,10},{9,11},{10,... | collective-permute-start | bytes 165896 | tf_op jit(solution)/shard_map/ppermute | solution.py:354
  11.3 5.6 %collective-permute-start.4 = (bf16[72,384]{1,0:T(8,128)(2,1)S(1)}, bf16[72,384]{1,0:T(8,128)(2,1)S(1)}, u32[]{:S(2)}, u32[]{:S(2)}) collective-permute-start(bf16[72,384]{1,0:T(8,128)(2,1)S(1)} %fusion.7), channel_id=1, source_target_pairs={{0,2},{1,3},{2,0},{3,1},{4,6},{5,7},{6,4},{7,5},{8,10},{9,11},{10,... | collective-permute-start | bytes 165896 | tf_op jit(solution)/shard_map/ppermute | solution.py:354
  13.5 5.6 %collective-permute-start.2 = (bf16[72,384]{1,0:T(8,128)(2,1)S(1)}, bf16[72,384]{1,0:T(8,128)(2,1)S(1)}, u32[]{:S(2)}, u32[]{:S(2)}) collective-permute-start(bf16[72,384]{1,0:T(8,128)(2,1)S(1)} %fusion.10), channel_id=1, source_target_pairs={{0,4},{1,5},{2,6},{3,7},{4,0},{5,1},{6,2},{7,3},{8,12},{9,13},{10,... | collective-permute-start | bytes 165896 | tf_op jit(solution)/shard_map/ppermute | solution.py:354
  16.9 5.1 %collective-permute-start.5 = (bf16[72,384]{1,0:T(8,128)(2,1)S(1)}, bf16[72,384]{1,0:T(8,128)(2,1)S(1)}, u32[]{:S(2)}, u32[]{:S(2)}) collective-permute-start(bf16[72,384]{1,0:T(8,128)(2,1)S(1)} %fusion.11), channel_id=1, source_target_pairs={{0,4},{1,5},{2,6},{3,7},{4,0},{5,1},{6,2},{7,3},{8,12},{9,13},{10,... | collective-permute-start | bytes 165896 | tf_op jit(solution)/shard_map/ppermute | solution.py:354
  19.1 5.9 %collective-permute-start.6 = (bf16[72,384]{1,0:T(8,128)(2,1)S(1)}, bf16[72,384]{1,0:T(8,128)(2,1)S(1)}, u32[]{:S(2)}, u32[]{:S(2)}) collective-permute-start(bf16[72,384]{1,0:T(8,128)(2,1)S(1)} %add_convert_fusion.3.rest_0_), channel_id=1, source_target_pairs={{0,1},{1,0},{2,3},{3,2},{4,5},{5,4},{6,7},{7,6},{8,9},{9,8},{10,11... | collective-permute-start | bytes 165896 | tf_op jit(solution)/shard_map/ppermute | solution.py:354
  22.1 4.2 %collective-permute-start.7 = (bf16[72,384]{1,0:T(8,128)(2,1)S(1)}, bf16[72,384]{1,0:T(8,128)(2,1)S(1)}, u32[]{:S(2)}, u32[]{:S(2)}) collective-permute-start(bf16[72,384]{1,0:T(8,128)(2,1)S(1)} %add_convert_fusion.2.rest_1_), channel_id=1, source_target_pairs={{0,1},{1,0},{2,3},{3,2},{4,5},{5,4},{6,7},{7,6},{8,9},{9,8},{10,11... | collective-permute-start | bytes 165896 | tf_op jit(solution)/shard_map/ppermute | solution.py:354
  27.1 4.5 %collective-permute-start.10 = (bf16[64,384]{1,0:T(8,128)(2,1)S(1)}, bf16[64,384]{1,0:T(8,128)(2,1)S(1)}, u32[]{:S(2)}, u32[]{:S(2)}) collective-permute-start(bf16[64,384]{1,0:T(8,128)(2,1)S(1)} %get-tuple-element.28.own_ref), channel_id=1, source_target_pairs={{0,16},{8,24},{16,0},{24,8},{1,17},{9,25},{17,1},{25,9},{2,18},{10... | collective-permute-start | bytes 147464 | tf_op jit(solution)/shard_map/ppermute | solution.py:354
  27.9 4.0 %collective-permute-start.9 = (bf16[64,384]{1,0:T(8,128)(2,1)S(1)}, bf16[64,384]{1,0:T(8,128)(2,1)S(1)}, u32[]{:S(2)}, u32[]{:S(2)}) collective-permute-start(bf16[64,384]{1,0:T(8,128)(2,1)S(1)} %get-tuple-element.28.own_ref), channel_id=1, source_target_pairs={{0,24},{8,16},{16,8},{24,0},{1,25},{9,17},{17,9},{25,1},{2,26},{10... | collective-permute-start | bytes 147464 | tf_op jit(solution)/shard_map/ppermute | solution.py:354
  27.9 4.0 %collective-permute-start.8 = (bf16[64,384]{1,0:T(8,128)(2,1)S(1)}, bf16[64,384]{1,0:T(8,128)(2,1)S(1)}, u32[]{:S(2)}, u32[]{:S(2)}) collective-permute-start(bf16[64,384]{1,0:T(8,128)(2,1)S(1)} %get-tuple-element.28.own_ref), channel_id=1, source_target_pairs={{0,8},{8,0},{16,24},{24,16},{1,9},{9,1},{17,25},{25,17},{2,10},{10... | collective-permute-start | bytes 147464 | tf_op jit(solution)/shard_map/ppermute | solution.py:354
  32.0 6.4 %collective-permute-start.13 = (bf16[64,384]{1,0:T(8,128)(2,1)S(1)}, bf16[64,384]{1,0:T(8,128)(2,1)S(1)}, u32[]{:S(2)}, u32[]{:S(2)}) collective-permute-start(bf16[64,384]{1,0:T(8,128)(2,1)S(1)} %get-tuple-element.34.piece_ref), channel_id=1, source_target_pairs={{16,0},{17,1},{18,2},{19,3},{20,4},{21,5},{22,6},{23,7}} | collective-permute-start | bytes 147464 | tf_op jit(solution)/shard_map/ppermute | solution.py:427
  33.3 5.1 %collective-permute-start.12 = (bf16[64,384]{1,0:T(8,128)(2,1)S(1)}, bf16[64,384]{1,0:T(8,128)(2,1)S(1)}, u32[]{:S(2)}, u32[]{:S(2)}) collective-permute-start(bf16[64,384]{1,0:T(8,128)(2,1)S(1)} %get-tuple-element.34.piece_ref), channel_id=1, source_target_pairs={{0,24},{8,16},{16,8},{24,0},{1,25},{9,17},{17,9},{25,1},{2,26},{10... | collective-permute-start | bytes 147464 | tf_op jit(solution)/shard_map/ppermute | solution.py:354
  35.9 2.5 %collective-permute-start.11 = (bf16[64,384]{1,0:T(8,128)(2,1)S(1)}, bf16[64,384]{1,0:T(8,128)(2,1)S(1)}, u32[]{:S(2)}, u32[]{:S(2)}) collective-permute-start(bf16[64,384]{1,0:T(8,128)(2,1)S(1)} %get-tuple-element.34.piece_ref), channel_id=1, source_target_pairs={{0,8},{8,0},{16,24},{24,16},{1,9},{9,1},{17,25},{25,17},{2,10},{10... | collective-permute-start | bytes 147464 | tf_op jit(solution)/shard_map/ppermute | solution.py:354
  39.2 4.8 %collective-permute-start.18 = (bf16[72,384]{1,0:T(8,128)(2,1)S(1)}, bf16[72,384]{1,0:T(8,128)(2,1)S(1)}, u32[]{:S(2)}, u32[]{:S(2)}) collective-permute-start(bf16[72,384]{1,0:T(8,128)(2,1)S(1)} %get-tuple-element.44), channel_id=1, source_target_pairs={{0,1},{1,0},{2,3},{3,2},{4,5},{5,4},{6,7},{7,6},{8,9},{9,8},{10,11... | collective-permute-start | bytes 165896 | tf_op jit(solution)/shard_map/ppermute | solution.py:354
  40.0 5.2 %collective-permute-start.14 = (bf16[72,384]{1,0:T(8,128)(2,1)S(1)}, bf16[72,384]{1,0:T(8,128)(2,1)S(1)}, u32[]{:S(2)}, u32[]{:S(2)}) collective-permute-start(bf16[72,384]{1,0:T(8,128)(2,1)S(1)} %get-tuple-element.42), channel_id=1, source_target_pairs={{0,1},{1,0},{2,3},{3,2},{4,5},{5,4},{6,7},{7,6},{8,9},{9,8},{10,11... | collective-permute-start | bytes 165896 | tf_op jit(solution)/shard_map/ppermute | solution.py:354
  44.0 4.2 %collective-permute-start.19 = (bf16[72,384]{1,0:T(8,128)(2,1)S(1)}, bf16[72,384]{1,0:T(8,128)(2,1)S(1)}, u32[]{:S(2)}, u32[]{:S(2)}) collective-permute-start(bf16[72,384]{1,0:T(8,128)(2,1)S(1)} %fusion.9), channel_id=1, source_target_pairs={{0,2},{1,3},{2,0},{3,1},{4,6},{5,7},{6,4},{7,5},{8,10},{9,11},{10,... | collective-permute-start | bytes 165896 | tf_op jit(solution)/shard_map/ppermute | solution.py:354
  45.2 4.8 %collective-permute-start.15 = (bf16[72,384]{1,0:T(8,128)(2,1)S(1)}, bf16[72,384]{1,0:T(8,128)(2,1)S(1)}, u32[]{:S(2)}, u32[]{:S(2)}) collective-permute-start(bf16[72,384]{1,0:T(8,128)(2,1)S(1)} %fusion.8), channel_id=1, source_target_pairs={{0,2},{1,3},{2,0},{3,1},{4,6},{5,7},{6,4},{7,5},{8,10},{9,11},{10,... | collective-permute-start | bytes 165896 | tf_op jit(solution)/shard_map/ppermute | solution.py:354
  48.2 5.1 %collective-permute-start.20 = (bf16[72,384]{1,0:T(8,128)(2,1)S(1)}, bf16[72,384]{1,0:T(8,128)(2,1)S(1)}, u32[]{:S(2)}, u32[]{:S(2)}) collective-permute-start(bf16[72,384]{1,0:T(8,128)(2,1)S(1)} %fusion.13), channel_id=1, source_target_pairs={{0,4},{1,5},{2,6},{3,7},{4,0},{5,1},{6,2},{7,3},{8,12},{9,13},{10,... | collective-permute-start | bytes 165896 | tf_op jit(solution)/shard_map/ppermute | solution.py:354
  50.0 5.1 %collective-permute-start.16 = (bf16[72,384]{1,0:T(8,128)(2,1)S(1)}, bf16[72,384]{1,0:T(8,128)(2,1)S(1)}, u32[]{:S(2)}, u32[]{:S(2)}) collective-permute-start(bf16[72,384]{1,0:T(8,128)(2,1)S(1)} %fusion.12), channel_id=1, source_target_pairs={{0,4},{1,5},{2,6},{3,7},{4,0},{5,1},{6,2},{7,3},{8,12},{9,13},{10,... | collective-permute-start | bytes 165896 | tf_op jit(solution)/shard_map/ppermute | solution.py:354
  53.4 4.9 %collective-permute-start.21 = (bf16[72,384]{1,0:T(8,128)(2,1)S(1)}, bf16[72,384]{1,0:T(8,128)(2,1)S(1)}, u32[]{:S(2)}, u32[]{:S(2)}) collective-permute-start(bf16[72,384]{1,0:T(8,128)(2,1)S(1)} %add_convert_fusion.rest_0_), channel_id=1, source_target_pairs={{0,1},{1,0},{2,3},{3,2},{4,5},{5,4},{6,7},{7,6},{8,9},{9,8},{10,11... | collective-permute-start | bytes 165896 | tf_op jit(solution)/shard_map/ppermute | solution.py:354
  55.2 4.2 %collective-permute-start.17 = (bf16[72,384]{1,0:T(8,128)(2,1)S(1)}, bf16[72,384]{1,0:T(8,128)(2,1)S(1)}, u32[]{:S(2)}, u32[]{:S(2)}) collective-permute-start(bf16[72,384]{1,0:T(8,128)(2,1)S(1)} %add_convert_fusion.1.rest_1_), channel_id=1, source_target_pairs={{0,1},{1,0},{2,3},{3,2},{4,5},{5,4},{6,7},{7,6},{8,9},{9,8},{10,11... | collective-permute-start | bytes 165896 | tf_op jit(solution)/shard_map/ppermute | solution.py:354
